TPU v7x, 32 devices: a whole 2x2x4 slice. The times are simulated.
32 devices in a mesh: ex: 2 (over x), tp: 4 (over y, core), blk: 4 (over z).
Axes of the slice: x: 2, y: 2, z: 4, core: 2. Of those that a mesh axis runs over, the one named last changes fastest.
Arguments:
- gradients: bfloat16 [512, 8192], P('ex', 'tp'), may hold values from -6 to 6
- selection: int32 [256], P('ex'), may hold values from 0 to 255, as said below
- seed_value: int32 [1], replicated, may hold values from 0 to 999999999
- ridge_value: float32 [1], replicated, may hold values from 0.3 to 3
Outputs:
- panel_out: float32 [2048, 512], P(('ex', 'blk'))
- trailing: float32 [2048, 2048], P(('ex', 'blk'), 'tp')
Inputs may be any that keep to these rules, and one draw needn't show every extreme that they name: `selection`: within each aligned block of 128 entries the values are distinct, and 0 and 255 occur in every block.
All inputs are finite; a program needn't handle non-finite values.
Results may differ from a plain program's by a relative error of at most 0.0046.
Values may be sent and summed in bfloat16 or wider, within the bound.
No kernel may reach another device: no remote copies, remote signals or barrier semaphores. Data moves between devices by JAX's collectives and lax.ppermute only.
A program may use at most 64 MiB of HBM per device.

v0:
```python
import math

import jax
import jax.numpy as jnp
from jax import lax
from jax.sharding import PartitionSpec as P

PANEL = 512
HALF = 256


def from_root(value, axis, source):
    kept = jnp.where(lax.axis_index(axis) == source, value, 0).astype(value.dtype)
    return lax.psum(kept, axis)


def scramble(hashed, amount):
    return hashed ^ lax.shift_right_logical(hashed, jnp.full_like(hashed, amount))


def sign_block(seed_word, coordinates, features):
    hashed = (
        coordinates[:, None] * jnp.int32(-1640531535)
        + features[None, :] * jnp.int32(668265263)
        + seed_word
    )
    hashed = scramble(hashed, 16) * jnp.int32(-2048144789)
    hashed = scramble(hashed, 13) * jnp.int32(-1028477387)
    hashed = scramble(hashed, 16)
    bit_value = lax.shift_right_logical(hashed, jnp.full_like(hashed, 7)) & jnp.int32(1)
    return jnp.int32(1) - jnp.int32(2) * bit_value


def contract_rows(left_part, right_part):
    return lax.dot_general(
        left_part, right_part, (((0,), (0,)), ((), ())), preferred_element_type=jnp.float32
    )


def shards(gradients, selection, seed_value, ridge_value):
    ex_count = lax.axis_size("ex")
    tp_count = lax.axis_size("tp")
    blk_count = lax.axis_size("blk")
    tp_index = lax.axis_index("tp")
    group_index = lax.axis_index("ex") * blk_count + lax.axis_index("blk")
    example_rows_dev = selection.shape[0]
    coord_dev = gradients.shape[1]
    chosen = gradients[selection]
    feature_ids = (
        (jnp.arange(ex_count, dtype=jnp.int32)[:, None] * blk_count + lax.axis_index("blk")) * HALF
        + jnp.arange(HALF, dtype=jnp.int32)[None, :]
    ).reshape(-1)
    stride = min(512, coord_dev)
    projected = jnp.zeros((example_rows_dev, ex_count * HALF), jnp.float32)
    for segment in range(coord_dev // stride):
        coordinates = tp_index * coord_dev + segment * stride + jnp.arange(stride, dtype=jnp.int32)
        sign_values = sign_block(seed_value[0], coordinates, feature_ids).astype(jnp.bfloat16)
        projected = projected + jnp.dot(
            chosen[:, segment * stride : (segment + 1) * stride],
            sign_values,
            preferred_element_type=jnp.float32,
        )
    summed = lax.psum(projected, "tp")
    scaling = 1.0 / math.sqrt(coord_dev * tp_count)
    phi_columns = (summed * scaling).astype(jnp.bfloat16)
    row_parts = []
    gathered = lax.all_gather(phi_columns, "blk", axis=1, tiled=True)
    gathered = gathered.reshape(example_rows_dev, blk_count * ex_count, HALF)
    for which in range(2):
        owner_group = 2 * tp_index + which
        slot_index = owner_group % blk_count * ex_count + owner_group // blk_count
        row_parts.append(lax.dynamic_index_in_dim(gathered, slot_index, 1, keepdims=False))
    phi_rows = jnp.concatenate(row_parts, axis=1)
    examples = float(example_rows_dev * ex_count)
    columns_all = lax.all_to_all(phi_columns, "ex", split_axis=1, concat_axis=0, tiled=True)
    summed_tile = contract_rows(columns_all, lax.all_gather(phi_rows, "ex", axis=0, tiled=True))
    row_features = group_index * HALF + jnp.arange(HALF, dtype=jnp.int32)
    column_features = tp_index * PANEL + jnp.arange(PANEL, dtype=jnp.int32)
    diag_mask = (row_features[:, None] == column_features[None, :]).astype(jnp.float32)
    own_tile = summed_tile / examples + ridge_value[0] * diag_mask
    top_pieces = [from_root(own_tile, ("ex", "blk"), which) for which in range(2)]
    top_block = jnp.concatenate(top_pieces, axis=0)
    diag_block, first_tile = (from_root(top_block, "tp", 0), from_root(own_tile, "tp", 0))
    factor = jnp.linalg.cholesky(diag_block)
    right_part = jax.scipy.linalg.solve_triangular(factor, top_block, lower=True)
    panel_out = jax.scipy.linalg.solve_triangular(factor, first_tile.T, lower=True).T
    trailing = own_tile - jnp.dot(panel_out, right_part, precision=lax.Precision.HIGHEST)
    return (panel_out, trailing)


def solution(mesh):
    in_specs = (P("ex", "tp"), P("ex"), P(), P())
    out_specs = (P(("ex", "blk"), None), P(("ex", "blk"), "tp"))
    return jax.shard_map(shards, mesh=mesh, in_specs=in_specs, out_specs=out_specs, check_vma=False)
```

profile of v0, /device:TPU:0, one launch (start us, length us, event | category | flops | bytes accessed | tf_op | source)
XLA Modules:
  0.0 362.1 jit_solution(10390722030701593445)
XLA Ops:
  8.1 0.6 copy-done.16
  8.8 0.9 gather_fusion
  9.7 0.8 fusion.45
  10.5 0.8 convolution_add_fusion.2
  11.3 0.8 convolution_add_fusion.1
  12.1 1.5 convolution_add_fusion
  14.3 34.1 %all-reduce.7.cloned.1.call-done = f32[128,512]{1,0:T(8,128)} async-done(((f32[128,512]{1,0:T(8,128)}), f32[128,512]{1,0:T(8,128)}) %all-reduce.7.cloned.1.call-update) | async-done | bytes 262160 | tf_op jit(solution)/shard_map/psum | solution.py:63
  48.4 1.0 multiply_convert_fusion
  49.4 14.8 %all_gather.6 = bf16[128,2048]{1,0:T(8,128)(2,1)S(1)} all-gather(bf16[128,512]{1,0:T(8,128)(2,1)S(1)} %multiply_convert_fusion), channel_id=1, replica_groups=mesh['ex'=2,'tp'=4,'blk'=4] {'blk'}, dimensions={1}, use_global_device_ids=true | all-gather | bytes 655360 | tf_op jit(solution)/shard_map/all_gather | solution.py:67
  64.3 0.7 copy.48
  64.9 3.4 all-to-all-start
  68.8 5.6 %all_gather.7 = bf16[256,512]{1,0:T(8,128)(2,1)S(1)} all-gather(bf16[128,512]{1,0:T(8,128)(2,1)S(1)} %pad_maximum_fusion.2), channel_id=1, replica_groups=mesh['ex'=2,'tp'=4,'blk'=4] {'ex'}, dimensions={0}, use_global_device_ids=true | all-gather | bytes 393216 | tf_op jit(solution)/shard_map/all_gather | solution.py:76
  74.8 1.3 broadcast_select_fusion.1
  76.3 79.7 %all-reduce.9.cloned.1.call-done = (f32[256,512]{0,1:T(8,128)}, f32[256,512]{0,1:T(8,128)}) async-done(((f32[256,512]{0,1:T(8,128)}, f32[256,512]{0,1:T(8,128)}), (f32[256,512]{0,1:T(8,128)}, f32[256,512]{0,1:T(8,128)})) %all-reduce.9.cloned.1.call-update) | async-done | bytes 1048592 | tf_op jit(solution)/shard_map/psum | solution.py:14
  156.0 2.4 maximum_select_fusion
  158.4 43.2 %all-reduce.11.cloned.1.call-done = (f32[512,256]{1,0:T(8,128)}, f32[512,512]{0,1:T(8,128)}) async-done(((f32[512,256]{1,0:T(8,128)}, f32[512,512]{0,1:T(8,128)}), (f32[512,256]{1,0:T(8,128)}, f32[512,512]{0,1:T(8,128)})) %all-reduce.11.cloned.1.call-update) | async-done | bytes 1572880 | tf_op jit(solution)/shard_map/psum | solution.py:14
  201.6 1.6 copy.23
  203.5 1.0 copy-done.2
  204.5 11.7 %cholesky.105 = f32[128,128]{1,0:T(8,128)S(1)} custom-call(f32[128,128]{1,0:T(8,128)S(1)} %cholesky.266), custom_call_target="Cholesky" | custom-call | tf_op jit(solution)/shard_map/jit(cholesky)/cholesky | solution.py:84
  216.3 9.8 %custom-call.34 = f32[1,128,128]{1,2,0:T(8,128)S(1)} custom-call(f32[1,128,128]{2,1,0:T(8,128)S(1)} %get-tuple-element.46), custom_call_target="InvertDiagBlocksLowerTriangular" | custom-call | tf_op jit(solution)/shard_map/jit(cholesky)/cholesky | solution.py:84
  226.1 1.2 fusion.103
  227.5 1.3 convolution_subtract_fusion.4
  228.8 11.7 %cholesky.218 = f32[128,128]{1,0:T(8,128)S(1)} custom-call(f32[128,128]{1,0:T(8,128)S(1)} %cholesky.270), custom_call_target="Cholesky" | custom-call | tf_op jit(solution)/shard_map/jit(cholesky)/cholesky | solution.py:84
  240.6 10.0 %custom-call.35 = f32[1,128,128]{1,2,0:T(8,128)S(1)} custom-call(f32[1,128,128]{2,1,0:T(8,128)S(1)} %get-tuple-element.44), custom_call_target="InvertDiagBlocksLowerTriangular" | custom-call | tf_op jit(solution)/shard_map/jit(cholesky)/cholesky | solution.py:84
  251.1 1.5 convolution_subtract_fusion.7
  252.7 11.7 %cholesky.239 = f32[128,128]{1,0:T(8,128)S(1)} custom-call(f32[128,128]{1,0:T(8,128)S(1)} %cholesky.275), custom_call_target="Cholesky" | custom-call | tf_op jit(solution)/shard_map/jit(cholesky)/cholesky | solution.py:84
  264.5 9.8 %custom-call.36 = f32[1,128,128]{1,2,0:T(8,128)S(1)} custom-call(f32[1,128,128]{2,1,0:T(8,128)S(1)} %get-tuple-element.42), custom_call_target="InvertDiagBlocksLowerTriangular" | custom-call | tf_op jit(solution)/shard_map/jit(cholesky)/cholesky | solution.py:84
  274.6 1.3 convolution_subtract_fusion.9
  276.0 11.9 %cholesky.256 = f32[128,128]{1,0:T(8,128)S(1)} custom-call(f32[128,128]{1,0:T(8,128)S(1)} %convolution_subtract_fusion.9), custom_call_target="Cholesky" | custom-call | tf_op jit(solution)/shard_map/jit(cholesky)/cholesky | solution.py:84
  288.0 0.6 compare_reduce_fusion.3
  288.7 0.6 compare_reduce_fusion.2
  289.3 0.6 compare_reduce_fusion.1
  289.9 0.7 compare_reduce_fusion
  293.3 8.5 %while.1 = (s32[]{:T(128)}, f32[512,512]{0,1:T(8,128)S(1)}, s32[4,2]{0,1:T(2,128)S(1)}, f32[4,128,128]{2,1,0:T(8,128)S(1)}, s32[]{:T(128)}) while((s32[]{:T(128)}, f32[512,512]{0,1:T(8,128)S(1)}, s32[4,2]{0,1:T(2,128)S(1)}, f32[4,128,128]{2,1,0:T(8,128)S(1)}, s32[]{:T(128)}) %tuple.34), condition=%wide.while_cond, body=%wide.while_body.sunk | while | flops 2 | bytes 393329 | solution.py:86
  293.4 0.5 fusion.176
  293.9 1.4 dynamic-slice.7
  296.1 1.4 dynamic-slice.7
  298.2 1.4 dynamic-slice.7
  300.3 1.4 dynamic-slice.7
  301.8 39.3 %custom-call.37 = f32[4,128,128]{1,2,0:T(8,128)S(1)} custom-call(f32[4,128,128]{2,1,0:T(8,128)S(1)} %get-tuple-element.9), custom_call_target="InvertDiagBlocksLowerTriangular" | custom-call | tf_op jit(solution)/shard_map/jit(_solve_triangular)/triangular_solve | solution.py:86
  341.1 1.5 fusion.96
  345.2 0.6 copy-done.14
  345.9 1.0 copy.33
  346.9 0.6 convolution_subtract_fusion.2
  348.3 1.0 convolution_subtract_fusion.1
  349.7 1.5 convolution_subtract_fusion.3
  352.3 1.8 convolution_subtract_fusion
  354.1 1.0 copy.34
  (104 shorter events, 10.0 us)
Async XLA Ops:
  7.2 1.6 copy-start
  7.2 41.3 %all-reduce.7.cloned.1.call-start = ((), (), s32[]{:S(2)}) async-start(), calls=%async_computation.1 | async-start | bytes 524288 | tf_op jit(solution)/shard_map/psum | solution.py:63
  8.0 0.7 copy-start.16
  64.9 9.5 %all-to-all-start = ((bf16[128,2,256]{2,0,1:T(8,128)(2,1)}), bf16[128,2,256]{2,0,1:T(8,128)(2,1)S(1)}, u32[]{:S(2)}, u32[]{:S(2)}) async-start(bf16[128,2,256]{2,0,1:T(8,128)(2,1)} %bitcast.71), calls=%async_computation | async-start | bytes 262144 | tf_op jit(solution)/shard_map/all_to_all | solution.py:75
  68.3 87.7 %all-reduce.9.cloned.1.call-start = ((), (), s32[]{:S(2)}) async-start(), calls=%async_computation.2 | async-start | bytes 2097152 | tf_op jit(solution)/shard_map/psum | solution.py:14
  74.7 1.3 copy-start.12
  76.1 125.5 %all-reduce.11.cloned.1.call-start = ((), (), s32[]{:S(2)}) async-start(), calls=%async_computation.3 | async-start | bytes 3145728 | tf_op jit(solution)/shard_map/psum | solution.py:14
  201.6 1.7 copy-start.1
  203.5 1.0 copy-start.2
  301.8 40.8 %copy-start.11 = (f32[512,256]{1,0:T(8,128)S(1)}, f32[512,256]{1,0:T(8,128)}, u32[]{:S(2)}) copy-start(f32[512,256]{1,0:T(8,128)} %get-tuple-element.32) | copy-start | bytes 1572868
  341.1 3.7 %copy-start.9 = (f32[4,128,128]{1,2,0:T(8,128)}, f32[4,128,128]{1,2,0:T(8,128)S(1)}, u32[]{:S(2)}) copy-start(f32[4,128,128]{1,2,0:T(8,128)S(1)} %custom-call.37) | copy-start | bytes 786436
  343.6 1.6 copy-start.5
  344.3 0.9 copy-start.7
  345.2 0.7 copy-start.14
  345.9 1.0 copy-start.3
  346.9 0.9 copy-start.10
  346.9 1.4 copy-start.4
  349.7 1.9 copy-start.13
  351.2 0.9 copy-start.6
  351.2 1.0 copy-start.8
  351.2 1.0 copy-start.15
Sparse Core Ops, SparseCore 0:
  13.7 34.6 all-reduce.6
  76.2 79.7 all-reduce.8
  159.0 42.5 all-reduce.10
where the time goes:
time: 366 us; the launch traced here: 362 us
  waiting for transfers between devices  157 us (43%)
  other arithmetic  124 us (34%)
  blocking collectives  20.5 us (6%)
  matrix products  20.1 us (5%)
  between operations  18.8 us (5%)
  local copies, waits for them, and re-layouts  18 us (5%)
  starting transfers between devices  3.67 us (1%)
    psum x2, waiting for transfers between devices, from_root(): return lax.psum(kept, axis)  123 us
    another operation x15, other arithmetic, shards(): factor = jnp.linalg.cholesky(diag_block)  79.4 us
    another operation x3, other arithmetic, shards(): jax.scipy.linalg.solve_triangular(factor, first_tile.T, lower=True)  39.4 us
    psum x1, waiting for transfers between devices, shards(): summed = lax.psum(projected, 'tp')  34.1 us
    all_gather x1, blocking collectives, shards(): gathered = lax.all_gather(phi_columns, 'blk', axis=1, tiled=True)  14.8 us
    another operation x20, local copies, waits for them, and re-layouts  8.32 us
  transfers between devices with their start and end apart: 4, of which 3 were waited for; matrix products, arithmetic and copies ran while one was open for 0% of the time, Pallas kernels for 0%

commit v1 on v0

v1 whole, which is shorter than its diff:
```python
import functools
import math

import jax
import jax.numpy as jnp
from jax import lax
from jax.experimental import pallas as pl
from jax.experimental.pallas import tpu as pltpu
from jax.sharding import PartitionSpec as P

PANEL = 512
HALF = 256
LEAF = 32
BLOCK = 128
HIGHEST = lax.Precision.HIGHEST
VMEM = pl.BlockSpec(memory_space=pltpu.VMEM)
SMEM = pl.BlockSpec(memory_space=pltpu.SMEM)


def scramble(hashed, amount):
    return hashed ^ lax.shift_right_logical(hashed, jnp.full_like(hashed, amount))


def sign_block(seed_word, coordinates, features):
    hashed = (
        coordinates[:, None] * jnp.int32(-1640531535)
        + features[None, :] * jnp.int32(668265263)
        + seed_word
    )
    hashed = scramble(hashed, 16) * jnp.int32(-2048144789)
    hashed = scramble(hashed, 13) * jnp.int32(-1028477387)
    hashed = scramble(hashed, 16)
    bit_value = lax.shift_right_logical(hashed, jnp.full_like(hashed, 7)) & jnp.int32(1)
    return jnp.int32(1) - jnp.int32(2) * bit_value


def project(chosen, seed_word, first_coordinate, feature_ids):
    coord_dev = chosen.shape[1]
    stride = min(512, coord_dev)
    projected = jnp.zeros((chosen.shape[0], feature_ids.shape[0]), jnp.float32)
    for start in range(0, coord_dev, stride):
        coordinates = first_coordinate + start + jnp.arange(stride, dtype=jnp.int32)
        sign_values = sign_block(seed_word, coordinates, feature_ids).astype(jnp.bfloat16)
        projected = projected + jnp.dot(
            chosen[:, start : start + stride], sign_values, preferred_element_type=jnp.float32
        )
    return projected


def tdot(left, right, precision=HIGHEST):
    return lax.dot_general(
        left, right, (((0,), (0,)), ((), ())), precision=precision, preferred_element_type=jnp.float32
    )


def row_of(value, row):
    return jnp.broadcast_to(value[row : row + 1, :], value.shape)


def factor_leaf(rows_u, rows_z, offset):
    groups = len(rows_u)
    sub = lax.broadcasted_iota(jnp.int32, (8, BLOCK), 0)
    columns = [
        [
            None if v < c // 8 else jnp.broadcast_to(rows_u[v][:, offset + c : offset + c + 1], (8, BLOCK))
            for v in range(groups)
        ]
        for c in range(8 * groups)
    ]
    rows_u, rows_z = list(rows_u), list(rows_z)
    pivots = [jnp.ones((8, BLOCK), jnp.float32) for _ in range(groups)]
    for j in range(8 * groups):
        g, s = divmod(j, 8)
        column = columns[j]
        pivot = row_of(column[g], s)
        pivots[g] = jnp.where(sub == s, pivot, pivots[g])
        inverse = 1.0 / pivot
        factors = {v: column[v] * inverse for v in range(g, groups)}
        factors[g] = jnp.where(sub > s, factors[g], 0.0)
        for c in range(j + 1, 8 * groups):
            weight = row_of(column[c // 8], c % 8)
            for v in range(c // 8, groups):
                columns[c][v] = columns[c][v] - factors[v] * weight
        row_u, row_z = row_of(rows_u[g], s), row_of(rows_z[g], s)
        for v in range(g, groups):
            rows_u[v] = rows_u[v] - factors[v] * row_u
            rows_z[v] = rows_z[v] - factors[v] * row_z
    scales = [lax.rsqrt(pivot) for pivot in pivots]
    return (
        jnp.concatenate([row * scale for row, scale in zip(rows_u, scales)], axis=0),
        jnp.concatenate([row * scale for row, scale in zip(rows_z, scales)], axis=0),
    )


def identity_mask(shape):
    return lax.broadcasted_iota(jnp.int32, shape, 0) == lax.broadcasted_iota(jnp.int32, shape, 1)


def factor_block(block):
    rest = jnp.concatenate([block, identity_mask(block.shape).astype(jnp.float32)], axis=1)
    done = []
    for leaf in range(BLOCK // LEAF):
        rows = [rest[8 * v : 8 * v + 8] for v in range(LEAF // 8)]
        upper, inverse = factor_leaf(
            [row[:, :BLOCK] for row in rows], [row[:, BLOCK:] for row in rows], LEAF * leaf
        )
        done.append(inverse)
        if leaf + 1 < BLOCK // LEAF:
            update = tdot(upper, jnp.concatenate([upper, inverse], axis=1))
            rest = rest[LEAF:] - update[LEAF * (leaf + 1) :]
    return jnp.concatenate(done, axis=0)


def cholesky_kernel(ridge_ref, phi_ref, upper_ref, lifted_ref, gram_ref):
    examples, width = phi_ref.shape
    phi = phi_ref[...]
    gram_ref[...] = tdot(phi, phi, None) / float(examples) + jnp.where(
        identity_mask((width, width)), ridge_ref[0], 0.0
    )
    lifted_ref[...] = phi.astype(jnp.float32).T
    for low in range(0, width, BLOCK):
        high = low + BLOCK
        inverse = factor_block(gram_ref[low:high, low:high])
        upper = jnp.dot(
            inverse, gram_ref[low:high, low:], precision=HIGHEST, preferred_element_type=jnp.float32
        )
        lifted = jnp.dot(
            inverse, lifted_ref[low:high, :], precision=HIGHEST, preferred_element_type=jnp.float32
        )
        keep = lax.broadcasted_iota(jnp.int32, upper.shape, 0) <= lax.broadcasted_iota(
            jnp.int32, upper.shape, 1
        )
        upper_ref[low:high, low:] = jnp.where(keep, upper, 0.0)
        if low > 0:
            upper_ref[low:high, :low] = jnp.zeros((BLOCK, low), jnp.float32)
        lifted_ref[low:high, :] = lifted
        if high < width:
            rest = upper[:, BLOCK:]
            gram_ref[high:, high:] = gram_ref[high:, high:] - tdot(rest, rest)
            lifted_ref[high:, :] = lifted_ref[high:, :] - tdot(rest, lifted)


def cholesky_panel(ridge_value, phi_panel):
    examples, width = phi_panel.shape
    return pl.pallas_call(
        cholesky_kernel,
        out_shape=(
            jax.ShapeDtypeStruct((width, width), jnp.float32),
            jax.ShapeDtypeStruct((width, examples), jnp.float32),
        ),
        in_specs=[SMEM, VMEM],
        out_specs=(VMEM, VMEM),
        scratch_shapes=[pltpu.VMEM((width, width), jnp.float32)],
        compiler_params=pltpu.CompilerParams(vmem_limit_bytes=32 * 1024 * 1024),
        cost_estimate=pl.CostEstimate(flops=20_000_000_000, bytes_accessed=4_000_000, transcendentals=0),
        name="cholesky_panel",
    )(ridge_value, phi_panel)


def split_dot(left, right):
    total = None
    for _ in range(3):
        part = left.astype(jnp.bfloat16)
        left = left - part.astype(jnp.float32)
        term = jnp.dot(part, right, preferred_element_type=jnp.float32)
        total = term if total is None else total + term
    return total


def finish_kernel(place_ref, ridge_ref, upper_ref, lifted_ref, rows_ref, columns_ref, panel_ref, trailing_ref):
    examples, height = rows_ref.shape
    width = columns_ref.shape[1]
    panel = upper_ref.shape[0]
    row_start = place_ref[0]
    column_start = place_ref[1]
    rows, columns = rows_ref[...], columns_ref[...]
    lifted = lifted_ref[...]
    solved_rows = split_dot(lifted, rows) / float(examples)
    solved_columns = split_dot(lifted, columns) / float(examples)
    for start in range(0, panel, height):
        solved_rows = jnp.where(row_start == start, upper_ref[:, start : start + height], solved_rows)
    for start in range(0, panel, width):
        solved_columns = jnp.where(column_start == start, upper_ref[:, start : start + width], solved_columns)
    panel_ref[...] = solved_rows.T
    shape = (height, width)
    diagonal = row_start + lax.broadcasted_iota(jnp.int32, shape, 0) == column_start + lax.broadcasted_iota(
        jnp.int32, shape, 1
    )
    gram = tdot(rows, columns, None) / float(examples) + jnp.where(diagonal, ridge_ref[0], 0.0)
    trailing_ref[...] = gram - tdot(solved_rows, solved_columns)


def finish(place, ridge_value, upper, lifted, phi_rows, phi_columns):
    height, width = phi_rows.shape[1], phi_columns.shape[1]
    return pl.pallas_call(
        finish_kernel,
        out_shape=(
            jax.ShapeDtypeStruct((height, upper.shape[0]), jnp.float32),
            jax.ShapeDtypeStruct((height, width), jnp.float32),
        ),
        in_specs=[SMEM, SMEM, VMEM, VMEM, VMEM, VMEM],
        out_specs=(VMEM, VMEM),
        compiler_params=pltpu.CompilerParams(vmem_limit_bytes=32 * 1024 * 1024),
        cost_estimate=pl.CostEstimate(flops=2_000_000_000, bytes_accessed=4_000_000, transcendentals=0),
        name="finish",
    )(place, ridge_value, upper, lifted, phi_rows, phi_columns)


def shifted(value, axis, step):
    count = lax.axis_size(axis)
    return lax.ppermute(value, axis, [(s, (s + step) % count) for s in range(count)])


def exchange(pieces, axis):
    count = lax.axis_size(axis)
    index = lax.axis_index(axis)
    return [pieces(index)] + [
        shifted(pieces((index + step) % count), axis, step) for step in range(1, count)
    ]


def shards(gradients, selection, seed_value, ridge_value):
    ex_count = lax.axis_size("ex")
    tp_count = lax.axis_size("tp")
    blk_count = lax.axis_size("blk")
    ex_index, tp_index, blk_index = (lax.axis_index(axis) for axis in ("ex", "tp", "blk"))
    example_rows_dev = selection.shape[0]
    coord_dev = gradients.shape[1]
    chunk = example_rows_dev // tp_count
    column_width = HALF * ex_count * blk_count // tp_count
    scaling = 1.0 / math.sqrt(coord_dev * tp_count)
    chosen = gradients[selection]
    first_coordinate = tp_index * coord_dev

    def reduced(partial):
        def piece(target):
            return lax.dynamic_slice_in_dim(partial, target * chunk, chunk, 0)

        parts = exchange(piece, "tp")
        return (functools.reduce(jnp.add, parts) * scaling).astype(jnp.bfloat16)

    panel_ids = jnp.arange(PANEL, dtype=jnp.int32)
    phi_panel = reduced(project(chosen, seed_value[0], first_coordinate, panel_ids))
    phi_panel = jnp.stack(exchange(lambda target: phi_panel, "ex"))
    phi_panel = jnp.stack(exchange(lambda target: phi_panel, "tp"), axis=1).reshape(-1, PANEL)

    upper, lifted = cholesky_panel(ridge_value, phi_panel)

    feature_ids = (
        (jnp.arange(ex_count, dtype=jnp.int32)[:, None] * blk_count + blk_index) * HALF
        + jnp.arange(HALF, dtype=jnp.int32)[None, :]
    ).reshape(-1)
    phi_own = reduced(project(chosen, seed_value[0], first_coordinate, feature_ids))
    back = exchange(lambda target: phi_own.reshape(chunk, ex_count, 1, HALF), "blk")
    steps = (blk_index - jnp.arange(blk_count)) % blk_count
    phi_all = jnp.take(jnp.concatenate(back, axis=2), steps, axis=2).reshape(chunk, -1)

    def both(target):
        columns = lax.dynamic_slice_in_dim(phi_all, target * column_width, column_width, 1)
        return jnp.concatenate([columns, phi_own], axis=1)

    phi_both = jnp.concatenate(exchange(both, "tp"), axis=0)

    def half_of(target):
        rows = lax.dynamic_slice_in_dim(phi_both, column_width + target * HALF, HALF, 1)
        return jnp.concatenate([phi_both[:, :column_width], rows], axis=1)

    phi_both = jnp.concatenate(exchange(half_of, "ex"), axis=0)
    phi_columns, phi_rows = phi_both[:, :column_width], phi_both[:, column_width:]
    place = jnp.stack([(ex_index * blk_count + blk_index) * HALF, tp_index * column_width]).astype(jnp.int32)
    return finish(place, ridge_value, upper, lifted, phi_rows, phi_columns)


def solution(mesh):
    in_specs = (P("ex", "tp"), P("ex"), P(), P())
    out_specs = (P(("ex", "blk"), None), P(("ex", "blk"), "tp"))
    return jax.shard_map(shards, mesh=mesh, in_specs=in_specs, out_specs=out_specs, check_vma=False)
```

time: 366 us -> 57.3 us (0.16)
  waiting for transfers between devices: 157 us -> 4.32 us
  other arithmetic: 124 us -> 0.44 us
  Pallas kernels: 0 us -> 20.9 us
  blocking collectives: 20.5 us -> 0 us
  between operations: 18.8 us -> 2.43 us
  starting transfers between devices: 3.67 us -> 20 us
  local copies, waits for them, and re-layouts: 18 us -> 2.19 us
  matrix products: 20.1 us -> 6.36 us
    psum x3 -> x0, waiting for transfers between devices: 157 us -> none  [the longest x2 123 us: from_root(): return lax.psum(kept, axis)]
    another operation x18 -> x3, other arithmetic: 119 us -> 0.12 us  [the longest x1 0.08 us: shards(): jnp.stack([(ex_index * blk_count + blk_index) * HALF, tp_index * column_w...]
    pallas_call x0 -> x2, Pallas kernels: none -> 20.9 us  [the longest x1 17.7 us: cholesky_panel(): pl.pallas_call(cholesky_kernel, out_shape=(jax.ShapeDtypeStruct((width, w...]
    all_gather x2 -> x0, blocking collectives: 20.5 us -> none  [the longest x1 14.8 us: shards(): gathered = lax.all_gather(phi_columns, 'blk', axis=1, tiled=True)]
    ppermute x0 -> x17, starting transfers between devices: none -> 20 us  [shifted(): lax.ppermute(value, axis, [(s, (s + step) % count) for s in range(count)])]
    another operation x20 -> x0, matrix products: 14.1 us -> none  [the longest x6 5.92 us: shards(): factor = jnp.linalg.cholesky(diag_block)]
    another operation x34 -> x1, local copies, waits for them, and re-layouts: 9 us -> 0.02 us  [shards(): jnp.stack(exchange(lambda target: phi_panel, 'tp'), axis=1)]
    unnamed x38 -> x5, local copies, waits for them, and re-layouts: 5.42 us -> 0.28 us
  transfers between devices with their start and end apart: 4 -> 17, of which waited for: 3 -> 5; matrix products, arithmetic and copies ran while one was open for 0% -> 8% of each run, Pallas kernels for 0% -> 31%
where the time goes in v1:
time: 57.3 us; the launch traced here: 56.7 us
  Pallas kernels  20.9 us (36%)
  starting transfers between devices  20 us (35%)
  matrix products  6.36 us (11%)
  waiting for transfers between devices  4.32 us (8%)
  between operations  2.43 us (4%)
  local copies, waits for them, and re-layouts  2.19 us (4%)
    ppermute x17, starting transfers between devices, shifted(): lax.ppermute(value, axis, [(s, (s + step) % count) for s in range(count)])  20 us
    pallas_call x1, Pallas kernels, cholesky_panel(): pl.pallas_call(cholesky_kernel, out_shape=(jax.ShapeDtypeStruct((width, w...  17.7 us
    dot_general x8, matrix products, project(): jnp.dot(chosen[:, start:start + stride], sign_values, preferred_element_t...  6.36 us
    ppermute x17, waiting for transfers between devices, shifted(): lax.ppermute(value, axis, [(s, (s + step) % count) for s in range(count)])  4.32 us
    pallas_call x1, Pallas kernels, finish(): pl.pallas_call(finish_kernel, out_shape=(jax.ShapeDtypeStruct((height, up...  3.19 us
  transfers between devices with their start and end apart: 17, of which 5 were waited for; matrix products, arithmetic and copies ran while one was open for 8% of the time, Pallas kernels for 31%

profile of v1, /device:TPU:0, one launch (start us, length us, event | category | flops | bytes accessed | tf_op | source)
XLA Modules:
  0.0 56.7 jit_solution(15503935330986923203)
XLA Ops:
  0.6 0.0 copy-start
  0.7 0.0 copy-start.1
  1.5 0.1 multiply_bitcast_fusion
  1.6 0.3 copy-done
  1.9 0.9 %gather_fusion = bf16[128,2048]{1,0:T(8,128)(2,1)S(1)} fusion(bf16[256,2048]{1,0:T(8,128)(2,1)S(1)} %copy-done, s32[1024]{0:T(1024)S(1)} %pad_clamp_fusion.1), kind=kCustom, calls=%fused_computation | custom fusion | bytes 1049088 | tf_op jit(solution)/shard_map/gather | solution.py:232
  2.8 0.8 %fusion.62 = f32[128,512]{1,0:T(8,128)S(1)} fusion(s32[512]{0:T(512)S(1)} %bitcast.32, s32[]{:T(128)} %bitcast.21, s32[512]{0:T(512)S(1)} %get-tuple-element.24, bf16[128,2048]{1,0:T(8,128)(2,1)S(1)} %gather_fusion), kind=kOutput, calls=%fused_computation.88 | convolution fusion | flops 71041024 | bytes 397316 | tf_op jit(solution)/shard_map/dot_general | solution.py:44
  3.6 0.8 %convolution_add_fusion.2 = f32[128,512]{1,0:T(8,128)S(1)} fusion(f32[128,512]{1,0:T(8,128)S(1)} %fusion.62, s32[512]{0:T(512)S(1)} %bitcast.33, s32[512]{0:T(512)S(1)} %add_multiply_fusion.2, s32[]{:T(128)} %bitcast.20, bf16[128,2048]{1,0:T(8,128)(2,1)S(1)} %gather_fusion), kind=kOutput, calls=%fused_computation.28 | convolution fusion | flops 71106560 | bytes 659460 | tf_op jit(solution)/shard_map/dot_general | solution.py:44
  4.4 0.8 %convolution_add_fusion.1 = f32[128,512]{1,0:T(8,128)S(1)} fusion(f32[128,512]{1,0:T(8,128)S(1)} %convolution_add_fusion.2, s32[512]{0:T(512)S(1)} %bitcast.34, s32[512]{0:T(512)S(1)} %add_multiply_fusion.1, s32[]{:T(128)} %bitcast.19, bf16[128,2048]{1,0:T(8,128)(2,1)S(1)} %gather_fusion), kind=kOutput, calls=%fused_computation.27 | convolution fusion | flops 71106560 | bytes 659460 | tf_op jit(solution)/shard_map/dot_general | solution.py:44
  5.2 0.8 %convolution_add_fusion = f32[128,512]{1,0:T(8,128)S(1)} fusion(f32[128,512]{1,0:T(8,128)S(1)} %convolution_add_fusion.1, s32[512]{0:T(512)S(1)} %bitcast.35, s32[512]{0:T(512)S(1)} %add_multiply_fusion, s32[]{:T(128)} %bitcast.18, bf16[128,2048]{1,0:T(8,128)(2,1)S(1)} %gather_fusion), kind=kOutput, calls=%fused_computation.26 | convolution fusion | flops 71106560 | bytes 659460 | tf_op jit(solution)/shard_map/dot_general | solution.py:44
  6.1 0.5 collective-permute-start.7
  6.6 2.0 %collective-permute-start.9 = (f32[32,512]{1,0:T(8,128)S(1)}, f32[32,512]{1,0:T(8,128)S(1)}, u32[]{:S(2)}, u32[]{:S(2)}) collective-permute-start(f32[32,512]{1,0:T(8,128)S(1)} %get-tuple-element.9), channel_id=1, source_target_pairs={{0,12},{4,0},{8,4},{12,8},{1,13},{5,1},{9,5},{13,9},{2,14},{6,2},{... | collective-permute-start | bytes 196616 | tf_op jit(solution)/shard_map/ppermute | solution.py:211
  8.6 2.2 %collective-permute-start.8 = (f32[32,512]{1,0:T(8,128)S(1)}, f32[32,512]{1,0:T(8,128)S(1)}, u32[]{:S(2)}, u32[]{:S(2)}) collective-permute-start(f32[32,512]{1,0:T(8,128)S(1)} %get-tuple-element.10), channel_id=1, source_target_pairs={{0,8},{4,12},{8,0},{12,4},{1,9},{5,13},{9,1},{13,5},{2,10},{6,14},... | collective-permute-start | bytes 196616 | tf_op jit(solution)/shard_map/ppermute | solution.py:211
  10.8 0.8 %fusion.64 = f32[128,512]{1,0:T(8,128)S(1)} fusion(s32[]{:T(128)} %bitcast.17, s32[512]{0:T(512)S(1)} %get-tuple-element.23, s32[512]{0:T(512)S(1)} %get-tuple-element.24, bf16[128,2048]{1,0:T(8,128)(2,1)S(1)} %gather_fusion), kind=kOutput, calls=%fused_computation.89 | convolution fusion | flops 71041024 | bytes 397316 | tf_op jit(solution)/shard_map/dot_general | solution.py:44
  11.6 0.8 %convolution_add_fusion.5 = f32[128,512]{1,0:T(8,128)S(1)} fusion(f32[128,512]{1,0:T(8,128)S(1)} %fusion.64, s32[512]{0:T(512)S(1)} %add_multiply_fusion.2, s32[]{:T(128)} %bitcast.24, s32[512]{0:T(512)S(1)} %get-tuple-element.23, bf16[128,2048]{1,0:T(8,128)(2,1)S(1)} %gather_fusion), kind=kOutput, calls=%fused_computation.31 | convolution fusion | flops 71106560 | bytes 659460 | tf_op jit(solution)/shard_map/dot_general | solution.py:44
  12.4 0.8 %convolution_add_fusion.4 = f32[128,512]{1,0:T(8,128)S(1)} fusion(f32[128,512]{1,0:T(8,128)S(1)} %convolution_add_fusion.5, s32[512]{0:T(512)S(1)} %add_multiply_fusion.1, s32[]{:T(128)} %bitcast.23, s32[512]{0:T(512)S(1)} %get-tuple-element.23, bf16[128,2048]{1,0:T(8,128)(2,1)S(1)} %gather_fusion), kind=kOutput, calls=%fused_computation.30 | convolution fusion | flops 71106560 | bytes 659460 | tf_op jit(solution)/shard_map/dot_general | solution.py:44
  13.2 0.8 %convolution_add_fusion.3 = f32[128,512]{1,0:T(8,128)S(1)} fusion(f32[128,512]{1,0:T(8,128)S(1)} %convolution_add_fusion.4, s32[512]{0:T(512)S(1)} %add_multiply_fusion, s32[]{:T(128)} %bitcast.22, s32[512]{0:T(512)S(1)} %get-tuple-element.23, bf16[128,2048]{1,0:T(8,128)(2,1)S(1)} %gather_fusion), kind=kOutput, calls=%fused_computation.29 | convolution fusion | flops 71106560 | bytes 659460 | tf_op jit(solution)/shard_map/dot_general | solution.py:44
  14.1 0.1 collective-permute-start
  14.2 1.7 %collective-permute-start.2 = (f32[32,512]{1,0:T(8,128)S(1)}, f32[32,512]{1,0:T(8,128)S(1)}, u32[]{:S(2)}, u32[]{:S(2)}) collective-permute-start(f32[32,512]{1,0:T(8,128)S(1)} %get-tuple-element.12), channel_id=1, source_target_pairs={{0,12},{4,0},{8,4},{12,8},{1,13},{5,1},{9,5},{13,9},{2,14},{6,2},{... | collective-permute-start | bytes 196616 | tf_op jit(solution)/shard_map/ppermute | solution.py:211
  16.6 0.1 broadcast_in_dim.14
  16.7 0.1 pad_add_fusion.place_ref
  16.8 0.0 collective-permute-done.7
  16.8 0.0 collective-permute-start.1
  16.8 0.0 collective-permute-done.9
  16.8 0.0 collective-permute-done.8
  16.9 4.1 %collective-permute-start.12 = (bf16[32,2,1,256]{3,0,2,1:T(8,128)(2,1)S(1)}, bf16[32,2,1,256]{3,0,2,1:T(8,128)(2,1)S(1)}, u32[]{:S(2)}, u32[]{:S(2)}) collective-permute-start(bf16[32,2,1,256]{3,0,2,1:T(8,128)(2,1)S(1)} %copy.10), channel_id=1, source_target_pairs={{0,3},{1,0},{2,1},{3,2},{4,7},{5,4},{6,5},{7,6},{8,11},{9,8},{10,9... | collective-permute-start | bytes 98312 | tf_op jit(solution)/shard_map/ppermute | solution.py:211
  21.0 0.0 collective-permute-start.11
  21.0 0.0 collective-permute-done
  21.0 1.0 %collective-permute-start.10 = (bf16[32,2,1,256]{3,0,2,1:T(8,128)(2,1)S(1)}, bf16[32,2,1,256]{3,0,2,1:T(8,128)(2,1)S(1)}, u32[]{:S(2)}, u32[]{:S(2)}) collective-permute-start(bf16[32,2,1,256]{3,0,2,1:T(8,128)(2,1)S(1)} %copy.10), channel_id=1, source_target_pairs={{0,1},{1,2},{2,3},{3,0},{4,5},{5,6},{6,7},{7,4},{8,9},{9,10},{10,1... | collective-permute-start | bytes 98312 | tf_op jit(solution)/shard_map/ppermute | solution.py:211
  22.0 0.0 collective-permute-done.1
  22.1 1.6 %collective-permute-start.3 = (bf16[32,512]{1,0:T(8,128)(2,1)S(1)}, bf16[32,512]{1,0:T(8,128)(2,1)S(1)}, u32[]{:S(2)}, u32[]{:S(2)}) collective-permute-start(bf16[32,512]{1,0:T(8,128)(2,1)S(1)} %multiply_convert_fusion.1), channel_id=1, source_target_pairs={{0,16},{16,0},{1,17},{17,1},{2,18},{18,2},{3,19},{19,3},{4,20},{20... | collective-permute-start | bytes 98312 | tf_op jit(solution)/shard_map/ppermute | solution.py:211
  23.6 0.0 collective-permute-done.12
  23.6 2.2 %collective-permute-done.11 = bf16[32,2,1,256]{3,0,2,1:T(8,128)(2,1)S(1)} collective-permute-done((bf16[32,2,1,256]{3,0,2,1:T(8,128)(2,1)S(1)}, bf16[32,2,1,256]{3,0,2,1:T(8,128)(2,1)S(1)}, u32[]{:S(2)}, u32[]{:S(2)}) %collective-permute-start.11) | collective-permute-done | bytes 32800 | tf_op jit(solution)/shard_map/ppermute | solution.py:211
  25.8 0.9 %collective-permute-done.10 = bf16[32,2,1,256]{3,0,2,1:T(8,128)(2,1)S(1)} collective-permute-done((bf16[32,2,1,256]{3,0,2,1:T(8,128)(2,1)S(1)}, bf16[32,2,1,256]{3,0,2,1:T(8,128)(2,1)S(1)}, u32[]{:S(2)}, u32[]{:S(2)}) %collective-permute-start.10) | collective-permute-done | bytes 32800 | tf_op jit(solution)/shard_map/ppermute | solution.py:211
  26.8 0.6 gather_fusion.1
  27.3 0.1 copy.11
  27.4 0.1 gather.11
  27.6 0.1 collective-permute-start.13
  27.7 1.6 %collective-permute-start.14 = (bf16[32,1024]{1,0:T(8,128)(2,1)S(1)}, bf16[32,1024]{1,0:T(8,128)(2,1)S(1)}, u32[]{:S(2)}, u32[]{:S(2)}) collective-permute-start(bf16[32,1024]{1,0:T(8,128)(2,1)S(1)} %get-tuple-element.21), channel_id=1, source_target_pairs={{0,8},{4,12},{8,0},{12,4},{1,9},{5,13},{9,1},{13,5},{2,10},{6,14},... | collective-permute-start | bytes 196616 | tf_op jit(solution)/shard_map/ppermute | solution.py:211
  29.2 1.4 %collective-permute-start.15 = (bf16[32,1024]{1,0:T(8,128)(2,1)S(1)}, bf16[32,1024]{1,0:T(8,128)(2,1)S(1)}, u32[]{:S(2)}, u32[]{:S(2)}) collective-permute-start(bf16[32,1024]{1,0:T(8,128)(2,1)S(1)} %get-tuple-element.22), channel_id=1, source_target_pairs={{0,12},{4,0},{8,4},{12,8},{1,13},{5,1},{9,5},{13,9},{2,14},{6,2},{... | collective-permute-start | bytes 196616 | tf_op jit(solution)/shard_map/ppermute | solution.py:211
  30.6 0.0 collective-permute-done.3
  30.6 0.6 %collective-permute-start.5 = (bf16[2,32,512]{2,1,0:T(8,128)(2,1)S(1)}, bf16[2,32,512]{2,1,0:T(8,128)(2,1)S(1)}, u32[]{:S(2)}, u32[]{:S(2)}) collective-permute-start(bf16[2,32,512]{2,1,0:T(8,128)(2,1)S(1)} %get-tuple-element.19), channel_id=1, source_target_pairs={{0,8},{4,12},{8,0},{12,4},{1,9},{5,13},{9,1},{13,5},{2,10},{6,14},... | collective-permute-start | bytes 196616 | tf_op jit(solution)/shard_map/ppermute | solution.py:211
  31.2 0.2 collective-permute-done.13
  31.4 1.5 %collective-permute-start.6 = (bf16[2,32,512]{2,1,0:T(8,128)(2,1)S(1)}, bf16[2,32,512]{2,1,0:T(8,128)(2,1)S(1)}, u32[]{:S(2)}, u32[]{:S(2)}) collective-permute-start(bf16[2,32,512]{2,1,0:T(8,128)(2,1)S(1)} %get-tuple-element.19), channel_id=1, source_target_pairs={{0,12},{4,0},{8,4},{12,8},{1,13},{5,1},{9,5},{13,9},{2,14},{6,2},{... | collective-permute-start | bytes 196616 | tf_op jit(solution)/shard_map/ppermute | solution.py:211
  33.0 0.2 collective-permute-done.15
  33.3 1.6 %collective-permute-start.16 = (bf16[128,768]{1,0:T(8,128)(2,1)S(1)}, bf16[128,768]{1,0:T(8,128)(2,1)S(1)}, u32[]{:S(2)}, u32[]{:S(2)}) collective-permute-start(bf16[128,768]{1,0:T(8,128)(2,1)S(1)} %pad_maximum_fusion.4), channel_id=1, source_target_pairs={{0,16},{16,0},{1,17},{17,1},{2,18},{18,2},{3,19},{19,3},{4,20},{20... | collective-permute-start | bytes 589832 | tf_op jit(solution)/shard_map/ppermute | solution.py:211
  34.8 0.8 %collective-permute-done.5 = bf16[2,32,512]{2,1,0:T(8,128)(2,1)S(1)} collective-permute-done((bf16[2,32,512]{2,1,0:T(8,128)(2,1)S(1)}, bf16[2,32,512]{2,1,0:T(8,128)(2,1)S(1)}, u32[]{:S(2)}, u32[]{:S(2)}) %collective-permute-start.5) | collective-permute-done | bytes 65568 | tf_op jit(solution)/shard_map/ppermute | solution.py:211
  35.7 17.7 %cholesky_panel.1 = (f32[512,512]{1,0:T(8,128)S(1)}, f32[512,256]{1,0:T(8,128)S(1)}) custom-call(f32[1]{0:T(128)S(6)} %copy.14.ridge_ref, bf16[256,512]{1,0:T(8,128)(2,1)S(1)} %bitcast.25), custom_call_target="tpu_custom_call" | custom-call | flops 20000000000 | bytes 4000000 | tf_op jit(solution)/shard_map/cholesky_panel/pallas_call | solution.py:145
  53.5 3.2 %finish.1 = (f32[256,512]{1,0:T(8,128)}, f32[256,512]{1,0:T(8,128)}) custom-call(s32[2]{0:T(128)S(1)} %pad_add_fusion.place_ref, f32[1]{0:T(128)S(6)} %copy.14.ridge_ref, f32[512,512]{1,0:T(8,128)S(1)} %get-tuple-element.4.upper_ref, f32[512,256]{1,0:T(8,128)S(1)} %get-tuple-element.5.lifted_ref, bf16[256,256]{1,0:T(8,128)(2,1)S(1)} %pad_maximum_fusion.5.rows_ref, ...), custom_call_target="tpu_custom_call" | custom-call | flops 2000000000 | bytes 4000000 | tf_op jit(solution)/shard_map/finish/pallas_call | solution.py:195
  (38 shorter events, 0.5 us)
Async XLA Ops:
  0.6 1.3 %copy-start = (bf16[256,2048]{1,0:T(8,128)(2,1)S(1)}, bf16[256,2048]{1,0:T(8,128)(2,1)}, u32[]{:S(2)}) copy-start(bf16[256,2048]{1,0:T(8,128)(2,1)} %param.4) | copy-start | bytes 3145732
  0.7 0.7 %copy-start.1 = (s32[128]{0:T(128)S(1)}, s32[128]{0:T(128)}, u32[]{:S(2)}) copy-start(s32[128]{0:T(128)} %param.5) | copy-start | bytes 1540
  6.1 10.7 %collective-permute-start.7 = (f32[32,512]{1,0:T(8,128)S(1)}, f32[32,512]{1,0:T(8,128)S(1)}, u32[]{:S(2)}, u32[]{:S(2)}) collective-permute-start(f32[32,512]{1,0:T(8,128)S(1)} %get-tuple-element.8), channel_id=1, source_target_pairs={{0,4},{4,8},{8,12},{12,0},{1,5},{5,9},{9,13},{13,1},{2,6},{6,10},{... | collective-permute-start | bytes 196616 | tf_op jit(solution)/shard_map/ppermute | solution.py:211
  6.6 10.2 %collective-permute-start.9 = (f32[32,512]{1,0:T(8,128)S(1)}, f32[32,512]{1,0:T(8,128)S(1)}, u32[]{:S(2)}, u32[]{:S(2)}) collective-permute-start(f32[32,512]{1,0:T(8,128)S(1)} %get-tuple-element.9), channel_id=1, source_target_pairs={{0,12},{4,0},{8,4},{12,8},{1,13},{5,1},{9,5},{13,9},{2,14},{6,2},{... | collective-permute-start | bytes 196616 | tf_op jit(solution)/shard_map/ppermute | solution.py:211
  8.6 8.2 %collective-permute-start.8 = (f32[32,512]{1,0:T(8,128)S(1)}, f32[32,512]{1,0:T(8,128)S(1)}, u32[]{:S(2)}, u32[]{:S(2)}) collective-permute-start(f32[32,512]{1,0:T(8,128)S(1)} %get-tuple-element.10), channel_id=1, source_target_pairs={{0,8},{4,12},{8,0},{12,4},{1,9},{5,13},{9,1},{13,5},{2,10},{6,14},... | collective-permute-start | bytes 196616 | tf_op jit(solution)/shard_map/ppermute | solution.py:211
  14.1 6.9 %collective-permute-start = (f32[32,512]{1,0:T(8,128)S(1)}, f32[32,512]{1,0:T(8,128)S(1)}, u32[]{:S(2)}, u32[]{:S(2)}) collective-permute-start(f32[32,512]{1,0:T(8,128)S(1)} %get-tuple-element.11), channel_id=1, source_target_pairs={{0,4},{4,8},{8,12},{12,0},{1,5},{5,9},{9,13},{13,1},{2,6},{6,10},{... | collective-permute-start | bytes 196616 | tf_op jit(solution)/shard_map/ppermute | solution.py:211
  14.2 7.9 %collective-permute-start.2 = (f32[32,512]{1,0:T(8,128)S(1)}, f32[32,512]{1,0:T(8,128)S(1)}, u32[]{:S(2)}, u32[]{:S(2)}) collective-permute-start(f32[32,512]{1,0:T(8,128)S(1)} %get-tuple-element.12), channel_id=1, source_target_pairs={{0,12},{4,0},{8,4},{12,8},{1,13},{5,1},{9,5},{13,9},{2,14},{6,2},{... | collective-permute-start | bytes 196616 | tf_op jit(solution)/shard_map/ppermute | solution.py:211
  16.8 5.3 %collective-permute-start.1 = (f32[32,512]{1,0:T(8,128)S(1)}, f32[32,512]{1,0:T(8,128)S(1)}, u32[]{:S(2)}, u32[]{:S(2)}) collective-permute-start(f32[32,512]{1,0:T(8,128)S(1)} %get-tuple-element.13), channel_id=1, source_target_pairs={{0,8},{4,12},{8,0},{12,4},{1,9},{5,13},{9,1},{13,5},{2,10},{6,14},... | collective-permute-start | bytes 196616 | tf_op jit(solution)/shard_map/ppermute | solution.py:211
  16.9 6.7 %collective-permute-start.12 = (bf16[32,2,1,256]{3,0,2,1:T(8,128)(2,1)S(1)}, bf16[32,2,1,256]{3,0,2,1:T(8,128)(2,1)S(1)}, u32[]{:S(2)}, u32[]{:S(2)}) collective-permute-start(bf16[32,2,1,256]{3,0,2,1:T(8,128)(2,1)S(1)} %copy.10), channel_id=1, source_target_pairs={{0,3},{1,0},{2,1},{3,2},{4,7},{5,4},{6,5},{7,6},{8,11},{9,8},{10,9... | collective-permute-start | bytes 98312 | tf_op jit(solution)/shard_map/ppermute | solution.py:211
  21.0 4.8 %collective-permute-start.11 = (bf16[32,2,1,256]{3,0,2,1:T(8,128)(2,1)S(1)}, bf16[32,2,1,256]{3,0,2,1:T(8,128)(2,1)S(1)}, u32[]{:S(2)}, u32[]{:S(2)}) collective-permute-start(bf16[32,2,1,256]{3,0,2,1:T(8,128)(2,1)S(1)} %copy.10), channel_id=1, source_target_pairs={{0,2},{1,3},{2,0},{3,1},{4,6},{5,7},{6,4},{7,5},{8,10},{9,11},{10,... | collective-permute-start | bytes 98312 | tf_op jit(solution)/shard_map/ppermute | solution.py:211
  21.0 5.7 %collective-permute-start.10 = (bf16[32,2,1,256]{3,0,2,1:T(8,128)(2,1)S(1)}, bf16[32,2,1,256]{3,0,2,1:T(8,128)(2,1)S(1)}, u32[]{:S(2)}, u32[]{:S(2)}) collective-permute-start(bf16[32,2,1,256]{3,0,2,1:T(8,128)(2,1)S(1)} %copy.10), channel_id=1, source_target_pairs={{0,1},{1,2},{2,3},{3,0},{4,5},{5,6},{6,7},{7,4},{8,9},{9,10},{10,1... | collective-permute-start | bytes 98312 | tf_op jit(solution)/shard_map/ppermute | solution.py:211
  22.1 8.6 %collective-permute-start.3 = (bf16[32,512]{1,0:T(8,128)(2,1)S(1)}, bf16[32,512]{1,0:T(8,128)(2,1)S(1)}, u32[]{:S(2)}, u32[]{:S(2)}) collective-permute-start(bf16[32,512]{1,0:T(8,128)(2,1)S(1)} %multiply_convert_fusion.1), channel_id=1, source_target_pairs={{0,16},{16,0},{1,17},{17,1},{2,18},{18,2},{3,19},{19,3},{4,20},{20... | collective-permute-start | bytes 98312 | tf_op jit(solution)/shard_map/ppermute | solution.py:211
  27.6 3.8 %collective-permute-start.13 = (bf16[32,1024]{1,0:T(8,128)(2,1)S(1)}, bf16[32,1024]{1,0:T(8,128)(2,1)S(1)}, u32[]{:S(2)}, u32[]{:S(2)}) collective-permute-start(bf16[32,1024]{1,0:T(8,128)(2,1)S(1)} %get-tuple-element.20), channel_id=1, source_target_pairs={{0,4},{4,8},{8,12},{12,0},{1,5},{5,9},{9,13},{13,1},{2,6},{6,10},{... | collective-permute-start | bytes 196616 | tf_op jit(solution)/shard_map/ppermute | solution.py:211
  27.7 5.3 %collective-permute-start.14 = (bf16[32,1024]{1,0:T(8,128)(2,1)S(1)}, bf16[32,1024]{1,0:T(8,128)(2,1)S(1)}, u32[]{:S(2)}, u32[]{:S(2)}) collective-permute-start(bf16[32,1024]{1,0:T(8,128)(2,1)S(1)} %get-tuple-element.21), channel_id=1, source_target_pairs={{0,8},{4,12},{8,0},{12,4},{1,9},{5,13},{9,1},{13,5},{2,10},{6,14},... | collective-permute-start | bytes 196616 | tf_op jit(solution)/shard_map/ppermute | solution.py:211
  29.2 3.9 %collective-permute-start.15 = (bf16[32,1024]{1,0:T(8,128)(2,1)S(1)}, bf16[32,1024]{1,0:T(8,128)(2,1)S(1)}, u32[]{:S(2)}, u32[]{:S(2)}) collective-permute-start(bf16[32,1024]{1,0:T(8,128)(2,1)S(1)} %get-tuple-element.22), channel_id=1, source_target_pairs={{0,12},{4,0},{8,4},{12,8},{1,13},{5,1},{9,5},{13,9},{2,14},{6,2},{... | collective-permute-start | bytes 196616 | tf_op jit(solution)/shard_map/ppermute | solution.py:211
  30.6 5.0 %collective-permute-start.5 = (bf16[2,32,512]{2,1,0:T(8,128)(2,1)S(1)}, bf16[2,32,512]{2,1,0:T(8,128)(2,1)S(1)}, u32[]{:S(2)}, u32[]{:S(2)}) collective-permute-start(bf16[2,32,512]{2,1,0:T(8,128)(2,1)S(1)} %get-tuple-element.19), channel_id=1, source_target_pairs={{0,8},{4,12},{8,0},{12,4},{1,9},{5,13},{9,1},{13,5},{2,10},{6,14},... | collective-permute-start | bytes 196616 | tf_op jit(solution)/shard_map/ppermute | solution.py:211
  31.2 4.4 %collective-permute-start.4 = (bf16[2,32,512]{2,1,0:T(8,128)(2,1)S(1)}, bf16[2,32,512]{2,1,0:T(8,128)(2,1)S(1)}, u32[]{:S(2)}, u32[]{:S(2)}) collective-permute-start(bf16[2,32,512]{2,1,0:T(8,128)(2,1)S(1)} %get-tuple-element.19), channel_id=1, source_target_pairs={{0,4},{4,8},{8,12},{12,0},{1,5},{5,9},{9,13},{13,1},{2,6},{6,10},{... | collective-permute-start | bytes 196616 | tf_op jit(solution)/shard_map/ppermute | solution.py:211
  31.4 4.2 %collective-permute-start.6 = (bf16[2,32,512]{2,1,0:T(8,128)(2,1)S(1)}, bf16[2,32,512]{2,1,0:T(8,128)(2,1)S(1)}, u32[]{:S(2)}, u32[]{:S(2)}) collective-permute-start(bf16[2,32,512]{2,1,0:T(8,128)(2,1)S(1)} %get-tuple-element.19), channel_id=1, source_target_pairs={{0,12},{4,0},{8,4},{12,8},{1,13},{5,1},{9,5},{13,9},{2,14},{6,2},{... | collective-permute-start | bytes 196616 | tf_op jit(solution)/shard_map/ppermute | solution.py:211
  33.3 20.1 %collective-permute-start.16 = (bf16[128,768]{1,0:T(8,128)(2,1)S(1)}, bf16[128,768]{1,0:T(8,128)(2,1)S(1)}, u32[]{:S(2)}, u32[]{:S(2)}) collective-permute-start(bf16[128,768]{1,0:T(8,128)(2,1)S(1)} %pad_maximum_fusion.4), channel_id=1, source_target_pairs={{0,16},{16,0},{1,17},{17,1},{2,18},{18,2},{3,19},{19,3},{4,20},{20... | collective-permute-start | bytes 589832 | tf_op jit(solution)/shard_map/ppermute | solution.py:211

commit v2 on v1

v2 whole, which is shorter than its diff:
```python
import math

import jax
import jax.numpy as jnp
from jax import lax
from jax.experimental import pallas as pl
from jax.experimental.pallas import tpu as pltpu
from jax.sharding import PartitionSpec as P

PANEL = 512
HALF = 256
STRIPE = 32
SUB = 16
BLOCK = 128
DEPTH = 256
HIGHEST = lax.Precision.HIGHEST
VMEM = pl.BlockSpec(memory_space=pltpu.VMEM)
SMEM = pl.BlockSpec(memory_space=pltpu.SMEM)


def scramble(hashed, amount):
    return hashed ^ lax.shift_right_logical(hashed, jnp.full_like(hashed, amount))


def sign_block(seed_word, coordinates, features):
    hashed = (
        coordinates[:, None] * jnp.int32(-1640531535)
        + features[None, :] * jnp.int32(668265263)
        + seed_word
    )
    hashed = scramble(hashed, 16) * jnp.int32(-2048144789)
    hashed = scramble(hashed, 13) * jnp.int32(-1028477387)
    hashed = scramble(hashed, 16)
    bit_value = lax.shift_right_logical(hashed, jnp.full_like(hashed, 7)) & jnp.int32(1)
    return jnp.int32(1) - jnp.int32(2) * bit_value


def project(chosen, seed_word, first_coordinate, feature_ids):
    coord_dev = chosen.shape[1]
    stride = min(512, coord_dev)
    projected = jnp.zeros((chosen.shape[0], feature_ids.shape[0]), jnp.float32)
    for start in range(0, coord_dev, stride):
        coordinates = first_coordinate + start + jnp.arange(stride, dtype=jnp.int32)
        sign_values = sign_block(seed_word, coordinates, feature_ids).astype(jnp.bfloat16)
        projected = projected + jnp.dot(
            chosen[:, start : start + stride], sign_values, preferred_element_type=jnp.float32
        )
    return projected


def tdot(left, right, precision=HIGHEST):
    return lax.dot_general(
        left, right, (((0,), (0,)), ((), ())), precision=precision, preferred_element_type=jnp.float32
    )


def row_of(value, row):
    return jnp.broadcast_to(value[row : row + 1, :], value.shape)


def join(parts, axis):
    return parts[0] if len(parts) == 1 else jnp.concatenate(parts, axis)


def factor_stripe(rows_u, rows_z, offset):
    groups = len(rows_u)
    sub = lax.broadcasted_iota(jnp.int32, (8, BLOCK), 0)
    rows_u, rows_z = list(rows_u), list(rows_z)
    pivots = [jnp.ones((8, BLOCK), jnp.float32) for _ in range(groups)]
    for base in range(0, 8 * groups, SUB):
        columns = {
            c: {
                v: jnp.broadcast_to(rows_u[v][:, offset + c : offset + c + 1], (8, BLOCK))
                for v in range(c // 8, groups)
            }
            for c in range(base, base + SUB)
        }
        pivot = row_of(columns[base][base // 8], 0)
        for j in range(base, base + SUB):
            g, s = divmod(j, 8)
            column = columns[j]
            inverse = 1.0 / pivot
            pivots[g] = jnp.where(sub == s, pivot, pivots[g])
            if j + 1 < base + SUB:
                n, r = divmod(j + 1, 8)
                weight = row_of(column[n], r)
                following = columns[j + 1]
                pivot = row_of(following[n], r) - (weight * weight) * inverse
                for v in range(n, groups):
                    following[v] = following[v] - (column[v] * weight) * inverse
            factors = {v: column[v] * inverse for v in range(g, groups)}
            for c in range(j + 2, base + SUB):
                weight = row_of(column[c // 8], c % 8)
                for v in range(c // 8, groups):
                    columns[c][v] = columns[c][v] - factors[v] * weight
            factors[g] = jnp.where(sub > s, factors[g], 0.0)
            row_u, row_z = row_of(rows_u[g], s), row_of(rows_z[g], s)
            for v in range(g + (s == 7), groups):
                rows_u[v] = rows_u[v] - factors[v] * row_u
                rows_z[v] = rows_z[v] - factors[v] * row_z
    scales = [lax.rsqrt(pivot) for pivot in pivots]
    return (
        [row * scale for row, scale in zip(rows_u, scales)],
        [row * scale for row, scale in zip(rows_z, scales)],
    )


def thirds(value):
    high = value.astype(jnp.bfloat16)
    rest = value - high.astype(jnp.float32)
    middle = rest.astype(jnp.bfloat16)
    return high, middle, (rest - middle.astype(jnp.float32)).astype(jnp.bfloat16)


def exact_dot(left, right, transposed=False):
    axis = 0 if transposed else 1
    left_parts, right_parts = thirds(left), thirds(right)
    terms = ((0, 0), (0, 1), (1, 0), (0, 2), (2, 0), (1, 1))
    count = max(1, min(len(terms), DEPTH // left.shape[axis]))
    total = None
    for start in range(0, len(terms), count):
        some = terms[start : start + count]
        term = lax.dot_general(
            join([left_parts[i] for i, _ in some], axis),
            join([right_parts[j] for _, j in some], 0),
            (((axis,), (0,)), ((), ())),
            preferred_element_type=jnp.float32,
        )
        total = term if total is None else total + term
    return total


def identity_mask(shape):
    return lax.broadcasted_iota(jnp.int32, shape, 0) == lax.broadcasted_iota(jnp.int32, shape, 1)


def factor_block(block):
    unit = identity_mask(block.shape).astype(jnp.float32)
    rows_u = [block[8 * v : 8 * v + 8] for v in range(BLOCK // 8)]
    rows_z = [unit[8 * v : 8 * v + 8] for v in range(BLOCK // 8)]
    groups = STRIPE // 8
    done = []
    for end in range(STRIPE, BLOCK + 1, STRIPE):
        upper, inverse = factor_stripe(rows_u[:groups], rows_z[:groups], end - STRIPE)
        done += inverse
        if end < BLOCK:
            upper, inverse = jnp.concatenate(upper, axis=0), jnp.concatenate(inverse, axis=0)
            update = exact_dot(upper, jnp.concatenate([upper, inverse], axis=1), True)[end:]
            rows_u = [row - update[8 * v : 8 * v + 8, :BLOCK] for v, row in enumerate(rows_u[groups:])]
            rows_z = [row - update[8 * v : 8 * v + 8, BLOCK:] for v, row in enumerate(rows_z[groups:])]
    return jnp.concatenate(done, axis=0)


def cholesky_kernel(ridge_ref, phi_ref, upper_ref, lifted_ref, gram_ref):
    examples, width = phi_ref.shape
    phi = phi_ref[...]
    gram_ref[...] = tdot(phi, phi, None) / float(examples) + jnp.where(
        identity_mask((width, width)), ridge_ref[0], 0.0
    )
    lifted_ref[...] = phi.astype(jnp.float32).T
    square = (BLOCK, BLOCK)
    keep = lax.broadcasted_iota(jnp.int32, square, 0) <= lax.broadcasted_iota(jnp.int32, square, 1)
    block = gram_ref[:BLOCK, :BLOCK]
    for low in range(0, width, BLOCK):
        high = low + BLOCK
        after = high + BLOCK
        current = block
        inverse = factor_block(current)
        if high < width:
            beside = exact_dot(inverse, gram_ref[low:high, high:after])
            block = gram_ref[high:after, high:after] - exact_dot(beside, beside, True)
            upper_ref[low:high, high:after] = beside
        upper_ref[low:high, low:high] = jnp.where(keep, exact_dot(inverse, current), 0.0)
        if low > 0:
            upper_ref[low:high, :low] = jnp.zeros((BLOCK, low), jnp.float32)
        lifted = exact_dot(inverse, lifted_ref[low:high, :])
        lifted_ref[low:high, :] = lifted
        if high < width:
            lifted_ref[high:after, :] = lifted_ref[high:after, :] - exact_dot(beside, lifted, True)
        if after < width:
            beyond = exact_dot(inverse, gram_ref[low:high, after:])
            upper_ref[low:high, after:] = beyond
            gram_ref[high:after, after:] = gram_ref[high:after, after:] - exact_dot(beside, beyond, True)
            gram_ref[after:, after:] = gram_ref[after:, after:] - exact_dot(beyond, beyond, True)
            lifted_ref[after:, :] = lifted_ref[after:, :] - exact_dot(beyond, lifted, True)


def cholesky_panel(ridge_value, phi_panel):
    examples, width = phi_panel.shape
    return pl.pallas_call(
        cholesky_kernel,
        out_shape=(
            jax.ShapeDtypeStruct((width, width), jnp.float32),
            jax.ShapeDtypeStruct((width, examples), jnp.float32),
        ),
        in_specs=[SMEM, VMEM],
        out_specs=(VMEM, VMEM),
        scratch_shapes=[pltpu.VMEM((width, width), jnp.float32)],
        compiler_params=pltpu.CompilerParams(vmem_limit_bytes=32 * 1024 * 1024),
        cost_estimate=pl.CostEstimate(flops=20_000_000_000, bytes_accessed=4_000_000, transcendentals=0),
        name="cholesky_panel",
    )(ridge_value, phi_panel)


def split_dot(left, right):
    total = None
    for _ in range(3):
        part = left.astype(jnp.bfloat16)
        left = left - part.astype(jnp.float32)
        term = jnp.dot(part, right, preferred_element_type=jnp.float32)
        total = term if total is None else total + term
    return total


def finish_kernel(place_ref, ridge_ref, upper_ref, lifted_ref, rows_ref, columns_ref, panel_ref, trailing_ref):
    examples, height = rows_ref.shape
    width = columns_ref.shape[1]
    panel = upper_ref.shape[0]
    row_start = place_ref[0]
    column_start = place_ref[1]
    rows, columns = rows_ref[...], columns_ref[...]
    lifted = lifted_ref[...]
    solved_rows = split_dot(lifted, rows) / float(examples)
    solved_columns = split_dot(lifted, columns) / float(examples)
    for start in range(0, panel, height):
        solved_rows = jnp.where(row_start == start, upper_ref[:, start : start + height], solved_rows)
    for start in range(0, panel, width):
        solved_columns = jnp.where(column_start == start, upper_ref[:, start : start + width], solved_columns)
    panel_ref[...] = solved_rows.T
    shape = (height, width)
    diagonal = row_start + lax.broadcasted_iota(jnp.int32, shape, 0) == column_start + lax.broadcasted_iota(
        jnp.int32, shape, 1
    )
    gram = tdot(rows, columns, None) / float(examples) + jnp.where(diagonal, ridge_ref[0], 0.0)
    trailing_ref[...] = gram - tdot(solved_rows, solved_columns)


def finish(place, ridge_value, upper, lifted, phi_rows, phi_columns):
    height, width = phi_rows.shape[1], phi_columns.shape[1]
    return pl.pallas_call(
        finish_kernel,
        out_shape=(
            jax.ShapeDtypeStruct((height, upper.shape[0]), jnp.float32),
            jax.ShapeDtypeStruct((height, width), jnp.float32),
        ),
        in_specs=[SMEM, SMEM, VMEM, VMEM, VMEM, VMEM],
        out_specs=(VMEM, VMEM),
        compiler_params=pltpu.CompilerParams(vmem_limit_bytes=32 * 1024 * 1024),
        cost_estimate=pl.CostEstimate(flops=2_000_000_000, bytes_accessed=4_000_000, transcendentals=0),
        name="finish",
    )(place, ridge_value, upper, lifted, phi_rows, phi_columns)


def swapped(value, axis, bit):
    return lax.ppermute(value, axis, [(s, s ^ bit) for s in range(lax.axis_size(axis))])


def shards(gradients, selection, seed_value, ridge_value):
    ex_count = lax.axis_size("ex")
    tp_count = lax.axis_size("tp")
    blk_count = lax.axis_size("blk")
    ex_index, tp_index, blk_index = (lax.axis_index(axis) for axis in ("ex", "tp", "blk"))
    coord_dev = gradients.shape[1]
    column_width = HALF * ex_count * blk_count // tp_count
    scaling = 1.0 / math.sqrt(coord_dev * tp_count)
    chosen = gradients[selection]

    feature_ids = jnp.concatenate(
        [
            jnp.arange(PANEL, dtype=jnp.int32),
            (
                (jnp.arange(ex_count, dtype=jnp.int32)[:, None] * blk_count + blk_index) * HALF
                + jnp.arange(HALF, dtype=jnp.int32)[None, :]
            ).reshape(-1),
        ]
    )
    partial = project(chosen, seed_value[0], tp_index * coord_dev, feature_ids)

    half = partial.shape[0] // 2
    low_bit = tp_index % 2
    total = lax.dynamic_slice_in_dim(partial, low_bit * half, half, 0) + swapped(
        lax.dynamic_slice_in_dim(partial, (1 - low_bit) * half, half, 0), "tp", 1
    )
    bit = 2
    while bit < tp_count:
        total = total + swapped(total, "tp", bit)
        bit *= 2
    phi = (total * scaling).astype(jnp.bfloat16)

    column_ex = tp_index * column_width // (blk_count * HALF)

    def group(which):
        return lax.dynamic_slice_in_dim(phi, PANEL + which * HALF, HALF, 1)

    def piece(target):
        return jnp.concatenate([phi[:, :PANEL], group(target), group(column_ex)], axis=1)

    gathered = [piece(ex_index)]
    for step in range(1, ex_count):
        gathered.append(swapped(piece(ex_index ^ step), "ex", step))
    gathered = jnp.concatenate(gathered, axis=0)
    gathered = jnp.concatenate([gathered, swapped(gathered, "tp", 1)], axis=0)
    phi_panel, phi_rows, share = (
        gathered[:, :PANEL],
        gathered[:, PANEL : PANEL + HALF],
        gathered[:, PANEL + HALF :],
    )

    groups = column_width // HALF

    def first_source(tp):
        return tp * groups % blk_count

    columns = [jnp.zeros_like(share)] * groups
    source = first_source(tp_index)
    for step in range(blk_count):
        if step == 0:
            came = share
        else:
            pairs = []
            for tp in range(tp_count):
                for blk in range(blk_count):
                    if first_source(tp) <= blk < first_source(tp) + groups:
                        pairs.append((tp * blk_count + blk, tp * blk_count + (blk ^ step)))
            came = lax.ppermute(share, ("tp", "blk"), pairs)
        for which in range(groups):
            columns[which] = jnp.where(blk_index ^ step == source + which, came, columns[which])
    phi_columns = jnp.concatenate(columns, axis=1)

    upper, lifted = cholesky_panel(ridge_value, phi_panel)
    place = jnp.stack([(ex_index * blk_count + blk_index) * HALF, tp_index * column_width]).astype(jnp.int32)
    return finish(place, ridge_value, upper, lifted, phi_rows, phi_columns)


def solution(mesh):
    in_specs = (P("ex", "tp"), P("ex"), P(), P())
    out_specs = (P(("ex", "blk"), None), P(("ex", "blk"), "tp"))
    return jax.shard_map(shards, mesh=mesh, in_specs=in_specs, out_specs=out_specs, check_vma=False)
```

time: 57.3 us -> 50.8 us (0.89)
  waiting for transfers between devices: 4.32 us -> 11.9 us
  starting transfers between devices: 20 us -> 13.1 us
  Pallas kernels: 20.9 us -> 16 us
  local copies, waits for them, and re-layouts: 2.19 us -> 1.03 us
  matrix products: 6.36 us -> 5.22 us
  other arithmetic: 0.44 us -> 1.07 us
    ppermute x17 -> x7, waiting for transfers between devices: 4.32 us -> 11.9 us  [the longest x4 11.8 us: swapped(): lax.ppermute(value, axis, [(s, s ^ bit) for s in range(lax.axis_size(axis...]
    ppermute x17 -> x7, starting transfers between devices: 20 us -> 13.1 us  [the longest x3 7.82 us: shards(): came = lax.ppermute(share, ('tp', 'blk'), pairs)]
    pallas_call x1, Pallas kernels: 17.7 us -> 12.8 us  [cholesky_panel(): pl.pallas_call(cholesky_kernel, out_shape=(jax.ShapeDtypeStruct((width, w...]
    dot_general x8 -> x4, matrix products: 6.36 us -> 5.22 us  [project(): jnp.dot(chosen[:, start:start + stride], sign_values, preferred_element_t...]
    gather x3 -> x0, local copies, waits for them, and re-layouts: 0.74 us -> none  [shards(): jnp.take(jnp.concatenate(back, axis=2), steps, axis=2).reshape(chunk, -1)]
    select_n x1, other arithmetic: 0.01 us -> 0.66 us  [shards(): chosen = gradients[selection]]
  transfers between devices with their start and end apart: 17 -> 7, of which waited for: 5 -> 4; matrix products, arithmetic and copies ran while one was open for 8% -> 0% of each run, Pallas kernels for 31% -> 25%
where the time goes in v2:
time: 50.8 us; the launch traced here: 50.6 us
  Pallas kernels  16 us (31%)
  starting transfers between devices  13.1 us (26%)
  waiting for transfers between devices  11.9 us (23%)
  matrix products  5.22 us (10%)
  between operations  2.31 us (5%)
  other arithmetic  1.07 us (2%)
  local copies, waits for them, and re-layouts  1.03 us (2%)
    pallas_call x1, Pallas kernels, cholesky_panel(): pl.pallas_call(cholesky_kernel, out_shape=(jax.ShapeDtypeStruct((width, w...  12.8 us
    ppermute x4, waiting for transfers between devices, swapped(): lax.ppermute(value, axis, [(s, s ^ bit) for s in range(lax.axis_size(axis...  11.8 us
    ppermute x3, starting transfers between devices, shards(): came = lax.ppermute(share, ('tp', 'blk'), pairs)  7.82 us
    ppermute x4, starting transfers between devices, swapped(): lax.ppermute(value, axis, [(s, s ^ bit) for s in range(lax.axis_size(axis...  5.32 us
    dot_general x4, matrix products, project(): jnp.dot(chosen[:, start:start + stride], sign_values, preferred_element_t...  5.22 us
    pallas_call x1, Pallas kernels, finish(): pl.pallas_call(finish_kernel, out_shape=(jax.ShapeDtypeStruct((height, up...  3.2 us
  transfers between devices with their start and end apart: 7, of which 4 were waited for; matrix products, arithmetic and copies ran while one was open for 0% of the time, Pallas kernels for 25%

profile of v2, /device:TPU:0, one launch (start us, length us, event | category | flops | bytes accessed | tf_op | source)
XLA Modules:
  0.0 50.6 jit_solution(4807703474112482223)
XLA Ops:
  0.6 0.0 copy-start
  1.4 0.7 %compare_select_fusion = s32[128]{0:T(128)S(1)} fusion(s32[128]{0:T(128)} %param.5), kind=kLoop, calls=%fused_computation.88 | loop fusion | flops 384 | bytes 1024 | tf_op jit(solution)/shard_map/select_n | solution.py:266
  2.1 0.1 add_bitcast_fusion
  2.2 0.0 copy-done
  2.2 0.9 %gather_fusion = bf16[128,2048]{1,0:T(8,128)(2,1)S(1)} fusion(bf16[256,2048]{1,0:T(8,128)(2,1)S(1)} %copy-done, s32[1024]{0:T(1024)S(1)} %pad_clamp_fusion), kind=kCustom, calls=%fused_computation | custom fusion | bytes 1049088 | tf_op jit(solution)/shard_map/gather | solution.py:266
  3.2 1.3 %fusion.58 = f32[128,1024]{1,0:T(8,128)S(1)} fusion(s32[]{:T(128)} %bitcast.6, s32[1024]{0:T(1024)S(1)} %add_multiply_fusion, s32[512]{0:T(512)S(1)} %add_multiply_fusion.4, bf16[128,2048]{1,0:T(8,128)(2,1)S(1)} %gather_fusion), kind=kOutput, calls=%fused_computation.71 | convolution fusion | flops 142082048 | bytes 661508 | tf_op jit(solution)/shard_map/dot_general | solution.py:45
  4.5 1.3 %convolution_add_fusion.2 = f32[128,1024]{1,0:T(8,128)S(1)} fusion(f32[128,1024]{1,0:T(8,128)S(1)} %fusion.58, s32[512]{0:T(512)S(1)} %add_multiply_fusion.3, s32[]{:T(128)} %bitcast.9, s32[1024]{0:T(1024)S(1)} %add_multiply_fusion, bf16[128,2048]{1,0:T(8,128)(2,1)S(1)} %gather_fusion), kind=kOutput, calls=%fused_computation.43 | convolution fusion | flops 142213120 | bytes 1185796 | tf_op jit(solution)/shard_map/dot_general | solution.py:45
  5.8 1.3 %convolution_add_fusion.1 = f32[128,1024]{1,0:T(8,128)S(1)} fusion(f32[128,1024]{1,0:T(8,128)S(1)} %convolution_add_fusion.2, s32[512]{0:T(512)S(1)} %add_multiply_fusion.2, s32[]{:T(128)} %bitcast.8, s32[1024]{0:T(1024)S(1)} %add_multiply_fusion, bf16[128,2048]{1,0:T(8,128)(2,1)S(1)} %gather_fusion), kind=kOutput, calls=%fused_computation.42 | convolution fusion | flops 142213120 | bytes 1185796 | tf_op jit(solution)/shard_map/dot_general | solution.py:45
  7.1 1.3 %convolution_add_fusion = f32[128,1024]{1,0:T(8,128)S(1)} fusion(f32[128,1024]{1,0:T(8,128)S(1)} %convolution_add_fusion.1, s32[512]{0:T(512)S(1)} %add_multiply_fusion.1, s32[]{:T(128)} %bitcast.7, s32[1024]{0:T(1024)S(1)} %add_multiply_fusion, bf16[128,2048]{1,0:T(8,128)(2,1)S(1)} %gather_fusion), kind=kOutput, calls=%fused_computation.41 | convolution fusion | flops 142213120 | bytes 1185796 | tf_op jit(solution)/shard_map/dot_general | solution.py:45
  8.5 0.5 %collective-permute-start = (f32[64,1024]{1,0:T(8,128)S(1)}, f32[64,1024]{1,0:T(8,128)S(1)}, u32[]{:S(2)}, u32[]{:S(2)}) collective-permute-start(f32[64,1024]{1,0:T(8,128)S(1)} %constant_dynamic-slice_fusion.3), channel_id=1, source_target_pairs={{0,4},{4,0},{8,12},{12,8},{1,5},{5,1},{9,13},{13,9},{2,6},{6,2},{1... | collective-permute-start | bytes 786440 | tf_op jit(solution)/shard_map/ppermute | solution.py:255
  9.0 1.2 %collective-permute-done = f32[64,1024]{1,0:T(8,128)S(1)} collective-permute-done((f32[64,1024]{1,0:T(8,128)S(1)}, f32[64,1024]{1,0:T(8,128)S(1)}, u32[]{:S(2)}, u32[]{:S(2)}) %collective-permute-start) | collective-permute-done | bytes 262176 | tf_op jit(solution)/shard_map/ppermute | solution.py:255
  10.2 3.0 %collective-permute-start.1 = (f32[64,1024]{1,0:T(8,128)S(1)}, f32[64,1024]{1,0:T(8,128)S(1)}, u32[]{:S(2)}, u32[]{:S(2)}) collective-permute-start(f32[64,1024]{1,0:T(8,128)S(1)} %dynamic-slice_add_fusion), channel_id=1, source_target_pairs={{0,8},{4,12},{8,0},{12,4},{1,9},{5,13},{9,1},{13,5},{2,10},{6,14},... | collective-permute-start | bytes 786440 | tf_op jit(solution)/shard_map/ppermute | solution.py:255
  13.1 6.6 %collective-permute-done.1 = f32[64,1024]{1,0:T(8,128)S(1)} collective-permute-done((f32[64,1024]{1,0:T(8,128)S(1)}, f32[64,1024]{1,0:T(8,128)S(1)}, u32[]{:S(2)}, u32[]{:S(2)}) %collective-permute-start.1) | collective-permute-done | bytes 262176 | tf_op jit(solution)/shard_map/ppermute | solution.py:255
  19.8 1.8 %collective-permute-start.2 = (bf16[64,1024]{1,0:T(8,128)(2,1)S(1)}, bf16[64,1024]{1,0:T(8,128)(2,1)S(1)}, u32[]{:S(2)}, u32[]{:S(2)}) collective-permute-start(bf16[64,1024]{1,0:T(8,128)(2,1)S(1)} %pad_maximum_fusion.5), channel_id=1, source_target_pairs={{0,16},{16,0},{1,17},{17,1},{2,18},{18,2},{3,19},{19,3},{4,20},{20... | collective-permute-start | bytes 393224 | tf_op jit(solution)/shard_map/ppermute | solution.py:255
  21.6 3.3 %collective-permute-done.2 = bf16[64,1024]{1,0:T(8,128)(2,1)S(1)} collective-permute-done((bf16[64,1024]{1,0:T(8,128)(2,1)S(1)}, bf16[64,1024]{1,0:T(8,128)(2,1)S(1)}, u32[]{:S(2)}, u32[]{:S(2)}) %collective-permute-start.2) | collective-permute-done | bytes 131104 | tf_op jit(solution)/shard_map/ppermute | solution.py:255
  25.0 0.1 collective-permute-start.3
  25.7 0.1 pad_add_fusion.place_ref
  25.8 0.8 %collective-permute-done.3 = bf16[128,1024]{1,0:T(8,128)(2,1)S(1)} collective-permute-done((bf16[128,1024]{1,0:T(8,128)(2,1)S(1)}, bf16[128,1024]{1,0:T(8,128)(2,1)S(1)}, u32[]{:S(2)}, u32[]{:S(2)}) %collective-permute-start.3) | collective-permute-done | bytes 262176 | tf_op jit(solution)/shard_map/ppermute | solution.py:255
  26.6 3.6 %collective-permute-start.6 = (bf16[256,256]{1,0:T(8,128)(2,1)S(1)}, bf16[256,256]{1,0:T(8,128)(2,1)S(1)}, u32[]{:S(2)}, u32[]{:S(2)}) collective-permute-start(bf16[256,256]{1,0:T(8,128)(2,1)S(1)} %get-tuple-element.8), channel_id=1, source_target_pairs={{0,1},{1,0},{6,7},{7,6},{8,9},{9,8},{14,15},{15,14},{16,17},{17,16... | collective-permute-start | bytes 393224 | tf_op jit(solution)/shard_map/ppermute | solution.py:325
  30.2 1.7 %collective-permute-start.5 = (bf16[256,256]{1,0:T(8,128)(2,1)S(1)}, bf16[256,256]{1,0:T(8,128)(2,1)S(1)}, u32[]{:S(2)}, u32[]{:S(2)}) collective-permute-start(bf16[256,256]{1,0:T(8,128)(2,1)S(1)} %get-tuple-element.8), channel_id=1, source_target_pairs={{0,2},{1,3},{6,4},{7,5},{8,10},{9,11},{14,12},{15,13},{16,18},{17,... | collective-permute-start | bytes 393224 | tf_op jit(solution)/shard_map/ppermute | solution.py:325
  31.9 2.5 %collective-permute-start.4 = (bf16[256,256]{1,0:T(8,128)(2,1)S(1)}, bf16[256,256]{1,0:T(8,128)(2,1)S(1)}, u32[]{:S(2)}, u32[]{:S(2)}) collective-permute-start(bf16[256,256]{1,0:T(8,128)(2,1)S(1)} %get-tuple-element.8), channel_id=1, source_target_pairs={{0,3},{1,2},{6,5},{7,4},{8,11},{9,10},{14,13},{15,12},{16,19},{17,... | collective-permute-start | bytes 393224 | tf_op jit(solution)/shard_map/ppermute | solution.py:325
  34.5 12.8 %cholesky_panel.1 = (f32[512,512]{1,0:T(8,128)S(1)}, f32[512,256]{1,0:T(8,128)S(1)}) custom-call(f32[1]{0:T(128)S(6)} %copy.8.ridge_ref, bf16[256,512]{1,0:T(8,128)(2,1)S(1)} %slice.40.phi_ref), custom_call_target="tpu_custom_call" | custom-call | flops 20000000000 | bytes 4000000 | tf_op jit(solution)/shard_map/cholesky_panel/pallas_call | solution.py:190
  47.3 0.0 collective-permute-done.6
  47.3 0.0 collective-permute-done.5
  47.3 0.0 collective-permute-done.4
  47.3 0.1 select_select_fusion.1
  47.4 3.2 %finish.1 = (f32[256,512]{1,0:T(8,128)}, f32[256,512]{1,0:T(8,128)}) custom-call(s32[2]{0:T(128)S(1)} %pad_add_fusion.place_ref, f32[1]{0:T(128)S(6)} %copy.8.ridge_ref, f32[512,512]{1,0:T(8,128)S(1)} %get-tuple-element.4.upper_ref, f32[512,256]{1,0:T(8,128)S(1)} %get-tuple-element.5.lifted_ref, bf16[256,256]{1,0:T(8,128)(2,1)S(1)} %get-tuple-element.9.rows_ref, ...), custom_call_target="tpu_custom_call" | custom-call | flops 2000000000 | bytes 4000000 | tf_op jit(solution)/shard_map/finish/pallas_call | solution.py:240
  (20 shorter events, 0.3 us)
Async XLA Ops:
  0.6 1.6 %copy-start = (bf16[256,2048]{1,0:T(8,128)(2,1)S(1)}, bf16[256,2048]{1,0:T(8,128)(2,1)}, u32[]{:S(2)}) copy-start(bf16[256,2048]{1,0:T(8,128)(2,1)} %param.4) | copy-start | bytes 3145732
  8.5 1.7 %collective-permute-start = (f32[64,1024]{1,0:T(8,128)S(1)}, f32[64,1024]{1,0:T(8,128)S(1)}, u32[]{:S(2)}, u32[]{:S(2)}) collective-permute-start(f32[64,1024]{1,0:T(8,128)S(1)} %constant_dynamic-slice_fusion.3), channel_id=1, source_target_pairs={{0,4},{4,0},{8,12},{12,8},{1,5},{5,1},{9,13},{13,9},{2,6},{6,2},{1... | collective-permute-start | bytes 786440 | tf_op jit(solution)/shard_map/ppermute | solution.py:255
  10.2 9.6 %collective-permute-start.1 = (f32[64,1024]{1,0:T(8,128)S(1)}, f32[64,1024]{1,0:T(8,128)S(1)}, u32[]{:S(2)}, u32[]{:S(2)}) collective-permute-start(f32[64,1024]{1,0:T(8,128)S(1)} %dynamic-slice_add_fusion), channel_id=1, source_target_pairs={{0,8},{4,12},{8,0},{12,4},{1,9},{5,13},{9,1},{13,5},{2,10},{6,14},... | collective-permute-start | bytes 786440 | tf_op jit(solution)/shard_map/ppermute | solution.py:255
  19.8 5.1 %collective-permute-start.2 = (bf16[64,1024]{1,0:T(8,128)(2,1)S(1)}, bf16[64,1024]{1,0:T(8,128)(2,1)S(1)}, u32[]{:S(2)}, u32[]{:S(2)}) collective-permute-start(bf16[64,1024]{1,0:T(8,128)(2,1)S(1)} %pad_maximum_fusion.5), channel_id=1, source_target_pairs={{0,16},{16,0},{1,17},{17,1},{2,18},{18,2},{3,19},{19,3},{4,20},{20... | collective-permute-start | bytes 393224 | tf_op jit(solution)/shard_map/ppermute | solution.py:255
  25.0 1.6 %collective-permute-start.3 = (bf16[128,1024]{1,0:T(8,128)(2,1)S(1)}, bf16[128,1024]{1,0:T(8,128)(2,1)S(1)}, u32[]{:S(2)}, u32[]{:S(2)}) collective-permute-start(bf16[128,1024]{1,0:T(8,128)(2,1)S(1)} %pad_maximum_fusion.1), channel_id=1, source_target_pairs={{0,4},{4,0},{8,12},{12,8},{1,5},{5,1},{9,13},{13,9},{2,6},{6,2},{1... | collective-permute-start | bytes 786440 | tf_op jit(solution)/shard_map/ppermute | solution.py:255
  26.6 20.7 %collective-permute-start.6 = (bf16[256,256]{1,0:T(8,128)(2,1)S(1)}, bf16[256,256]{1,0:T(8,128)(2,1)S(1)}, u32[]{:S(2)}, u32[]{:S(2)}) collective-permute-start(bf16[256,256]{1,0:T(8,128)(2,1)S(1)} %get-tuple-element.8), channel_id=1, source_target_pairs={{0,1},{1,0},{6,7},{7,6},{8,9},{9,8},{14,15},{15,14},{16,17},{17,16... | collective-permute-start | bytes 393224 | tf_op jit(solution)/shard_map/ppermute | solution.py:325
  30.2 17.0 %collective-permute-start.5 = (bf16[256,256]{1,0:T(8,128)(2,1)S(1)}, bf16[256,256]{1,0:T(8,128)(2,1)S(1)}, u32[]{:S(2)}, u32[]{:S(2)}) collective-permute-start(bf16[256,256]{1,0:T(8,128)(2,1)S(1)} %get-tuple-element.8), channel_id=1, source_target_pairs={{0,2},{1,3},{6,4},{7,5},{8,10},{9,11},{14,12},{15,13},{16,18},{17,... | collective-permute-start | bytes 393224 | tf_op jit(solution)/shard_map/ppermute | solution.py:325
  31.9 15.4 %collective-permute-start.4 = (bf16[256,256]{1,0:T(8,128)(2,1)S(1)}, bf16[256,256]{1,0:T(8,128)(2,1)S(1)}, u32[]{:S(2)}, u32[]{:S(2)}) collective-permute-start(bf16[256,256]{1,0:T(8,128)(2,1)S(1)} %get-tuple-element.8), channel_id=1, source_target_pairs={{0,3},{1,2},{6,5},{7,4},{8,11},{9,10},{14,13},{15,12},{16,19},{17,... | collective-permute-start | bytes 393224 | tf_op jit(solution)/shard_map/ppermute | solution.py:325

commit v3 on v0

v3 whole, which is shorter than its diff:
```python
import functools
import math

import jax
import jax.numpy as jnp
import numpy as np
from jax import lax
from jax.experimental import pallas as pl
from jax.experimental.pallas import tpu as pltpu
from jax.sharding import PartitionSpec as P

PANEL = 512
HALF = 256
STRIPE = 32
SUB = 16
BLOCK = 128
DEPTH = 256
SEGMENT = 128
SECOND_BY_8 = int(np.array(-1028477387 << 8 & 0xFFFFFFFF, np.uint32).astype(np.int32))
SECOND_BY_24 = int(np.array(-1028477387 << 24 & 0xFFFFFFFF, np.uint32).astype(np.int32))
VMEM = pl.BlockSpec(memory_space=pltpu.VMEM)
SMEM = pl.BlockSpec(memory_space=pltpu.SMEM)
ANYWHERE = pl.BlockSpec(memory_space=pl.ANY)


def call(kernel, out_shape, in_specs, microseconds, name, scratch=(), vmem=16):
    shapes = [jax.ShapeDtypeStruct(shape, dtype) for shape, dtype in out_shape]
    return pl.pallas_call(
        kernel,
        out_shape=shapes,
        in_specs=in_specs,
        out_specs=[VMEM] * len(shapes),
        scratch_shapes=list(scratch),
        compiler_params=pltpu.CompilerParams(vmem_limit_bytes=vmem * 1024 * 1024),
        cost_estimate=pl.CostEstimate(
            flops=int(microseconds * 1_100_000_000), bytes_accessed=1_000_000, transcendentals=0
        ),
        name=name,
    )


def join(parts, axis):
    return parts[0] if len(parts) == 1 else jnp.concatenate(parts, axis)


def shifted(value, amount):
    return lax.shift_right_logical(value, jnp.full_like(value, amount))


def sign_tile(seed_word, coordinate, feature, shape):
    rows = (lax.broadcasted_iota(jnp.int32, (shape[0], 1), 0) + coordinate) * jnp.int32(-1640531535)
    columns = (lax.broadcasted_iota(jnp.int32, (1, shape[1]), 1) + feature) * jnp.int32(668265263) + seed_word
    hashed = rows + columns
    hashed = (hashed ^ shifted(hashed, 16)) * jnp.int32(-2048144789)
    hashed = hashed ^ shifted(hashed, 13)
    decided = (hashed * jnp.int32(SECOND_BY_8)) ^ (hashed * jnp.int32(SECOND_BY_24))
    return jnp.where(decided < 0, -1.0, 1.0).astype(jnp.bfloat16)


def segment_signs(words_ref, feature, width, index):
    return sign_tile(words_ref[0], words_ref[1] + index * SEGMENT, feature, (SEGMENT, width))


def project_step(words_ref, chosen_ref, feature, width, index, total):
    start = pl.multiple_of(index * SEGMENT, SEGMENT)
    signs = segment_signs(words_ref, feature, width, index)
    return total + jnp.dot(chosen_ref[:, pl.ds(start, SEGMENT)], signs, preferred_element_type=jnp.float32)


def project_tile(words_ref, chosen_ref, feature, width, unroll):
    rows, coordinates = chosen_ref.shape
    step = functools.partial(project_step, words_ref, chosen_ref, feature, width)
    zero = jnp.zeros((rows, width), jnp.float32)
    return lax.fori_loop(0, coordinates // SEGMENT, step, zero, unroll=unroll)


def panel_signs_kernel(words_ref, signs_ref):
    coordinates, width = signs_ref.shape
    for step in range(coordinates // SEGMENT):
        signs_ref[step * SEGMENT : (step + 1) * SEGMENT, :] = segment_signs(words_ref, 0, width, step)


def panel_signs(words, coordinates):
    return call(
        panel_signs_kernel, [((coordinates, PANEL), jnp.bfloat16)], [SMEM], 2, "panel_signs"
    )(words)[0]


def panel_part_kernel(words_ref, selection_ref, pool_ref, signs_ref, mine_ref, theirs_ref, chosen_ref):
    half = mine_ref.shape[0]
    shape = (pool_ref.shape[0], chosen_ref.shape[0])
    picked = jnp.where(lax.broadcasted_iota(jnp.int32, shape, 0) == selection_ref[...], 1.0, 0.0)
    chosen = tdot(picked.astype(jnp.bfloat16), pool_ref[...]).astype(jnp.bfloat16)
    chosen_ref[...] = chosen
    total = jnp.dot(chosen, signs_ref[...], preferred_element_type=jnp.float32)
    even = words_ref[2] == 0
    mine_ref[...] = jnp.where(even, total[:half], total[half:])
    theirs_ref[...] = jnp.where(even, total[half:], total[:half])


def panel_part(words, selection, pool):
    rows, coordinates = selection.shape[0], pool.shape[1]
    return call(
        panel_part_kernel,
        [((rows // 2, PANEL), jnp.float32)] * 2 + [((rows, coordinates), jnp.bfloat16)],
        [SMEM, VMEM, VMEM, VMEM],
        1,
        "panel_part",
    )(words, selection[None, :], pool, panel_signs(words, coordinates))


def blocks_part_kernel(blocks, words_ref, chosen_ref, _, *part_refs):
    width = part_refs[0].shape[1]
    for block, part_ref in zip(blocks, part_refs):
        part_ref[...] = project_tile(words_ref, chosen_ref, block * width, width, len(blocks) <= 2)


def blocks_part(words, chosen, blocks, width, after):
    return call(
        functools.partial(blocks_part_kernel, blocks),
        [((chosen.shape[0], width), jnp.float32)] * len(blocks),
        [SMEM, VMEM, ANYWHERE],
        2 * len(blocks),
        "blocks_part",
        vmem=32 if len(blocks) > 2 else 16,
    )(words, chosen, after)


def other_parts_kernel(tp_count, blk_count, words_ref, chosen_ref, _, *refs):
    *first_refs, mine_ref, theirs_ref = refs
    rows = chosen_ref.shape[0]
    half = rows // 2
    width = first_refs[0].shape[1]
    groups = width // HALF
    row_lanes = tp_count * groups // blk_count * HALF
    even = words_ref[2] == 0
    for ref in (mine_ref, theirs_ref):
        ref[:, : row_lanes + 2 * width] = jnp.zeros((half, row_lanes + 2 * width), jnp.float32)

    def place(ref, lane, part):
        ref[:, lane : lane + width] = part[:half]
        ref[:, lane + width : lane + 2 * width] = part[half:]

    for block in range(1, tp_count):
        lane = row_lanes + block // 2 * 2 * width
        if block <= len(first_refs):
            part = first_refs[block - 1][...]
        else:
            part = project_tile(words_ref, chosen_ref, block * width, width, tp_count <= 4)
        own = words_ref[2] == block % 2
        pl.when(own)(functools.partial(place, mine_ref, lane, part))
        pl.when(jnp.logical_not(own))(functools.partial(place, theirs_ref, lane, part))
        for which in range(groups):
            group = block * groups + which

            @pl.when(words_ref[3] == group % blk_count)
            def _(part=part[:, which * HALF : (which + 1) * HALF], lane=group // blk_count * HALF):
                mine_ref[:, lane : lane + HALF] = jnp.where(even, part[:half], part[half:])
                theirs_ref[:, lane : lane + HALF] = jnp.where(even, part[half:], part[:half])


def other_parts(words, chosen, first, tp_count, blk_count, after):
    rows, width = first[0].shape
    lanes = tp_count * (width // HALF) // blk_count * HALF + tp_count // 2 * 2 * width
    return call(
        functools.partial(other_parts_kernel, tp_count, blk_count),
        [((rows // 2, lanes), jnp.float32)] * 2,
        [SMEM, VMEM, ANYWHERE] + [VMEM] * len(first),
        2 * (tp_count - 1 - len(first)),
        "other_parts",
        vmem=16 if tp_count <= 4 else 48,
    )(words, chosen, after, *first)


def halve_kernel(row_lanes, bit, words_ref, left_ref, right_ref, keep_ref, send_ref):
    upper = words_ref[4] & bit != 0
    rows = left_ref[:, :row_lanes] + right_ref[:, :row_lanes]
    columns = left_ref[:, row_lanes:] + right_ref[:, row_lanes:]
    middle = columns.shape[1] // 2
    keep_ref[:, :row_lanes] = rows
    send_ref[:, :row_lanes] = rows
    keep_ref[:, row_lanes:] = jnp.where(upper, columns[:, middle:], columns[:, :middle])
    send_ref[:, row_lanes:] = jnp.where(upper, columns[:, :middle], columns[:, middle:])


def halve(words, left, right, row_lanes, bit):
    shape = (left.shape[0], (left.shape[1] + row_lanes) // 2)
    return call(
        functools.partial(halve_kernel, row_lanes, bit),
        [(shape, jnp.float32)] * 2,
        [SMEM, VMEM, VMEM],
        0.5,
        "halve",
    )(words, left, right)


def pieces_kernel(ex_count, scaling, words_ref, left_ref, right_ref, _, *piece_refs):
    row_lanes = ex_count * HALF
    total = ((left_ref[...] + right_ref[...]) * scaling).astype(jnp.bfloat16)
    for step, ref in enumerate(piece_refs):
        target = words_ref[5] ^ step
        rows = total[:, :HALF]
        for index in range(1, ex_count):
            rows = jnp.where(target == index, total[:, index * HALF : (index + 1) * HALF], rows)
        ref[:, :HALF] = rows
        ref[:, HALF:] = total[:, row_lanes:]


def pieces(words, left, right, ex_count, scaling, after):
    shape = (left.shape[0], left.shape[1] - (ex_count - 1) * HALF)
    return call(
        functools.partial(pieces_kernel, ex_count, scaling),
        [(shape, jnp.bfloat16)] * ex_count,
        [SMEM, VMEM, VMEM, ANYWHERE],
        0.5,
        "pieces",
    )(words, left, right, after)


def tdot(left, right):
    return lax.dot_general(left, right, (((0,), (0,)), ((), ())), preferred_element_type=jnp.float32)


def row_of(value, row):
    return jnp.broadcast_to(value[row : row + 1, :], value.shape)


def factor_stripe(rows_u, rows_z, offset):
    groups = len(rows_u)
    sub = lax.broadcasted_iota(jnp.int32, (8, BLOCK), 0)
    rows_u, rows_z = list(rows_u), list(rows_z)
    pivots = [jnp.ones((8, BLOCK), jnp.float32) for _ in range(groups)]
    for base in range(0, 8 * groups, SUB):
        columns = {
            c: {
                v: jnp.broadcast_to(rows_u[v][:, offset + c : offset + c + 1], (8, BLOCK))
                for v in range(c // 8, groups)
            }
            for c in range(base, base + SUB)
        }
        pivot = row_of(columns[base][base // 8], 0)
        for j in range(base, base + SUB):
            g, s = divmod(j, 8)
            column = columns[j]
            inverse = 1.0 / pivot
            pivots[g] = jnp.where(sub == s, pivot, pivots[g])
            if j + 1 < base + SUB:
                n, r = divmod(j + 1, 8)
                weight = row_of(column[n], r)
                following = columns[j + 1]
                pivot = row_of(following[n], r) - (weight * weight) * inverse
                for v in range(n, groups):
                    following[v] = following[v] - (column[v] * weight) * inverse
            factors = {v: column[v] * inverse for v in range(g, groups)}
            for c in range(j + 2, base + SUB):
                weight = row_of(column[c // 8], c % 8)
                for v in range(c // 8, groups):
                    columns[c][v] = columns[c][v] - factors[v] * weight
            factors[g] = jnp.where(sub > s, factors[g], 0.0)
            row_u, row_z = row_of(rows_u[g], s), row_of(rows_z[g], s)
            for v in range(g + (s == 7), groups):
                rows_u[v] = rows_u[v] - factors[v] * row_u
                rows_z[v] = rows_z[v] - factors[v] * row_z
    scales = [lax.rsqrt(pivot) for pivot in pivots]
    return (
        [row * scale for row, scale in zip(rows_u, scales)],
        [row * scale for row, scale in zip(rows_z, scales)],
    )


def thirds(value):
    high = value.astype(jnp.bfloat16)
    rest = value - high.astype(jnp.float32)
    middle = rest.astype(jnp.bfloat16)
    return high, middle, (rest - middle.astype(jnp.float32)).astype(jnp.bfloat16)


def exact_dot(left, right, transposed=False):
    axis = 0 if transposed else 1
    left_parts, right_parts = thirds(left), thirds(right)
    terms = ((0, 0), (0, 1), (1, 0), (0, 2), (2, 0), (1, 1))
    count = max(1, min(len(terms), DEPTH // left.shape[axis]))
    total = None
    for start in range(0, len(terms), count):
        some = terms[start : start + count]
        term = lax.dot_general(
            join([left_parts[i] for i, _ in some], axis),
            join([right_parts[j] for _, j in some], 0),
            (((axis,), (0,)), ((), ())),
            preferred_element_type=jnp.float32,
        )
        total = term if total is None else total + term
    return total


def sum_kernel(scaling, left_ref, right_ref, _, sum_ref):
    sum_ref[...] = ((left_ref[...] + right_ref[...]) * scaling).astype(jnp.bfloat16)


def scaled_sum(left, right, scaling, after):
    return pl.pallas_call(
        functools.partial(sum_kernel, scaling),
        out_shape=jax.ShapeDtypeStruct(left.shape, jnp.bfloat16),
        in_specs=[VMEM, VMEM, ANYWHERE],
        out_specs=VMEM,
        cost_estimate=pl.CostEstimate(flops=1_000_000, bytes_accessed=1_000_000, transcendentals=0),
        name="scaled_sum",
    )(left, right, after)


def identity_mask(shape):
    return lax.broadcasted_iota(jnp.int32, shape, 0) == lax.broadcasted_iota(jnp.int32, shape, 1)


def factor_block(block):
    unit = identity_mask(block.shape).astype(jnp.float32)
    rows_u = [block[8 * v : 8 * v + 8] for v in range(BLOCK // 8)]
    rows_z = [unit[8 * v : 8 * v + 8] for v in range(BLOCK // 8)]
    groups = STRIPE // 8
    done = []
    for end in range(STRIPE, BLOCK + 1, STRIPE):
        upper, inverse = factor_stripe(rows_u[:groups], rows_z[:groups], end - STRIPE)
        done += inverse
        if end < BLOCK:
            upper, inverse = jnp.concatenate(upper, axis=0), jnp.concatenate(inverse, axis=0)
            update = exact_dot(upper, jnp.concatenate([upper, inverse], axis=1), True)[end:]
            rows_u = [row - update[8 * v : 8 * v + 8, :BLOCK] for v, row in enumerate(rows_u[groups:])]
            rows_z = [row - update[8 * v : 8 * v + 8, BLOCK:] for v, row in enumerate(rows_z[groups:])]
    return jnp.concatenate(done, axis=0)


def in_pair_order(even, refs, lanes=slice(None)):
    values = [ref[:, lanes] for ref in refs]
    count = len(values) // 2
    mine, other = join(values[:count], 0), join(values[count:], 0)
    return join([jnp.where(even, mine, other), jnp.where(even, other, mine)], 0)


def eliminate(gram, lifted, upper_ref, done_ref, gram_ref, lifted_ref):
    inverse = factor_block(gram(slice(0, BLOCK), slice(0, BLOCK)))
    square = (BLOCK, BLOCK)
    keep = lax.broadcasted_iota(jnp.int32, square, 0) <= lax.broadcasted_iota(jnp.int32, square, 1)
    upper = exact_dot(inverse, gram(slice(0, BLOCK), slice(None)))
    upper_ref[:, :BLOCK] = jnp.where(keep, upper[:, :BLOCK], 0.0)
    done = exact_dot(inverse, lifted(slice(0, BLOCK)))
    done_ref[...] = done
    if gram_ref is not None:
        rest = upper[:, BLOCK:]
        upper_ref[:, BLOCK:] = rest
        gram_ref[...] = gram(slice(BLOCK, None), slice(BLOCK, None)) - exact_dot(rest, rest, True)
        lifted_ref[...] = lifted(slice(BLOCK, None)) - exact_dot(rest, done, True)


def first_block_kernel(words_ref, ridge_ref, *refs):
    *phi_refs, upper_ref, done_ref, gram_ref, lifted_ref, whole_ref, turned_ref = refs
    phi = in_pair_order(words_ref[2] == 0, phi_refs)
    examples, width = phi.shape
    whole_ref[...] = tdot(phi, phi) * (1.0 / examples) + jnp.where(
        identity_mask((width, width)), ridge_ref[0], 0.0
    )
    turned_ref[...] = phi.astype(jnp.float32).T
    eliminate(
        lambda rows, lanes: whole_ref[rows, lanes],
        lambda rows: turned_ref[rows, :],
        upper_ref,
        done_ref,
        gram_ref,
        lifted_ref,
    )


def block_kernel(gram_in, lifted_in, upper_ref, done_ref, gram_ref=None, lifted_ref=None):
    eliminate(
        lambda rows, lanes: gram_in[rows, lanes],
        lambda rows: lifted_in[rows, :],
        upper_ref,
        done_ref,
        gram_ref,
        lifted_ref,
    )


def block_shapes(width, examples):
    rest = width - BLOCK
    shapes = [(BLOCK, width), (BLOCK, examples)]
    if rest:
        shapes += [(rest, rest), (rest, examples)]
    return [(shape, jnp.float32) for shape in shapes]


def first_block(words, ridge_value, phi):
    examples, width = sum(part.shape[0] for part in phi), phi[0].shape[1]
    return call(
        first_block_kernel,
        block_shapes(width, examples),
        [SMEM, SMEM] + [VMEM] * len(phi),
        3.5,
        "gram_first_block",
        [pltpu.VMEM((width, width), jnp.float32), pltpu.VMEM((width, examples), jnp.float32)],
    )(words, ridge_value, *phi)


def next_block(gram, lifted, microseconds):
    return call(
        block_kernel, block_shapes(gram.shape[0], lifted.shape[1]), [VMEM, VMEM], microseconds, "eliminate_block"
    )(gram, lifted)


def finish_kernel(blocks, count, words_ref, ridge_ref, *refs):
    uppers, dones = refs[:blocks], refs[blocks : 2 * blocks]
    phi_refs, piece_refs = refs[2 * blocks : 2 * blocks + count], refs[2 * blocks + count : -3]
    panel_ref, trailing_ref, solved_ref = refs[-3:]
    height, panel = panel_ref.shape
    width = trailing_ref.shape[1]
    even = words_ref[2] == 0
    row_group, column_block = words_ref[6], words_ref[4]
    phi = in_pair_order(even, phi_refs)
    examples = phi.shape[0]
    rows = in_pair_order(even, piece_refs, slice(0, height))
    for start in range(0, panel, height):
        rows = jnp.where(row_group * height == start, phi[:, start : start + height], rows)
    mine = piece_refs[: count // 2]
    columns = join(
        [ref[:, start : start + width] for start in (height, height + width) for ref in mine], 0
    )
    columns = jnp.where(column_block == 0, phi, columns)
    parts = thirds(join([ref[...] for ref in dones], 0))
    parts = join(list(parts), 1)
    scale = 1.0 / examples
    solved_ref[...] = jnp.dot(parts, join([columns] * 3, 0), preferred_element_type=jnp.float32) * scale
    panel_ref[...] = (
        lax.dot_general(
            join([rows] * 3, 0), parts, (((0,), (1,)), ((), ())), preferred_element_type=jnp.float32
        )
        * scale
    )

    @pl.when(column_block == 0)
    def _():
        for index, ref in enumerate(uppers):
            low = index * BLOCK
            if low:
                solved_ref[low : low + BLOCK, :low] = jnp.zeros((BLOCK, low), jnp.float32)
            solved_ref[low : low + BLOCK, low:] = ref[...]

    for group in range(panel // height):

        @pl.when(row_group == group)
        def _(left=group * height, right=(group + 1) * height):
            for index, ref in enumerate(uppers):
                low = index * BLOCK
                lanes = slice(low, low + BLOCK)
                for start in range(left, right, BLOCK):
                    if start < low:
                        value = jnp.zeros((BLOCK, BLOCK), jnp.float32)
                    else:
                        value = ref[:, start - low : start - low + BLOCK].T
                    panel_ref[start - left : start - left + BLOCK, lanes] = value

    shape = (height, width)
    diagonal = row_group * height + lax.broadcasted_iota(
        jnp.int32, shape, 0
    ) == column_block * width + lax.broadcasted_iota(jnp.int32, shape, 1)
    gram = tdot(rows, columns) * scale + jnp.where(diagonal, ridge_ref[0], 0.0)
    trailing_ref[...] = gram - exact_dot(panel_ref[...], solved_ref[...])


def finish(words, ridge_value, uppers, dones, phi, gathered, height, width):
    panel = uppers[0].shape[1]
    operands = [*uppers, *dones, *phi, *gathered]
    return call(
        functools.partial(finish_kernel, len(uppers), len(phi)),
        [((height, panel), jnp.float32), ((height, width), jnp.float32)],
        [SMEM, SMEM] + [VMEM] * len(operands),
        3,
        "finish",
        [pltpu.VMEM((panel, width), jnp.float32)],
        vmem=24,
    )(words, ridge_value, *operands)


def swapped(value, axis, bit):
    return lax.ppermute(value, axis, [(s, s ^ bit) for s in range(lax.axis_size(axis))])


def ex_parts(own):
    return [own[0]] + [swapped(own[step], "ex", step) for step in range(1, lax.axis_size("ex"))]


def with_pair(parts):
    return list(parts) + [swapped(part, "tp", 1) for part in parts]


def shards(gradients, selection, seed_value, ridge_value):
    ex_count = lax.axis_size("ex")
    tp_count = lax.axis_size("tp")
    blk_count = lax.axis_size("blk")
    ex_index, tp_index, blk_index = (lax.axis_index(axis) for axis in ("ex", "tp", "blk"))
    coord_dev = gradients.shape[1]
    column_width = HALF * ex_count * blk_count // tp_count
    row_lanes = ex_count * HALF
    scaling = 1.0 / math.sqrt(coord_dev * tp_count)
    words = jnp.stack(
        [
            seed_value[0],
            tp_index * coord_dev,
            tp_index % 2,
            blk_index,
            tp_index,
            ex_index,
            ex_index * blk_count + blk_index,
        ]
    ).astype(jnp.int32)

    mine, theirs, chosen = panel_part(words, selection, gradients)
    total = mine + swapped(theirs, "tp", 1)
    halves = total
    bit = 2
    while bit < tp_count:
        total = total + swapped(total, "tp", bit)
        bit *= 2
    phi = ex_parts([(total * scaling).astype(jnp.bfloat16)] * ex_count)

    first = blocks_part(words, chosen, range(1, 1 + tp_count // 2), column_width, halves)
    left, right = other_parts(words, chosen, first, tp_count, blk_count, total)
    right = swapped(right, "tp", 1)
    bit = tp_count // 2
    while bit > 1:
        left, right = halve(words, left, right, row_lanes, bit)
        right = swapped(right, "tp", bit)
        bit //= 2

    phi[1:], left = lax.optimization_barrier((phi[1:], left))
    phi = with_pair(phi)
    uppers, dones = [], []
    upper, done, *rest = first_block(words, ridge_value, phi)
    while True:
        uppers.append(upper)
        dones.append(done)
        if not rest:
            break
        upper, done, *rest = next_block(*rest, 0.3 if len(dones) < 2 else 4)
    gathered = pieces(words, left, right, ex_count, scaling, dones[len(dones) // 2 - 1])
    gathered = with_pair(ex_parts(gathered))
    return tuple(finish(words, ridge_value, uppers, dones, phi, gathered, HALF, column_width))


def solution(mesh):
    in_specs = (P("ex", "tp"), P("ex"), P(), P())
    out_specs = (P(("ex", "blk"), None), P(("ex", "blk"), "tp"))
    return jax.shard_map(shards, mesh=mesh, in_specs=in_specs, out_specs=out_specs, check_vma=False)
```

time: 366 us -> 45.8 us (0.13); the launches traced: 362 us -> 45.6 us
  waiting for transfers between devices: 157 us -> 6.13 us
  other arithmetic: 124 us -> 0.04 us
  Pallas kernels: 0 us -> 29.3 us
  blocking collectives: 20.5 us -> 0 us
  matrix products: 20.1 us -> 0 us
  local copies, waits for them, and re-layouts: 18 us -> 0.09 us
  between operations: 18.8 us -> 2.09 us
  starting transfers between devices: 3.67 us -> 7.99 us
    psum x3 -> x0, waiting for transfers between devices: 157 us -> none  [the longest x2 123 us: from_root(): return lax.psum(kept, axis)]
    another operation x18 -> x0, other arithmetic: 119 us -> none  [the longest x15 79.4 us: shards(): factor = jnp.linalg.cholesky(diag_block)]
    pallas_call x0 -> x11, Pallas kernels: none -> 29.3 us  [the longest x3 9.52 us: next_block(): call(block_kernel, block_shapes(gram.shape[0], lifted.shape[1]), [VMEM, V...]
    all_gather x2 -> x0, blocking collectives: 20.5 us -> none  [the longest x1 14.8 us: shards(): gathered = lax.all_gather(phi_columns, 'blk', axis=1, tiled=True)]
    another operation x20 -> x0, matrix products: 14.1 us -> none  [the longest x6 5.92 us: shards(): factor = jnp.linalg.cholesky(diag_block)]
    another operation x34 -> x1, local copies, waits for them, and re-layouts: 9 us -> 0.09 us  [shards(): jnp.stack([seed_value[0], tp_index * coord_dev, tp_index % 2, blk_index,...]
    ppermute x0 -> x10, starting transfers between devices: none -> 7.99 us  [swapped(): lax.ppermute(value, axis, [(s, s ^ bit) for s in range(lax.axis_size(axis...]
    ppermute x0 -> x10, waiting for transfers between devices: none -> 6.13 us  [swapped(): lax.ppermute(value, axis, [(s, s ^ bit) for s in range(lax.axis_size(axis...]
  transfers between devices with their start and end apart: 4 -> 10, of which waited for: 3 -> 5; matrix products, arithmetic and copies ran while one was open for 0% -> 0% of each run, Pallas kernels for 0% -> 42%
where the time goes in v3:
time: 45.8 us; the launch traced here: 45.6 us
  Pallas kernels  29.3 us (64%)
  starting transfers between devices  7.99 us (17%)
  waiting for transfers between devices  6.13 us (13%)
  between operations  2.09 us (5%)
    pallas_call x3, Pallas kernels, next_block(): call(block_kernel, block_shapes(gram.shape[0], lifted.shape[1]), [VMEM, V...  9.52 us
    ppermute x10, starting transfers between devices, swapped(): lax.ppermute(value, axis, [(s, s ^ bit) for s in range(lax.axis_size(axis...  7.99 us
    ppermute x10, waiting for transfers between devices, swapped(): lax.ppermute(value, axis, [(s, s ^ bit) for s in range(lax.axis_size(axis...  6.13 us
    pallas_call x1, Pallas kernels, first_block(): call(first_block_kernel, block_shapes(width, examples), [SMEM, SMEM] + [V...  4.43 us
    pallas_call x1, Pallas kernels, blocks_part(): call(functools.partial(blocks_part_kernel, blocks), [((chosen.shape[0], w...  4.41 us
    pallas_call x1, Pallas kernels, finish(): call(functools.partial(finish_kernel, len(uppers), len(phi)), [((height,...  3.44 us
    pallas_call x1, Pallas kernels, other_parts(): call(functools.partial(other_parts_kernel, tp_count, blk_count), [((rows...  2.91 us
    pallas_call x1, Pallas kernels, panel_signs(): call(panel_signs_kernel, [((coordinates, PANEL), jnp.bfloat16)], [SMEM],...  2.19 us
  transfers between devices with their start and end apart: 10, of which 5 were waited for; matrix products, arithmetic and copies ran while one was open for 0% of the time, Pallas kernels for 42%

profile of v3, /device:TPU:0, one launch (start us, length us, event | category | flops | bytes accessed | tf_op | source)
XLA Modules:
  0.0 45.6 jit_solution(14097396010922826228)
XLA Ops:
  1.3 0.1 stack.27.words_ref
  1.4 0.0 copy-start
  1.4 0.0 copy-start.1
  1.4 2.2 %panel_signs.1.signs_ref = bf16[2048,512]{1,0:T(8,128)(2,1)S(1)} custom-call(s32[7]{0:T(128)S(1)} %stack.27.words_ref), custom_call_target="tpu_custom_call" | custom-call | flops 2200000000 | bytes 1000000 | tf_op jit(solution)/shard_map/panel_signs/pallas_call | solution.py:84
  3.6 0.0 copy-done
  3.6 0.0 copy-done.1
  3.6 1.2 %panel_part.1 = (f32[64,512]{1,0:T(8,128)S(1)}, f32[64,512]{1,0:T(8,128)S(1)}, bf16[128,2048]{1,0:T(8,128)(2,1)S(1)}) custom-call(s32[7]{0:T(128)S(1)} %stack.27.words_ref, s32[1,128]{1,0:T(1,128)S(1)} %bitcast.7, bf16[256,2048]{1,0:T(8,128)(2,1)S(1)} %copy-done, bf16[2048,512]{1,0:T(8,128)(2,1)S(1)} %panel_signs.1.signs_ref), custom_call_target="tpu_custom_call" | custom-call | flops 1100000000 | bytes 1000000 | tf_op jit(solution)/shard_map/panel_part/pallas_call | solution.py:103
  4.8 0.5 %collective-permute-start = (f32[64,512]{1,0:T(8,128)S(1)}, f32[64,512]{1,0:T(8,128)S(1)}, u32[]{:S(2)}, u32[]{:S(2)}) collective-permute-start(f32[64,512]{1,0:T(8,128)S(1)} %get-tuple-element.30), channel_id=1, source_target_pairs={{0,4},{4,0},{8,12},{12,8},{1,5},{5,1},{9,13},{13,9},{2,6},{6,2},{1... | collective-permute-start | bytes 393224 | tf_op jit(solution)/shard_map/ppermute | solution.py:483
  5.3 1.0 %collective-permute-done = f32[64,512]{1,0:T(8,128)S(1)} collective-permute-done((f32[64,512]{1,0:T(8,128)S(1)}, f32[64,512]{1,0:T(8,128)S(1)}, u32[]{:S(2)}, u32[]{:S(2)}) %collective-permute-start) | collective-permute-done | bytes 131104 | tf_op jit(solution)/shard_map/ppermute | solution.py:483
  6.3 2.9 %collective-permute-start.1 = (f32[64,512]{1,0:T(8,128)S(1)}, f32[64,512]{1,0:T(8,128)S(1)}, u32[]{:S(2)}, u32[]{:S(2)}) collective-permute-start(f32[64,512]{1,0:T(8,128)S(1)} %add.15._), channel_id=1, source_target_pairs={{0,8},{4,12},{8,0},{12,4},{1,9},{5,13},{9,1},{13,5},{2,10},{6,14},... | collective-permute-start | bytes 393224 | tf_op jit(solution)/shard_map/ppermute | solution.py:483
  9.2 4.4 %blocks_part.1 = (f32[128,512]{1,0:T(8,128)S(1)}, f32[128,512]{1,0:T(8,128)S(1)}) custom-call(s32[7]{0:T(128)S(1)} %stack.27.words_ref, bf16[128,2048]{1,0:T(8,128)(2,1)S(1)} %get-tuple-element.31.chosen_ref, f32[64,512]{1,0:T(8,128)S(1)} %add.15._), custom_call_target="tpu_custom_call" | custom-call | flops 4400000000 | bytes 1000000 | tf_op jit(solution)/shard_map/blocks_part/pallas_call | solution.py:119
  13.6 0.0 collective-permute-done.1
  13.7 2.9 %other_parts.1 = (f32[64,2560]{1,0:T(8,128)S(1)}, f32[64,2560]{1,0:T(8,128)S(1)}) custom-call(s32[7]{0:T(128)S(1)} %stack.27.words_ref, bf16[128,2048]{1,0:T(8,128)(2,1)S(1)} %get-tuple-element.31.chosen_ref, f32[64,512]{1,0:T(8,128)S(1)} %get-tuple-element.57._, f32[128,512]{1,0:T(8,128)S(1)} %get-tuple-element.32.refs_0_, ...), custom_call_target="tpu_custom_call" | custom-call | flops 2200000000 | bytes 1000000 | tf_op jit(solution)/shard_map/other_parts/pallas_call | solution.py:165
  16.6 0.1 collective-permute-start.3
  16.7 1.6 %collective-permute-start.2 = (bf16[64,512]{1,0:T(8,128)(2,1)S(1)}, bf16[64,512]{1,0:T(8,128)(2,1)S(1)}, u32[]{:S(2)}, u32[]{:S(2)}) collective-permute-start(bf16[64,512]{1,0:T(8,128)(2,1)S(1)} %get-tuple-element.56.refs_0_.refs_8_), channel_id=1, source_target_pairs={{0,16},{16,0},{1,17},{17,1},{2,18},{18,2},{3,19},{19,3},{4,20},{20... | collective-permute-start | bytes 196616 | tf_op jit(solution)/shard_map/ppermute | solution.py:483
  18.2 0.2 collective-permute-start.4
  18.4 0.4 collective-permute-done.3.right_ref
  18.8 0.6 %halve.1 = (f32[64,1536]{1,0:T(8,128)S(1)}, f32[64,1536]{1,0:T(8,128)S(1)}) custom-call(s32[7]{0:T(128)S(1)} %stack.27.words_ref, f32[64,2560]{1,0:T(8,128)S(1)} %get-tuple-element.34.left_ref, f32[64,2560]{1,0:T(8,128)S(1)} %collective-permute-done.3.right_ref), custom_call_target="tpu_custom_call" | custom-call | flops 550000000 | bytes 1000000 | tf_op jit(solution)/shard_map/halve/pallas_call | solution.py:188
  19.4 1.8 %collective-permute-done.2.refs_1_.refs_9_ = bf16[64,512]{1,0:T(8,128)(2,1)S(1)} collective-permute-done((bf16[64,512]{1,0:T(8,128)(2,1)S(1)}, bf16[64,512]{1,0:T(8,128)(2,1)S(1)}, u32[]{:S(2)}, u32[]{:S(2)}) %collective-permute-start.2) | collective-permute-done | bytes 65568 | tf_op jit(solution)/shard_map/ppermute | solution.py:483
  21.2 0.0 collective-permute-start.5
  21.2 1.1 %collective-permute-start.6 = (f32[64,1536]{1,0:T(8,128)S(1)}, f32[64,1536]{1,0:T(8,128)S(1)}, u32[]{:S(2)}, u32[]{:S(2)}) collective-permute-start(f32[64,1536]{1,0:T(8,128)S(1)} %get-tuple-element.53), channel_id=1, source_target_pairs={{0,8},{4,12},{8,0},{12,4},{1,9},{5,13},{9,1},{13,5},{2,10},{6,14},... | collective-permute-start | bytes 1179656 | tf_op jit(solution)/shard_map/ppermute | solution.py:483
  23.0 0.0 collective-permute-done.4.refs_2_.refs_10_
  23.0 0.0 collective-permute-done.5.refs_3_.refs_11_
  23.0 4.4 %gram_first_block.1 = (f32[128,512]{1,0:T(8,128)S(1)}, f32[128,256]{1,0:T(8,128)S(1)}, f32[384,384]{1,0:T(8,128)S(1)}, f32[384,256]{1,0:T(8,128)S(1)}) custom-call(s32[7]{0:T(128)S(1)} %stack.27.words_ref, f32[1]{0:T(128)S(6)} %copy.7.ridge_ref, bf16[64,512]{1,0:T(8,128)(2,1)S(1)} %get-tuple-element.56.refs_0_.refs_8_, ...), custom_call_target="tpu_custom_call" | custom-call | flops 3849999872 | bytes 1000000 | tf_op jit(solution)/shard_map/gram_first_block/pallas_call | solution.py:393
  27.4 3.3 %eliminate_block.3 = (f32[128,384]{1,0:T(8,128)S(1)}, f32[128,256]{1,0:T(8,128)S(1)}, f32[256,256]{1,0:T(8,128)S(1)}, f32[256,256]{1,0:T(8,128)S(1)}) custom-call(f32[384,384]{1,0:T(8,128)S(1)} %get-tuple-element.39.gram_in, f32[384,256]{1,0:T(8,128)S(1)} %get-tuple-element.40.lifted_in), custom_call_target="tpu_custom_call" | custom-call | flops 330000000 | bytes 1000000 | tf_op jit(solution)/shard_map/eliminate_block/pallas_call | solution.py:404
  30.8 2.0 %collective-permute-done.6.right_ref = f32[64,1536]{1,0:T(8,128)S(1)} collective-permute-done((f32[64,1536]{1,0:T(8,128)S(1)}, f32[64,1536]{1,0:T(8,128)S(1)}, u32[]{:S(2)}, u32[]{:S(2)}) %collective-permute-start.6) | collective-permute-done | bytes 393248 | tf_op jit(solution)/shard_map/ppermute | solution.py:483
  32.7 0.6 %pieces.1 = (bf16[64,1280]{1,0:T(8,128)(2,1)S(1)}, bf16[64,1280]{1,0:T(8,128)(2,1)S(1)}) custom-call(s32[7]{0:T(128)S(1)} %stack.27.words_ref, f32[64,1536]{1,0:T(8,128)S(1)} %get-tuple-element.52.left_ref, f32[64,1536]{1,0:T(8,128)S(1)} %collective-permute-done.6.right_ref, f32[128,256]{1,0:T(8,128)S(1)} %get-tuple-element.49._.refs_5_), custom_call_target="tpu_custom_call" | custom-call | flops 550000000 | bytes 1000000 | tf_op jit(solution)/shard_map/pieces/pallas_call | solution.py:211
  33.3 1.6 %collective-permute-start.7 = (bf16[64,1280]{1,0:T(8,128)(2,1)S(1)}, bf16[64,1280]{1,0:T(8,128)(2,1)S(1)}, u32[]{:S(2)}, u32[]{:S(2)}) collective-permute-start(bf16[64,1280]{1,0:T(8,128)(2,1)S(1)} %get-tuple-element.55), channel_id=1, source_target_pairs={{0,16},{16,0},{1,17},{17,1},{2,18},{18,2},{3,19},{19,3},{4,20},{20... | collective-permute-start | bytes 491528 | tf_op jit(solution)/shard_map/ppermute | solution.py:483
  34.9 3.2 %eliminate_block.4 = (f32[128,256]{1,0:T(8,128)S(1)}, f32[128,256]{1,0:T(8,128)S(1)}, f32[128,128]{1,0:T(8,128)S(1)}, f32[128,256]{1,0:T(8,128)S(1)}) custom-call(f32[256,256]{1,0:T(8,128)S(1)} %get-tuple-element.42.gram_in, f32[256,256]{1,0:T(8,128)S(1)} %get-tuple-element.43.lifted_in), custom_call_target="tpu_custom_call" | custom-call | flops 4400000000 | bytes 1000000 | tf_op jit(solution)/shard_map/eliminate_block/pallas_call | solution.py:404
  38.1 0.1 collective-permute-start.8
  38.2 1.0 %collective-permute-done.7.refs_13_ = bf16[64,1280]{1,0:T(8,128)(2,1)S(1)} collective-permute-done((bf16[64,1280]{1,0:T(8,128)(2,1)S(1)}, bf16[64,1280]{1,0:T(8,128)(2,1)S(1)}, u32[]{:S(2)}, u32[]{:S(2)}) %collective-permute-start.7) | collective-permute-done | bytes 163872 | tf_op jit(solution)/shard_map/ppermute | solution.py:483
  39.2 0.0 collective-permute-start.9
  39.2 3.0 %eliminate_block.5 = (f32[128,128]{1,0:T(8,128)S(1)}, f32[128,256]{1,0:T(8,128)S(1)}) custom-call(f32[128,128]{1,0:T(8,128)S(1)} %get-tuple-element.45.gram_in, f32[128,256]{1,0:T(8,128)S(1)} %get-tuple-element.46.lifted_in), custom_call_target="tpu_custom_call" | custom-call | flops 4400000000 | bytes 1000000 | tf_op jit(solution)/shard_map/eliminate_block/pallas_call | solution.py:404
  42.2 0.0 collective-permute-done.8.refs_14_
  42.2 0.0 collective-permute-done.9.refs_15_
  42.2 3.4 %finish.1 = (f32[256,512]{1,0:T(8,128)}, f32[256,512]{1,0:T(8,128)}) custom-call(s32[7]{0:T(128)S(1)} %stack.27.words_ref, f32[1]{0:T(128)S(6)} %copy.7.ridge_ref, f32[128,512]{1,0:T(8,128)S(1)} %get-tuple-element.38.refs_0_, f32[128,384]{1,0:T(8,128)S(1)} %get-tuple-element.41.refs_1_, f32[128,256]{1,0:T(8,128)S(1)} %get-tuple-element.44.refs_2_, ...), custom_call_target="tpu_custom_call" | custom-call | flops 3300000000 | bytes 1000000 | tf_op jit(solution)/shard_map/finish/pallas_call | solution.py:471
  (2 shorter events, 0.0 us)
Async XLA Ops:
  1.4 2.2 %copy-start = (bf16[256,2048]{1,0:T(8,128)(2,1)S(1)}, bf16[256,2048]{1,0:T(8,128)(2,1)}, u32[]{:S(2)}) copy-start(bf16[256,2048]{1,0:T(8,128)(2,1)} %pool_ref.1) | copy-start | bytes 3145732
  1.4 2.2 %copy-start.1 = (s32[128]{0:T(128)S(1)}, s32[128]{0:T(128)}, u32[]{:S(2)}) copy-start(s32[128]{0:T(128)} %param.5) | copy-start | bytes 1540
  4.8 1.5 %collective-permute-start = (f32[64,512]{1,0:T(8,128)S(1)}, f32[64,512]{1,0:T(8,128)S(1)}, u32[]{:S(2)}, u32[]{:S(2)}) collective-permute-start(f32[64,512]{1,0:T(8,128)S(1)} %get-tuple-element.30), channel_id=1, source_target_pairs={{0,4},{4,0},{8,12},{12,8},{1,5},{5,1},{9,13},{13,9},{2,6},{6,2},{1... | collective-permute-start | bytes 393224 | tf_op jit(solution)/shard_map/ppermute | solution.py:483
  6.3 7.4 %collective-permute-start.1 = (f32[64,512]{1,0:T(8,128)S(1)}, f32[64,512]{1,0:T(8,128)S(1)}, u32[]{:S(2)}, u32[]{:S(2)}) collective-permute-start(f32[64,512]{1,0:T(8,128)S(1)} %add.15._), channel_id=1, source_target_pairs={{0,8},{4,12},{8,0},{12,4},{1,9},{5,13},{9,1},{13,5},{2,10},{6,14},... | collective-permute-start | bytes 393224 | tf_op jit(solution)/shard_map/ppermute | solution.py:483
  16.6 2.2 %collective-permute-start.3 = (f32[64,2560]{1,0:T(8,128)S(1)}, f32[64,2560]{1,0:T(8,128)S(1)}, u32[]{:S(2)}, u32[]{:S(2)}) collective-permute-start(f32[64,2560]{1,0:T(8,128)S(1)} %get-tuple-element.35), channel_id=1, source_target_pairs={{0,4},{4,0},{8,12},{12,8},{1,5},{5,1},{9,13},{13,9},{2,6},{6,2},{1... | collective-permute-start | bytes 1966088 | tf_op jit(solution)/shard_map/ppermute | solution.py:483
  16.7 4.5 %collective-permute-start.2 = (bf16[64,512]{1,0:T(8,128)(2,1)S(1)}, bf16[64,512]{1,0:T(8,128)(2,1)S(1)}, u32[]{:S(2)}, u32[]{:S(2)}) collective-permute-start(bf16[64,512]{1,0:T(8,128)(2,1)S(1)} %get-tuple-element.56.refs_0_.refs_8_), channel_id=1, source_target_pairs={{0,16},{16,0},{1,17},{17,1},{2,18},{18,2},{3,19},{19,3},{4,20},{20... | collective-permute-start | bytes 196616 | tf_op jit(solution)/shard_map/ppermute | solution.py:483
  18.2 4.7 %collective-permute-start.4 = (bf16[64,512]{1,0:T(8,128)(2,1)S(1)}, bf16[64,512]{1,0:T(8,128)(2,1)S(1)}, u32[]{:S(2)}, u32[]{:S(2)}) collective-permute-start(bf16[64,512]{1,0:T(8,128)(2,1)S(1)} %get-tuple-element.56.refs_0_.refs_8_), channel_id=1, source_target_pairs={{0,4},{4,0},{8,12},{12,8},{1,5},{5,1},{9,13},{13,9},{2,6},{6,2},{1... | collective-permute-start | bytes 196616 | tf_op jit(solution)/shard_map/ppermute | solution.py:483
  21.2 1.8 %collective-permute-start.5 = (bf16[64,512]{1,0:T(8,128)(2,1)S(1)}, bf16[64,512]{1,0:T(8,128)(2,1)S(1)}, u32[]{:S(2)}, u32[]{:S(2)}) collective-permute-start(bf16[64,512]{1,0:T(8,128)(2,1)S(1)} %collective-permute-done.2.refs_1_.refs_9_), channel_id=1, source_target_pairs={{0,4},{4,0},{8,12},{12,8},{1,5},{5,1},{9,13},{13,9},{2,6},{6,2},{1... | collective-permute-start | bytes 196616 | tf_op jit(solution)/shard_map/ppermute | solution.py:483
  21.2 11.5 %collective-permute-start.6 = (f32[64,1536]{1,0:T(8,128)S(1)}, f32[64,1536]{1,0:T(8,128)S(1)}, u32[]{:S(2)}, u32[]{:S(2)}) collective-permute-start(f32[64,1536]{1,0:T(8,128)S(1)} %get-tuple-element.53), channel_id=1, source_target_pairs={{0,8},{4,12},{8,0},{12,4},{1,9},{5,13},{9,1},{13,5},{2,10},{6,14},... | collective-permute-start | bytes 1179656 | tf_op jit(solution)/shard_map/ppermute | solution.py:483
  33.3 5.9 %collective-permute-start.7 = (bf16[64,1280]{1,0:T(8,128)(2,1)S(1)}, bf16[64,1280]{1,0:T(8,128)(2,1)S(1)}, u32[]{:S(2)}, u32[]{:S(2)}) collective-permute-start(bf16[64,1280]{1,0:T(8,128)(2,1)S(1)} %get-tuple-element.55), channel_id=1, source_target_pairs={{0,16},{16,0},{1,17},{17,1},{2,18},{18,2},{3,19},{19,3},{4,20},{20... | collective-permute-start | bytes 491528 | tf_op jit(solution)/shard_map/ppermute | solution.py:483
  38.1 4.1 %collective-permute-start.8 = (bf16[64,1280]{1,0:T(8,128)(2,1)S(1)}, bf16[64,1280]{1,0:T(8,128)(2,1)S(1)}, u32[]{:S(2)}, u32[]{:S(2)}) collective-permute-start(bf16[64,1280]{1,0:T(8,128)(2,1)S(1)} %get-tuple-element.54.refs_12_), channel_id=1, source_target_pairs={{0,4},{4,0},{8,12},{12,8},{1,5},{5,1},{9,13},{13,9},{2,6},{6,2},{1... | collective-permute-start | bytes 491528 | tf_op jit(solution)/shard_map/ppermute | solution.py:483
  39.2 3.0 %collective-permute-start.9 = (bf16[64,1280]{1,0:T(8,128)(2,1)S(1)}, bf16[64,1280]{1,0:T(8,128)(2,1)S(1)}, u32[]{:S(2)}, u32[]{:S(2)}) collective-permute-start(bf16[64,1280]{1,0:T(8,128)(2,1)S(1)} %collective-permute-done.7.refs_13_), channel_id=1, source_target_pairs={{0,4},{4,0},{8,12},{12,8},{1,5},{5,1},{9,13},{13,9},{2,6},{6,2},{1... | collective-permute-start | bytes 491528 | tf_op jit(solution)/shard_map/ppermute | solution.py:483

commit v4 on v3

--- a/solution.py
+++ b/solution.py
@@ -3,7 +3,6 @@
 
 import jax
 import jax.numpy as jnp
-import numpy as np
 from jax import lax
 from jax.experimental import pallas as pl
 from jax.experimental.pallas import tpu as pltpu
@@ -16,8 +15,6 @@
 BLOCK = 128
 DEPTH = 256
 SEGMENT = 128
-SECOND_BY_8 = int(np.array(-1028477387 << 8 & 0xFFFFFFFF, np.uint32).astype(np.int32))
-SECOND_BY_24 = int(np.array(-1028477387 << 24 & 0xFFFFFFFF, np.uint32).astype(np.int32))
 VMEM = pl.BlockSpec(memory_space=pltpu.VMEM)
 SMEM = pl.BlockSpec(memory_space=pltpu.SMEM)
 ANYWHERE = pl.BlockSpec(memory_space=pl.ANY)
@@ -52,9 +49,9 @@
     columns = (lax.broadcasted_iota(jnp.int32, (1, shape[1]), 1) + feature) * jnp.int32(668265263) + seed_word
     hashed = rows + columns
     hashed = (hashed ^ shifted(hashed, 16)) * jnp.int32(-2048144789)
-    hashed = hashed ^ shifted(hashed, 13)
-    decided = (hashed * jnp.int32(SECOND_BY_8)) ^ (hashed * jnp.int32(SECOND_BY_24))
-    return jnp.where(decided < 0, -1.0, 1.0).astype(jnp.bfloat16)
+    hashed = (hashed ^ shifted(hashed, 13)) * jnp.int32(-1028477387)
+    decided = (hashed ^ shifted(hashed, 16)).astype(jnp.int16) & jnp.int16(128)
+    return jnp.where(decided == 0, jnp.bfloat16(1.0), jnp.bfloat16(-1.0))
 
 
 def segment_signs(words_ref, feature, width, index):
@@ -172,21 +169,37 @@
     )(words, chosen, after, *first)
 
 
-def halve_kernel(row_lanes, bit, words_ref, left_ref, right_ref, keep_ref, send_ref):
+def group_at(rows, index, count):
+    found = rows[:, :HALF]
+    for place in range(1, count):
+        found = jnp.where(index == place, rows[:, place * HALF : (place + 1) * HALF], found)
+    return found
+
+
+def halve_kernel(ex_count, bit, words_ref, left_ref, right_ref, keep_ref, send_ref):
+    row_lanes = ex_count * HALF
     upper = words_ref[4] & bit != 0
     rows = left_ref[:, :row_lanes] + right_ref[:, :row_lanes]
     columns = left_ref[:, row_lanes:] + right_ref[:, row_lanes:]
     middle = columns.shape[1] // 2
-    keep_ref[:, :row_lanes] = rows
-    send_ref[:, :row_lanes] = rows
-    keep_ref[:, row_lanes:] = jnp.where(upper, columns[:, middle:], columns[:, :middle])
-    send_ref[:, row_lanes:] = jnp.where(upper, columns[:, :middle], columns[:, middle:])
-
-
-def halve(words, left, right, row_lanes, bit):
-    shape = (left.shape[0], (left.shape[1] + row_lanes) // 2)
-    return call(
-        functools.partial(halve_kernel, row_lanes, bit),
+    lanes = keep_ref.shape[1] - middle
+    if bit > 2:
+        keep_ref[:, :lanes] = rows
+        send_ref[:, :lanes] = rows
+    else:
+        for step in range(1, ex_count):
+            place = slice((step - 1) * HALF, step * HALF)
+            keep_ref[:, place] = group_at(rows, words_ref[4] // 2 ^ step, ex_count)
+            send_ref[:, place] = group_at(rows, words_ref[4] // 2 ^ 1 ^ step, ex_count)
+    keep_ref[:, lanes:] = jnp.where(upper, columns[:, middle:], columns[:, :middle])
+    send_ref[:, lanes:] = jnp.where(upper, columns[:, :middle], columns[:, middle:])
+
+
+def halve(words, left, right, ex_count, bit):
+    lanes = (ex_count if bit > 2 else ex_count - 1) * HALF
+    shape = (left.shape[0], (left.shape[1] - ex_count * HALF) // 2 + lanes)
+    return call(
+        functools.partial(halve_kernel, ex_count, bit),
         [(shape, jnp.float32)] * 2,
         [SMEM, VMEM, VMEM],
         0.5,
@@ -195,19 +208,14 @@
 
 
 def pieces_kernel(ex_count, scaling, words_ref, left_ref, right_ref, _, *piece_refs):
-    row_lanes = ex_count * HALF
     total = ((left_ref[...] + right_ref[...]) * scaling).astype(jnp.bfloat16)
     for step, ref in enumerate(piece_refs):
-        target = words_ref[5] ^ step
-        rows = total[:, :HALF]
-        for index in range(1, ex_count):
-            rows = jnp.where(target == index, total[:, index * HALF : (index + 1) * HALF], rows)
-        ref[:, :HALF] = rows
-        ref[:, HALF:] = total[:, row_lanes:]
+        ref[:, :HALF] = group_at(total, (words_ref[5] ^ step ^ (words_ref[4] // 2)) - 1, ex_count - 1)
+        ref[:, HALF:] = total[:, (ex_count - 1) * HALF :]
 
 
 def pieces(words, left, right, ex_count, scaling, after):
-    shape = (left.shape[0], left.shape[1] - (ex_count - 1) * HALF)
+    shape = (left.shape[0], left.shape[1] - (ex_count - 2) * HALF)
     return call(
         functools.partial(pieces_kernel, ex_count, scaling),
         [(shape, jnp.bfloat16)] * ex_count,
@@ -275,37 +283,21 @@
     return high, middle, (rest - middle.astype(jnp.float32)).astype(jnp.bfloat16)
 
 
-def exact_dot(left, right, transposed=False):
-    axis = 0 if transposed else 1
+def exact_dot(left, right, axes=(1, 0)):
     left_parts, right_parts = thirds(left), thirds(right)
     terms = ((0, 0), (0, 1), (1, 0), (0, 2), (2, 0), (1, 1))
-    count = max(1, min(len(terms), DEPTH // left.shape[axis]))
+    count = max(1, min(len(terms), DEPTH // left.shape[axes[0]]))
     total = None
     for start in range(0, len(terms), count):
         some = terms[start : start + count]
         term = lax.dot_general(
-            join([left_parts[i] for i, _ in some], axis),
-            join([right_parts[j] for _, j in some], 0),
-            (((axis,), (0,)), ((), ())),
+            join([left_parts[i] for i, _ in some], axes[0]),
+            join([right_parts[j] for _, j in some], axes[1]),
+            (((axes[0],), (axes[1],)), ((), ())),
             preferred_element_type=jnp.float32,
         )
         total = term if total is None else total + term
     return total
-
-
-def sum_kernel(scaling, left_ref, right_ref, _, sum_ref):
-    sum_ref[...] = ((left_ref[...] + right_ref[...]) * scaling).astype(jnp.bfloat16)
-
-
-def scaled_sum(left, right, scaling, after):
-    return pl.pallas_call(
-        functools.partial(sum_kernel, scaling),
-        out_shape=jax.ShapeDtypeStruct(left.shape, jnp.bfloat16),
-        in_specs=[VMEM, VMEM, ANYWHERE],
-        out_specs=VMEM,
-        cost_estimate=pl.CostEstimate(flops=1_000_000, bytes_accessed=1_000_000, transcendentals=0),
-        name="scaled_sum",
-    )(left, right, after)
 
 
 def identity_mask(shape):
@@ -323,7 +315,7 @@
         done += inverse
         if end < BLOCK:
             upper, inverse = jnp.concatenate(upper, axis=0), jnp.concatenate(inverse, axis=0)
-            update = exact_dot(upper, jnp.concatenate([upper, inverse], axis=1), True)[end:]
+            update = exact_dot(upper, jnp.concatenate([upper, inverse], axis=1), (0, 0))[end:]
             rows_u = [row - update[8 * v : 8 * v + 8, :BLOCK] for v, row in enumerate(rows_u[groups:])]
             rows_z = [row - update[8 * v : 8 * v + 8, BLOCK:] for v, row in enumerate(rows_z[groups:])]
     return jnp.concatenate(done, axis=0)
@@ -336,74 +328,78 @@
     return join([jnp.where(even, mine, other), jnp.where(even, other, mine)], 0)
 
 
-def eliminate(gram, lifted, upper_ref, done_ref, gram_ref, lifted_ref):
-    inverse = factor_block(gram(slice(0, BLOCK), slice(0, BLOCK)))
+def eliminate(gram, turned, upper_refs, done_refs, rest_refs):
     square = (BLOCK, BLOCK)
     keep = lax.broadcasted_iota(jnp.int32, square, 0) <= lax.broadcasted_iota(jnp.int32, square, 1)
-    upper = exact_dot(inverse, gram(slice(0, BLOCK), slice(None)))
-    upper_ref[:, :BLOCK] = jnp.where(keep, upper[:, :BLOCK], 0.0)
-    done = exact_dot(inverse, lifted(slice(0, BLOCK)))
-    done_ref[...] = done
-    if gram_ref is not None:
-        rest = upper[:, BLOCK:]
-        upper_ref[:, BLOCK:] = rest
-        gram_ref[...] = gram(slice(BLOCK, None), slice(BLOCK, None)) - exact_dot(rest, rest, True)
-        lifted_ref[...] = lifted(slice(BLOCK, None)) - exact_dot(rest, done, True)
-
-
-def first_block_kernel(words_ref, ridge_ref, *refs):
-    *phi_refs, upper_ref, done_ref, gram_ref, lifted_ref, whole_ref, turned_ref = refs
+    block = gram[:BLOCK, :BLOCK]
+    for index, (upper_ref, done_ref) in enumerate(zip(upper_refs, done_refs)):
+        inverse = factor_block(block)
+        if index + 1 < len(upper_refs):
+            beside = exact_dot(inverse, gram[:BLOCK, BLOCK : 2 * BLOCK])
+            ahead = gram[BLOCK : 2 * BLOCK, BLOCK : 2 * BLOCK] - exact_dot(beside, beside, (0, 0))
+        upper_ref[:, :BLOCK] = jnp.where(keep, exact_dot(inverse, block), 0.0)
+        done = exact_dot(turned[:, :BLOCK], inverse, (1, 1))
+        done_ref[...] = done
+        if gram.shape[0] > BLOCK:
+            rest = exact_dot(inverse, gram[:BLOCK, BLOCK:])
+            upper_ref[:, BLOCK:] = rest
+            gram = gram[BLOCK:, BLOCK:] - exact_dot(rest, rest, (0, 0))
+            turned = turned[:, BLOCK:] - exact_dot(done, rest)
+        if index + 1 < len(upper_refs):
+            block = ahead
+    if rest_refs:
+        rest_refs[0][...] = gram
+        rest_refs[1][...] = turned
+
+
+def first_blocks_kernel(blocks, count, words_ref, ridge_ref, *refs):
+    phi_refs, out_refs = refs[:count], refs[count:]
     phi = in_pair_order(words_ref[2] == 0, phi_refs)
     examples, width = phi.shape
-    whole_ref[...] = tdot(phi, phi) * (1.0 / examples) + jnp.where(
-        identity_mask((width, width)), ridge_ref[0], 0.0
+    gram = tdot(phi, phi) * (1.0 / examples) + jnp.where(identity_mask((width, width)), ridge_ref[0], 0.0)
+    eliminate(
+        gram, phi.astype(jnp.float32), out_refs[:blocks], out_refs[blocks : 2 * blocks], out_refs[2 * blocks :]
     )
-    turned_ref[...] = phi.astype(jnp.float32).T
-    eliminate(
-        lambda rows, lanes: whole_ref[rows, lanes],
-        lambda rows: turned_ref[rows, :],
-        upper_ref,
-        done_ref,
-        gram_ref,
-        lifted_ref,
-    )
-
-
-def block_kernel(gram_in, lifted_in, upper_ref, done_ref, gram_ref=None, lifted_ref=None):
-    eliminate(
-        lambda rows, lanes: gram_in[rows, lanes],
-        lambda rows: lifted_in[rows, :],
-        upper_ref,
-        done_ref,
-        gram_ref,
-        lifted_ref,
-    )
-
-
-def block_shapes(width, examples):
-    rest = width - BLOCK
-    shapes = [(BLOCK, width), (BLOCK, examples)]
+
+
+def next_blocks_kernel(blocks, gram_ref, turned_ref, *refs):
+    eliminate(gram_ref[...], turned_ref[...], refs[:blocks], refs[blocks : 2 * blocks], refs[2 * blocks :])
+
+
+def block_shapes(width, examples, blocks):
+    rest = width - blocks * BLOCK
+    shapes = [(BLOCK, width - index * BLOCK) for index in range(blocks)] + [(examples, BLOCK)] * blocks
     if rest:
-        shapes += [(rest, rest), (rest, examples)]
+        shapes += [(rest, rest), (examples, rest)]
     return [(shape, jnp.float32) for shape in shapes]
 
 
-def first_block(words, ridge_value, phi):
+def taken_apart(results, blocks):
+    return list(results[:blocks]), list(results[blocks : 2 * blocks]), results[2 * blocks :]
+
+
+def first_blocks(words, ridge_value, phi, blocks):
     examples, width = sum(part.shape[0] for part in phi), phi[0].shape[1]
-    return call(
-        first_block_kernel,
-        block_shapes(width, examples),
+    results = call(
+        functools.partial(first_blocks_kernel, blocks, len(phi)),
+        block_shapes(width, examples, blocks),
         [SMEM, SMEM] + [VMEM] * len(phi),
         3.5,
-        "gram_first_block",
-        [pltpu.VMEM((width, width), jnp.float32), pltpu.VMEM((width, examples), jnp.float32)],
+        "gram_first_blocks",
     )(words, ridge_value, *phi)
-
-
-def next_block(gram, lifted, microseconds):
-    return call(
-        block_kernel, block_shapes(gram.shape[0], lifted.shape[1]), [VMEM, VMEM], microseconds, "eliminate_block"
-    )(gram, lifted)
+    return taken_apart(results, blocks)
+
+
+def next_blocks(rest, blocks):
+    gram, turned = rest
+    results = call(
+        functools.partial(next_blocks_kernel, blocks),
+        block_shapes(gram.shape[0], turned.shape[0], blocks),
+        [VMEM, VMEM],
+        4 * blocks,
+        "eliminate_blocks",
+    )(gram, turned)
+    return taken_apart(results, blocks)
 
 
 def finish_kernel(blocks, count, words_ref, ridge_ref, *refs):
@@ -416,53 +412,49 @@
     row_group, column_block = words_ref[6], words_ref[4]
     phi = in_pair_order(even, phi_refs)
     examples = phi.shape[0]
+    mine, others = piece_refs[: count // 2], piece_refs[count // 2 :]
+    columns, pair_columns = (
+        join([ref[:, start : start + width] for start in (height, height + width) for ref in some], 0)
+        for some in (mine, others)
+    )
     rows = in_pair_order(even, piece_refs, slice(0, height))
+    groups = width // height
+    holder = words_ref[3] // groups
+    held = jnp.where(holder == words_ref[2], columns, pair_columns)
+    for place in range(groups):
+        inside = (words_ref[5] == column_block // 2) & (words_ref[3] % groups == place)
+        rows = jnp.where(inside, held[:, place * height : (place + 1) * height], rows)
     for start in range(0, panel, height):
         rows = jnp.where(row_group * height == start, phi[:, start : start + height], rows)
-    mine = piece_refs[: count // 2]
-    columns = join(
-        [ref[:, start : start + width] for start in (height, height + width) for ref in mine], 0
-    )
     columns = jnp.where(column_block == 0, phi, columns)
-    parts = thirds(join([ref[...] for ref in dones], 0))
-    parts = join(list(parts), 1)
+    turned = jnp.concatenate([rows, columns], axis=1).T
+    parts = join(list(thirds(join([ref[...] for ref in dones], 1))), 0)
     scale = 1.0 / examples
-    solved_ref[...] = jnp.dot(parts, join([columns] * 3, 0), preferred_element_type=jnp.float32) * scale
-    panel_ref[...] = (
-        lax.dot_general(
-            join([rows] * 3, 0), parts, (((0,), (1,)), ((), ())), preferred_element_type=jnp.float32
-        )
-        * scale
-    )
-
-    @pl.when(column_block == 0)
-    def _():
-        for index, ref in enumerate(uppers):
-            low = index * BLOCK
-            if low:
-                solved_ref[low : low + BLOCK, :low] = jnp.zeros((BLOCK, low), jnp.float32)
-            solved_ref[low : low + BLOCK, low:] = ref[...]
-
+    solved = jnp.dot(join([turned] * 3, 1), parts, preferred_element_type=jnp.float32) * scale
+    panel_ref[...] = solved[:height]
+    solved_ref[...] = solved[height:]
+
+    def lower(row, lane):
+        if row < lane:
+            return jnp.zeros((BLOCK, BLOCK), jnp.float32)
+        return uppers[lane // BLOCK][:, row - lane : row - lane + BLOCK].T
+
+    def put(ref, first):
+        for row in range(0, ref.shape[0], BLOCK):
+            for lane in range(0, panel, BLOCK):
+                ref[row : row + BLOCK, lane : lane + BLOCK] = lower(first + row, lane)
+
+    pl.when(column_block == 0)(functools.partial(put, solved_ref, 0))
     for group in range(panel // height):
-
-        @pl.when(row_group == group)
-        def _(left=group * height, right=(group + 1) * height):
-            for index, ref in enumerate(uppers):
-                low = index * BLOCK
-                lanes = slice(low, low + BLOCK)
-                for start in range(left, right, BLOCK):
-                    if start < low:
-                        value = jnp.zeros((BLOCK, BLOCK), jnp.float32)
-                    else:
-                        value = ref[:, start - low : start - low + BLOCK].T
-                    panel_ref[start - left : start - left + BLOCK, lanes] = value
-
+        pl.when(row_group == group)(functools.partial(put, panel_ref, group * height))
     shape = (height, width)
     diagonal = row_group * height + lax.broadcasted_iota(
         jnp.int32, shape, 0
     ) == column_block * width + lax.broadcasted_iota(jnp.int32, shape, 1)
-    gram = tdot(rows, columns) * scale + jnp.where(diagonal, ridge_ref[0], 0.0)
-    trailing_ref[...] = gram - exact_dot(panel_ref[...], solved_ref[...])
+    gram = jnp.dot(turned[:height], columns, preferred_element_type=jnp.float32) * scale
+    trailing_ref[...] = (
+        gram + jnp.where(diagonal, ridge_ref[0], 0.0) - exact_dot(panel_ref[...], solved_ref[...], (1, 1))
+    )
 
 
 def finish(words, ridge_value, uppers, dones, phi, gathered, height, width):
@@ -474,7 +466,7 @@
         [SMEM, SMEM] + [VMEM] * len(operands),
         3,
         "finish",
-        [pltpu.VMEM((panel, width), jnp.float32)],
+        [pltpu.VMEM((width, panel), jnp.float32)],
         vmem=24,
     )(words, ridge_value, *operands)
 
@@ -498,7 +490,6 @@
     ex_index, tp_index, blk_index = (lax.axis_index(axis) for axis in ("ex", "tp", "blk"))
     coord_dev = gradients.shape[1]
     column_width = HALF * ex_count * blk_count // tp_count
-    row_lanes = ex_count * HALF
     scaling = 1.0 / math.sqrt(coord_dev * tp_count)
     words = jnp.stack(
         [
@@ -523,25 +514,22 @@
 
     first = blocks_part(words, chosen, range(1, 1 + tp_count // 2), column_width, halves)
     left, right = other_parts(words, chosen, first, tp_count, blk_count, total)
+    phi[1:], right = lax.optimization_barrier((phi[1:], right))
     right = swapped(right, "tp", 1)
     bit = tp_count // 2
     while bit > 1:
-        left, right = halve(words, left, right, row_lanes, bit)
+        left, right = halve(words, left, right, ex_count, bit)
         right = swapped(right, "tp", bit)
         bit //= 2
 
-    phi[1:], left = lax.optimization_barrier((phi[1:], left))
     phi = with_pair(phi)
-    uppers, dones = [], []
-    upper, done, *rest = first_block(words, ridge_value, phi)
-    while True:
-        uppers.append(upper)
-        dones.append(done)
-        if not rest:
-            break
-        upper, done, *rest = next_block(*rest, 0.3 if len(dones) < 2 else 4)
-    gathered = pieces(words, left, right, ex_count, scaling, dones[len(dones) // 2 - 1])
+    half = PANEL // BLOCK // 2
+    uppers, dones, rest = first_blocks(words, ridge_value, phi, half)
+    gathered = pieces(words, left, right, ex_count, scaling, dones[-1])
     gathered = with_pair(ex_parts(gathered))
+    while rest:
+        more_uppers, more_dones, rest = next_blocks(rest, 1)
+        uppers, dones = uppers + more_uppers, dones + more_dones
     return tuple(finish(words, ridge_value, uppers, dones, phi, gathered, HALF, column_width))
 
 

time: 45.8 us -> 43.3 us (0.945)
  waiting for transfers between devices: 6.13 us -> 3.29 us
  starting transfers between devices: 7.99 us -> 8.66 us
    ppermute x10, waiting for transfers between devices: 6.13 us -> 3.29 us  [swapped(): lax.ppermute(value, axis, [(s, s ^ bit) for s in range(lax.axis_size(axis...]
    ppermute x10, starting transfers between devices: 7.99 us -> 8.66 us  [swapped(): lax.ppermute(value, axis, [(s, s ^ bit) for s in range(lax.axis_size(axis...]
    pallas_call x5 -> x4, Pallas kernels: 14.6 us -> 14.5 us  [the longest x1 7.51 us: first_blocks(): call(functools.partial(first_blocks_kernel, blocks, len(phi)), block_shap...]
  transfers between devices with their start and end apart: 10 -> 10, of which waited for: 5 -> 4; matrix products, arithmetic and copies ran while one was open for 0% -> 0% of each run, Pallas kernels for 42% -> 50%
where the time goes in v4:
time: 43.3 us; the launch traced here: 43.2 us
  Pallas kernels  29 us (67%)
  starting transfers between devices  8.66 us (20%)
  waiting for transfers between devices  3.29 us (8%)
  between operations  2.08 us (5%)
    ppermute x10, starting transfers between devices, swapped(): lax.ppermute(value, axis, [(s, s ^ bit) for s in range(lax.axis_size(axis...  8.66 us
    pallas_call x1, Pallas kernels, first_blocks(): call(functools.partial(first_blocks_kernel, blocks, len(phi)), block_shap...  7.51 us
    pallas_call x2, Pallas kernels, next_blocks(): call(functools.partial(next_blocks_kernel, blocks), block_shapes(gram.sha...  6.32 us
    pallas_call x1, Pallas kernels, blocks_part(): call(functools.partial(blocks_part_kernel, blocks), [((chosen.shape[0], w...  4.11 us
    pallas_call x1, Pallas kernels, finish(): call(functools.partial(finish_kernel, len(uppers), len(phi)), [((height,...  3.67 us
    ppermute x10, waiting for transfers between devices, swapped(): lax.ppermute(value, axis, [(s, s ^ bit) for s in range(lax.axis_size(axis...  3.29 us
    pallas_call x1, Pallas kernels, other_parts(): call(functools.partial(other_parts_kernel, tp_count, blk_count), [((rows...  2.8 us
    pallas_call x1, Pallas kernels, panel_signs(): call(panel_signs_kernel, [((coordinates, PANEL), jnp.bfloat16)], [SMEM],...  2.2 us
  transfers between devices with their start and end apart: 10, of which 4 were waited for; matrix products, arithmetic and copies ran while one was open for 0% of the time, Pallas kernels for 50%

profile of v4, /device:TPU:0, one launch (start us, length us, event | category | flops | bytes accessed | tf_op | source)
XLA Modules:
  0.0 43.2 jit_solution(15603386541693599628)
XLA Ops:
  1.3 0.1 stack.27.words_ref
  1.4 0.0 copy-start
  1.4 0.0 copy-start.1
  1.4 2.2 %panel_signs.1.signs_ref = bf16[2048,512]{1,0:T(8,128)(2,1)S(1)} custom-call(s32[7]{0:T(128)S(1)} %stack.27.words_ref), custom_call_target="tpu_custom_call" | custom-call | flops 2200000000 | bytes 1000000 | tf_op jit(solution)/shard_map/panel_signs/pallas_call | solution.py:81
  3.6 0.0 copy-done
  3.6 0.0 copy-done.1
  3.6 1.1 %panel_part.1 = (f32[64,512]{1,0:T(8,128)S(1)}, f32[64,512]{1,0:T(8,128)S(1)}, bf16[128,2048]{1,0:T(8,128)(2,1)S(1)}) custom-call(s32[7]{0:T(128)S(1)} %stack.27.words_ref, s32[1,128]{1,0:T(1,128)S(1)} %bitcast.7, bf16[256,2048]{1,0:T(8,128)(2,1)S(1)} %copy-done, bf16[2048,512]{1,0:T(8,128)(2,1)S(1)} %panel_signs.1.signs_ref), custom_call_target="tpu_custom_call" | custom-call | flops 1100000000 | bytes 1000000 | tf_op jit(solution)/shard_map/panel_part/pallas_call | solution.py:100
  4.8 0.5 %collective-permute-start = (f32[64,512]{1,0:T(8,128)S(1)}, f32[64,512]{1,0:T(8,128)S(1)}, u32[]{:S(2)}, u32[]{:S(2)}) collective-permute-start(f32[64,512]{1,0:T(8,128)S(1)} %get-tuple-element.28), channel_id=1, source_target_pairs={{0,4},{4,0},{8,12},{12,8},{1,5},{5,1},{9,13},{13,9},{2,6},{6,2},{1... | collective-permute-start | bytes 393224 | tf_op jit(solution)/shard_map/ppermute | solution.py:475
  5.3 1.0 %collective-permute-done = f32[64,512]{1,0:T(8,128)S(1)} collective-permute-done((f32[64,512]{1,0:T(8,128)S(1)}, f32[64,512]{1,0:T(8,128)S(1)}, u32[]{:S(2)}, u32[]{:S(2)}) %collective-permute-start) | collective-permute-done | bytes 131104 | tf_op jit(solution)/shard_map/ppermute | solution.py:475
  6.3 2.9 %collective-permute-start.1 = (f32[64,512]{1,0:T(8,128)S(1)}, f32[64,512]{1,0:T(8,128)S(1)}, u32[]{:S(2)}, u32[]{:S(2)}) collective-permute-start(f32[64,512]{1,0:T(8,128)S(1)} %add.15._), channel_id=1, source_target_pairs={{0,8},{4,12},{8,0},{12,4},{1,9},{5,13},{9,1},{13,5},{2,10},{6,14},... | collective-permute-start | bytes 393224 | tf_op jit(solution)/shard_map/ppermute | solution.py:475
  9.2 4.1 %blocks_part.1 = (f32[128,512]{1,0:T(8,128)S(1)}, f32[128,512]{1,0:T(8,128)S(1)}) custom-call(s32[7]{0:T(128)S(1)} %stack.27.words_ref, bf16[128,2048]{1,0:T(8,128)(2,1)S(1)} %get-tuple-element.29.chosen_ref, f32[64,512]{1,0:T(8,128)S(1)} %add.15._), custom_call_target="tpu_custom_call" | custom-call | flops 4400000000 | bytes 1000000 | tf_op jit(solution)/shard_map/blocks_part/pallas_call | solution.py:116
  13.3 0.0 collective-permute-done.1
  13.4 1.6 %collective-permute-start.2 = (bf16[64,512]{1,0:T(8,128)(2,1)S(1)}, bf16[64,512]{1,0:T(8,128)(2,1)S(1)}, u32[]{:S(2)}, u32[]{:S(2)}) collective-permute-start(bf16[64,512]{1,0:T(8,128)(2,1)S(1)} %get-tuple-element.52.refs_0_.refs_8_), channel_id=1, source_target_pairs={{0,16},{16,0},{1,17},{17,1},{2,18},{18,2},{3,19},{19,3},{4,20},{20... | collective-permute-start | bytes 196616 | tf_op jit(solution)/shard_map/ppermute | solution.py:475
  14.9 2.8 %other_parts.1 = (f32[64,2560]{1,0:T(8,128)S(1)}, f32[64,2560]{1,0:T(8,128)S(1)}) custom-call(s32[7]{0:T(128)S(1)} %stack.27.words_ref, bf16[128,2048]{1,0:T(8,128)(2,1)S(1)} %get-tuple-element.29.chosen_ref, f32[64,512]{1,0:T(8,128)S(1)} %get-tuple-element.53._, f32[128,512]{1,0:T(8,128)S(1)} %get-tuple-element.30.refs_0_, ...), custom_call_target="tpu_custom_call" | custom-call | flops 2200000000 | bytes 1000000 | tf_op jit(solution)/shard_map/other_parts/pallas_call | solution.py:162
  17.8 0.0 collective-permute-done.2.refs_1_.refs_9_
  17.8 0.1 collective-permute-start.5
  17.8 0.5 %collective-permute-start.3 = (bf16[64,512]{1,0:T(8,128)(2,1)S(1)}, bf16[64,512]{1,0:T(8,128)(2,1)S(1)}, u32[]{:S(2)}, u32[]{:S(2)}) collective-permute-start(bf16[64,512]{1,0:T(8,128)(2,1)S(1)} %get-tuple-element.52.refs_0_.refs_8_), channel_id=1, source_target_pairs={{0,4},{4,0},{8,12},{12,8},{1,5},{5,1},{9,13},{13,9},{2,6},{6,2},{1... | collective-permute-start | bytes 196616 | tf_op jit(solution)/shard_map/ppermute | solution.py:475
  18.3 0.1 collective-permute-start.4
  19.1 0.9 %collective-permute-done.5.right_ref = f32[64,2560]{1,0:T(8,128)S(1)} collective-permute-done((f32[64,2560]{1,0:T(8,128)S(1)}, f32[64,2560]{1,0:T(8,128)S(1)}, u32[]{:S(2)}, u32[]{:S(2)}) %collective-permute-start.5) | collective-permute-done | bytes 655392 | tf_op jit(solution)/shard_map/ppermute | solution.py:475
  19.9 0.7 %halve.1 = (f32[64,1280]{1,0:T(8,128)S(1)}, f32[64,1280]{1,0:T(8,128)S(1)}) custom-call(s32[7]{0:T(128)S(1)} %stack.27.words_ref, f32[64,2560]{1,0:T(8,128)S(1)} %get-tuple-element.46.left_ref, f32[64,2560]{1,0:T(8,128)S(1)} %collective-permute-done.5.right_ref), custom_call_target="tpu_custom_call" | custom-call | flops 550000000 | bytes 1000000 | tf_op jit(solution)/shard_map/halve/pallas_call | solution.py:201
  20.6 1.5 %collective-permute-start.6 = (f32[64,1280]{1,0:T(8,128)S(1)}, f32[64,1280]{1,0:T(8,128)S(1)}, u32[]{:S(2)}, u32[]{:S(2)}) collective-permute-start(f32[64,1280]{1,0:T(8,128)S(1)} %get-tuple-element.49), channel_id=1, source_target_pairs={{0,8},{4,12},{8,0},{12,4},{1,9},{5,13},{9,1},{13,5},{2,10},{6,14},... | collective-permute-start | bytes 983048 | tf_op jit(solution)/shard_map/ppermute | solution.py:475
  22.1 0.0 collective-permute-done.3.refs_2_.refs_10_
  22.1 0.0 collective-permute-done.4.refs_3_.refs_11_
  22.1 7.5 %gram_first_blocks.1 = (f32[128,512]{1,0:T(8,128)S(1)}, f32[128,384]{1,0:T(8,128)S(1)}, f32[256,128]{1,0:T(8,128)S(1)}, f32[256,128]{1,0:T(8,128)S(1)}, f32[256,256]{1,0:T(8,128)S(1)}, /*index=5*/f32[256,256]{1,0:T(8,128)S(1)}) custom-call(s32[7]{0:T(128)S(1)} %stack.27.words_ref, f32[1]{0:T(128)S(6)} %copy.7.ridge_ref, ...), custom_call_target="tpu_custom_call" | custom-call | flops 3849999872 | bytes 1000000 | tf_op jit(solution)/shard_map/gram_first_blocks/pallas_call | solution.py:383
  29.6 0.8 %collective-permute-done.6.right_ref = f32[64,1280]{1,0:T(8,128)S(1)} collective-permute-done((f32[64,1280]{1,0:T(8,128)S(1)}, f32[64,1280]{1,0:T(8,128)S(1)}, u32[]{:S(2)}, u32[]{:S(2)}) %collective-permute-start.6) | collective-permute-done | bytes 327712 | tf_op jit(solution)/shard_map/ppermute | solution.py:475
  30.4 0.6 %pieces.1 = (bf16[64,1280]{1,0:T(8,128)(2,1)S(1)}, bf16[64,1280]{1,0:T(8,128)(2,1)S(1)}) custom-call(s32[7]{0:T(128)S(1)} %stack.27.words_ref, f32[64,1280]{1,0:T(8,128)S(1)} %get-tuple-element.48.left_ref, f32[64,1280]{1,0:T(8,128)S(1)} %collective-permute-done.6.right_ref, f32[256,128]{1,0:T(8,128)S(1)} %get-tuple-element.43._.refs_5_), custom_call_target="tpu_custom_call" | custom-call | flops 550000000 | bytes 1000000 | tf_op jit(solution)/shard_map/pieces/pallas_call | solution.py:219
  31.0 1.4 %collective-permute-start.7 = (bf16[64,1280]{1,0:T(8,128)(2,1)S(1)}, bf16[64,1280]{1,0:T(8,128)(2,1)S(1)}, u32[]{:S(2)}, u32[]{:S(2)}) collective-permute-start(bf16[64,1280]{1,0:T(8,128)(2,1)S(1)} %get-tuple-element.51), channel_id=1, source_target_pairs={{0,16},{16,0},{1,17},{17,1},{2,18},{18,2},{3,19},{19,3},{4,20},{20... | collective-permute-start | bytes 491528 | tf_op jit(solution)/shard_map/ppermute | solution.py:475
  32.4 3.3 %eliminate_blocks.2 = (f32[128,256]{1,0:T(8,128)S(1)}, f32[256,128]{1,0:T(8,128)S(1)}, f32[128,128]{1,0:T(8,128)S(1)}, f32[256,128]{1,0:T(8,128)S(1)}) custom-call(f32[256,256]{1,0:T(8,128)S(1)} %get-tuple-element.36.gram_ref, f32[256,256]{1,0:T(8,128)S(1)} %get-tuple-element.37.turned_ref), custom_call_target="tpu_custom_call" | custom-call | flops 4400000000 | bytes 1000000 | tf_op jit(solution)/shard_map/eliminate_blocks/pallas_call | solution.py:395
  35.8 0.1 collective-permute-start.8
  35.8 0.6 %collective-permute-done.7.refs_13_ = bf16[64,1280]{1,0:T(8,128)(2,1)S(1)} collective-permute-done((bf16[64,1280]{1,0:T(8,128)(2,1)S(1)}, bf16[64,1280]{1,0:T(8,128)(2,1)S(1)}, u32[]{:S(2)}, u32[]{:S(2)}) %collective-permute-start.7) | collective-permute-done | bytes 163872 | tf_op jit(solution)/shard_map/ppermute | solution.py:475
  36.5 0.0 collective-permute-start.9
  36.5 3.0 %eliminate_blocks.3 = (f32[128,128]{1,0:T(8,128)S(1)}, f32[256,128]{1,0:T(8,128)S(1)}) custom-call(f32[128,128]{1,0:T(8,128)S(1)} %get-tuple-element.39.gram_ref, f32[256,128]{1,0:T(8,128)S(1)} %get-tuple-element.40.turned_ref), custom_call_target="tpu_custom_call" | custom-call | flops 4400000000 | bytes 1000000 | tf_op jit(solution)/shard_map/eliminate_blocks/pallas_call | solution.py:395
  39.5 0.0 collective-permute-done.8.refs_14_
  39.5 0.0 collective-permute-done.9.refs_15_
  39.5 3.7 %finish.1 = (f32[256,512]{1,0:T(8,128)}, f32[256,512]{1,0:T(8,128)}) custom-call(s32[7]{0:T(128)S(1)} %stack.27.words_ref, f32[1]{0:T(128)S(6)} %copy.7.ridge_ref, f32[128,512]{1,0:T(8,128)S(1)} %get-tuple-element.34.refs_0_, f32[128,384]{1,0:T(8,128)S(1)} %get-tuple-element.35.refs_1_, f32[128,256]{1,0:T(8,128)S(1)} %get-tuple-element.38.refs_2_, ...), custom_call_target="tpu_custom_call" | custom-call | flops 3300000000 | bytes 1000000 | tf_op jit(solution)/shard_map/finish/pallas_call | solution.py:463
  (2 shorter events, 0.0 us)
Async XLA Ops:
  1.4 2.2 %copy-start = (bf16[256,2048]{1,0:T(8,128)(2,1)S(1)}, bf16[256,2048]{1,0:T(8,128)(2,1)}, u32[]{:S(2)}) copy-start(bf16[256,2048]{1,0:T(8,128)(2,1)} %pool_ref.1) | copy-start | bytes 3145732
  1.4 2.2 %copy-start.1 = (s32[128]{0:T(128)S(1)}, s32[128]{0:T(128)}, u32[]{:S(2)}) copy-start(s32[128]{0:T(128)} %param.5) | copy-start | bytes 1540
  4.8 1.5 %collective-permute-start = (f32[64,512]{1,0:T(8,128)S(1)}, f32[64,512]{1,0:T(8,128)S(1)}, u32[]{:S(2)}, u32[]{:S(2)}) collective-permute-start(f32[64,512]{1,0:T(8,128)S(1)} %get-tuple-element.28), channel_id=1, source_target_pairs={{0,4},{4,0},{8,12},{12,8},{1,5},{5,1},{9,13},{13,9},{2,6},{6,2},{1... | collective-permute-start | bytes 393224 | tf_op jit(solution)/shard_map/ppermute | solution.py:475
  6.3 7.1 %collective-permute-start.1 = (f32[64,512]{1,0:T(8,128)S(1)}, f32[64,512]{1,0:T(8,128)S(1)}, u32[]{:S(2)}, u32[]{:S(2)}) collective-permute-start(f32[64,512]{1,0:T(8,128)S(1)} %add.15._), channel_id=1, source_target_pairs={{0,8},{4,12},{8,0},{12,4},{1,9},{5,13},{9,1},{13,5},{2,10},{6,14},... | collective-permute-start | bytes 393224 | tf_op jit(solution)/shard_map/ppermute | solution.py:475
  13.4 4.4 %collective-permute-start.2 = (bf16[64,512]{1,0:T(8,128)(2,1)S(1)}, bf16[64,512]{1,0:T(8,128)(2,1)S(1)}, u32[]{:S(2)}, u32[]{:S(2)}) collective-permute-start(bf16[64,512]{1,0:T(8,128)(2,1)S(1)} %get-tuple-element.52.refs_0_.refs_8_), channel_id=1, source_target_pairs={{0,16},{16,0},{1,17},{17,1},{2,18},{18,2},{3,19},{19,3},{4,20},{20... | collective-permute-start | bytes 196616 | tf_op jit(solution)/shard_map/ppermute | solution.py:475
  17.8 2.2 %collective-permute-start.5 = (f32[64,2560]{1,0:T(8,128)S(1)}, f32[64,2560]{1,0:T(8,128)S(1)}, u32[]{:S(2)}, u32[]{:S(2)}) collective-permute-start(f32[64,2560]{1,0:T(8,128)S(1)} %get-tuple-element.47), channel_id=1, source_target_pairs={{0,4},{4,0},{8,12},{12,8},{1,5},{5,1},{9,13},{13,9},{2,6},{6,2},{1... | collective-permute-start | bytes 1966088 | tf_op jit(solution)/shard_map/ppermute | solution.py:475
  17.8 4.2 %collective-permute-start.3 = (bf16[64,512]{1,0:T(8,128)(2,1)S(1)}, bf16[64,512]{1,0:T(8,128)(2,1)S(1)}, u32[]{:S(2)}, u32[]{:S(2)}) collective-permute-start(bf16[64,512]{1,0:T(8,128)(2,1)S(1)} %get-tuple-element.52.refs_0_.refs_8_), channel_id=1, source_target_pairs={{0,4},{4,0},{8,12},{12,8},{1,5},{5,1},{9,13},{13,9},{2,6},{6,2},{1... | collective-permute-start | bytes 196616 | tf_op jit(solution)/shard_map/ppermute | solution.py:475
  18.3 3.7 %collective-permute-start.4 = (bf16[64,512]{1,0:T(8,128)(2,1)S(1)}, bf16[64,512]{1,0:T(8,128)(2,1)S(1)}, u32[]{:S(2)}, u32[]{:S(2)}) collective-permute-start(bf16[64,512]{1,0:T(8,128)(2,1)S(1)} %collective-permute-done.2.refs_1_.refs_9_), channel_id=1, source_target_pairs={{0,4},{4,0},{8,12},{12,8},{1,5},{5,1},{9,13},{13,9},{2,6},{6,2},{1... | collective-permute-start | bytes 196616 | tf_op jit(solution)/shard_map/ppermute | solution.py:475
  20.6 9.8 %collective-permute-start.6 = (f32[64,1280]{1,0:T(8,128)S(1)}, f32[64,1280]{1,0:T(8,128)S(1)}, u32[]{:S(2)}, u32[]{:S(2)}) collective-permute-start(f32[64,1280]{1,0:T(8,128)S(1)} %get-tuple-element.49), channel_id=1, source_target_pairs={{0,8},{4,12},{8,0},{12,4},{1,9},{5,13},{9,1},{13,5},{2,10},{6,14},... | collective-permute-start | bytes 983048 | tf_op jit(solution)/shard_map/ppermute | solution.py:475
  31.0 5.5 %collective-permute-start.7 = (bf16[64,1280]{1,0:T(8,128)(2,1)S(1)}, bf16[64,1280]{1,0:T(8,128)(2,1)S(1)}, u32[]{:S(2)}, u32[]{:S(2)}) collective-permute-start(bf16[64,1280]{1,0:T(8,128)(2,1)S(1)} %get-tuple-element.51), channel_id=1, source_target_pairs={{0,16},{16,0},{1,17},{17,1},{2,18},{18,2},{3,19},{19,3},{4,20},{20... | collective-permute-start | bytes 491528 | tf_op jit(solution)/shard_map/ppermute | solution.py:475
  35.8 3.7 %collective-permute-start.8 = (bf16[64,1280]{1,0:T(8,128)(2,1)S(1)}, bf16[64,1280]{1,0:T(8,128)(2,1)S(1)}, u32[]{:S(2)}, u32[]{:S(2)}) collective-permute-start(bf16[64,1280]{1,0:T(8,128)(2,1)S(1)} %get-tuple-element.50.refs_12_), channel_id=1, source_target_pairs={{0,4},{4,0},{8,12},{12,8},{1,5},{5,1},{9,13},{13,9},{2,6},{6,2},{1... | collective-permute-start | bytes 491528 | tf_op jit(solution)/shard_map/ppermute | solution.py:475
  36.5 3.0 %collective-permute-start.9 = (bf16[64,1280]{1,0:T(8,128)(2,1)S(1)}, bf16[64,1280]{1,0:T(8,128)(2,1)S(1)}, u32[]{:S(2)}, u32[]{:S(2)}) collective-permute-start(bf16[64,1280]{1,0:T(8,128)(2,1)S(1)} %collective-permute-done.7.refs_13_), channel_id=1, source_target_pairs={{0,4},{4,0},{8,12},{12,8},{1,5},{5,1},{9,13},{13,9},{2,6},{6,2},{1... | collective-permute-start | bytes 491528 | tf_op jit(solution)/shard_map/ppermute | solution.py:475

commit v5 on v4

--- a/solution.py
+++ b/solution.py
@@ -10,13 +10,13 @@
 
 PANEL = 512
 HALF = 256
-STRIPE = 32
-SUB = 16
+STRIPE = 64
+SUB = 8
+LEAD = 3
 BLOCK = 128
 DEPTH = 256
 SEGMENT = 128
 VMEM = pl.BlockSpec(memory_space=pltpu.VMEM)
-SMEM = pl.BlockSpec(memory_space=pltpu.SMEM)
 ANYWHERE = pl.BlockSpec(memory_space=pl.ANY)
 
 
@@ -54,83 +54,90 @@
     return jnp.where(decided == 0, jnp.bfloat16(1.0), jnp.bfloat16(-1.0))
 
 
-def segment_signs(words_ref, feature, width, index):
-    return sign_tile(words_ref[0], words_ref[1] + index * SEGMENT, feature, (SEGMENT, width))
-
-
-def project_step(words_ref, chosen_ref, feature, width, index, total):
+def segment_signs(seed_ref, coordinates, feature, width, index):
+    first = lax.axis_index("tp") * coordinates + index * SEGMENT
+    return sign_tile(seed_ref[...], first, feature, (SEGMENT, width))
+
+
+def project_step(seed_ref, chosen_ref, feature, width, index, total):
     start = pl.multiple_of(index * SEGMENT, SEGMENT)
-    signs = segment_signs(words_ref, feature, width, index)
+    signs = segment_signs(seed_ref, chosen_ref.shape[1], feature, width, index)
     return total + jnp.dot(chosen_ref[:, pl.ds(start, SEGMENT)], signs, preferred_element_type=jnp.float32)
 
 
-def project_tile(words_ref, chosen_ref, feature, width, unroll):
+def project_tile(seed_ref, chosen_ref, feature, width, unroll):
     rows, coordinates = chosen_ref.shape
-    step = functools.partial(project_step, words_ref, chosen_ref, feature, width)
+    step = functools.partial(project_step, seed_ref, chosen_ref, feature, width)
     zero = jnp.zeros((rows, width), jnp.float32)
     return lax.fori_loop(0, coordinates // SEGMENT, step, zero, unroll=unroll)
 
 
-def panel_signs_kernel(words_ref, signs_ref):
+def even_of_pair():
+    return lax.axis_index("tp") % 2 == 0
+
+
+def panel_signs_kernel(seed_ref, signs_ref):
     coordinates, width = signs_ref.shape
     for step in range(coordinates // SEGMENT):
-        signs_ref[step * SEGMENT : (step + 1) * SEGMENT, :] = segment_signs(words_ref, 0, width, step)
-
-
-def panel_signs(words, coordinates):
-    return call(
-        panel_signs_kernel, [((coordinates, PANEL), jnp.bfloat16)], [SMEM], 2, "panel_signs"
-    )(words)[0]
-
-
-def panel_part_kernel(words_ref, selection_ref, pool_ref, signs_ref, mine_ref, theirs_ref, chosen_ref):
+        signs_ref[step * SEGMENT : (step + 1) * SEGMENT, :] = segment_signs(
+            seed_ref, coordinates, 0, width, step
+        )
+
+
+def panel_signs(seed, coordinates):
+    return call(
+        panel_signs_kernel, [((coordinates, PANEL), jnp.bfloat16)], [VMEM], 2, "panel_signs"
+    )(seed)[0]
+
+
+def panel_part_kernel(selection_ref, pool_ref, signs_ref, mine_ref, theirs_ref, chosen_ref):
     half = mine_ref.shape[0]
     shape = (pool_ref.shape[0], chosen_ref.shape[0])
     picked = jnp.where(lax.broadcasted_iota(jnp.int32, shape, 0) == selection_ref[...], 1.0, 0.0)
     chosen = tdot(picked.astype(jnp.bfloat16), pool_ref[...]).astype(jnp.bfloat16)
     chosen_ref[...] = chosen
     total = jnp.dot(chosen, signs_ref[...], preferred_element_type=jnp.float32)
-    even = words_ref[2] == 0
+    even = even_of_pair()
     mine_ref[...] = jnp.where(even, total[:half], total[half:])
     theirs_ref[...] = jnp.where(even, total[half:], total[:half])
 
 
-def panel_part(words, selection, pool):
+def panel_part(seed, selection, pool):
     rows, coordinates = selection.shape[0], pool.shape[1]
     return call(
         panel_part_kernel,
         [((rows // 2, PANEL), jnp.float32)] * 2 + [((rows, coordinates), jnp.bfloat16)],
-        [SMEM, VMEM, VMEM, VMEM],
+        [VMEM, VMEM, VMEM],
         1,
         "panel_part",
-    )(words, selection[None, :], pool, panel_signs(words, coordinates))
-
-
-def blocks_part_kernel(blocks, words_ref, chosen_ref, _, *part_refs):
+    )(selection[None, :], pool, panel_signs(seed, coordinates))
+
+
+def blocks_part_kernel(blocks, seed_ref, chosen_ref, _, *part_refs):
     width = part_refs[0].shape[1]
     for block, part_ref in zip(blocks, part_refs):
-        part_ref[...] = project_tile(words_ref, chosen_ref, block * width, width, len(blocks) <= 2)
-
-
-def blocks_part(words, chosen, blocks, width, after):
+        part_ref[...] = project_tile(seed_ref, chosen_ref, block * width, width, len(blocks) <= 2)
+
+
+def blocks_part(seed, chosen, blocks, width, after):
     return call(
         functools.partial(blocks_part_kernel, blocks),
         [((chosen.shape[0], width), jnp.float32)] * len(blocks),
-        [SMEM, VMEM, ANYWHERE],
+        [VMEM, VMEM, ANYWHERE],
         2 * len(blocks),
         "blocks_part",
         vmem=32 if len(blocks) > 2 else 16,
-    )(words, chosen, after)
-
-
-def other_parts_kernel(tp_count, blk_count, words_ref, chosen_ref, _, *refs):
+    )(seed, chosen, after)
+
+
+def other_parts_kernel(tp_count, blk_count, seed_ref, chosen_ref, _, *refs):
     *first_refs, mine_ref, theirs_ref = refs
     rows = chosen_ref.shape[0]
     half = rows // 2
     width = first_refs[0].shape[1]
     groups = width // HALF
     row_lanes = tp_count * groups // blk_count * HALF
-    even = words_ref[2] == 0
+    even = even_of_pair()
     for ref in (mine_ref, theirs_ref):
         ref[:, : row_lanes + 2 * width] = jnp.zeros((half, row_lanes + 2 * width), jnp.float32)
 
@@ -143,30 +150,30 @@
         if block <= len(first_refs):
             part = first_refs[block - 1][...]
         else:
-            part = project_tile(words_ref, chosen_ref, block * width, width, tp_count <= 4)
-        own = words_ref[2] == block % 2
+            part = project_tile(seed_ref, chosen_ref, block * width, width, tp_count <= 4)
+        own = lax.axis_index("tp") % 2 == block % 2
         pl.when(own)(functools.partial(place, mine_ref, lane, part))
         pl.when(jnp.logical_not(own))(functools.partial(place, theirs_ref, lane, part))
         for which in range(groups):
             group = block * groups + which
 
-            @pl.when(words_ref[3] == group % blk_count)
+            @pl.when(lax.axis_index("blk") == group % blk_count)
             def _(part=part[:, which * HALF : (which + 1) * HALF], lane=group // blk_count * HALF):
                 mine_ref[:, lane : lane + HALF] = jnp.where(even, part[:half], part[half:])
                 theirs_ref[:, lane : lane + HALF] = jnp.where(even, part[half:], part[:half])
 
 
-def other_parts(words, chosen, first, tp_count, blk_count, after):
+def other_parts(seed, chosen, first, tp_count, blk_count, after):
     rows, width = first[0].shape
     lanes = tp_count * (width // HALF) // blk_count * HALF + tp_count // 2 * 2 * width
     return call(
         functools.partial(other_parts_kernel, tp_count, blk_count),
         [((rows // 2, lanes), jnp.float32)] * 2,
-        [SMEM, VMEM, ANYWHERE] + [VMEM] * len(first),
+        [VMEM, VMEM, ANYWHERE] + [VMEM] * len(first),
         2 * (tp_count - 1 - len(first)),
         "other_parts",
         vmem=16 if tp_count <= 4 else 48,
-    )(words, chosen, after, *first)
+    )(seed, chosen, after, *first)
 
 
 def group_at(rows, index, count):
@@ -176,53 +183,92 @@
     return found
 
 
-def halve_kernel(ex_count, bit, words_ref, left_ref, right_ref, keep_ref, send_ref):
+def halve_kernel(ex_count, bit, left_ref, right_ref, keep_ref, send_ref):
     row_lanes = ex_count * HALF
-    upper = words_ref[4] & bit != 0
-    rows = left_ref[:, :row_lanes] + right_ref[:, :row_lanes]
-    columns = left_ref[:, row_lanes:] + right_ref[:, row_lanes:]
-    middle = columns.shape[1] // 2
-    lanes = keep_ref.shape[1] - middle
-    if bit > 2:
-        keep_ref[:, :lanes] = rows
-        send_ref[:, :lanes] = rows
-    else:
-        for step in range(1, ex_count):
-            place = slice((step - 1) * HALF, step * HALF)
-            keep_ref[:, place] = group_at(rows, words_ref[4] // 2 ^ step, ex_count)
-            send_ref[:, place] = group_at(rows, words_ref[4] // 2 ^ 1 ^ step, ex_count)
-    keep_ref[:, lanes:] = jnp.where(upper, columns[:, middle:], columns[:, :middle])
-    send_ref[:, lanes:] = jnp.where(upper, columns[:, :middle], columns[:, middle:])
-
-
-def halve(words, left, right, ex_count, bit):
-    lanes = (ex_count if bit > 2 else ex_count - 1) * HALF
-    shape = (left.shape[0], (left.shape[1] - ex_count * HALF) // 2 + lanes)
+    upper = lax.axis_index("tp") & bit != 0
+    total = left_ref[...] + right_ref[...]
+    middle = (total.shape[1] + row_lanes) // 2
+    keep_ref[:, :row_lanes] = total[:, :row_lanes]
+    send_ref[:, :row_lanes] = total[:, :row_lanes]
+    keep_ref[:, row_lanes:] = jnp.where(upper, total[:, middle:], total[:, row_lanes:middle])
+    send_ref[:, row_lanes:] = jnp.where(upper, total[:, row_lanes:middle], total[:, middle:])
+
+
+def halve(left, right, ex_count, bit):
+    shape = (left.shape[0], (left.shape[1] + ex_count * HALF) // 2)
     return call(
         functools.partial(halve_kernel, ex_count, bit),
         [(shape, jnp.float32)] * 2,
-        [SMEM, VMEM, VMEM],
+        [VMEM, VMEM],
         0.5,
         "halve",
-    )(words, left, right)
-
-
-def pieces_kernel(ex_count, scaling, words_ref, left_ref, right_ref, _, *piece_refs):
-    total = ((left_ref[...] + right_ref[...]) * scaling).astype(jnp.bfloat16)
+    )(left, right)
+
+
+def last_half(ex_count, holder, left_ref, right_ref):
+    def picked(index, places):
+        found = None
+        for place, lanes in enumerate(places):
+            value = (left_ref[:, lanes], right_ref[:, lanes])
+            if found is None:
+                found = value
+            else:
+                found = tuple(jnp.where(index == place, new, old) for new, old in zip(value, found))
+        return found[0] + found[1]
+
+    groups = [slice(place * HALF, (place + 1) * HALF) for place in range(ex_count)]
+    row_lanes = ex_count * HALF
+    middle = (left_ref.shape[1] + row_lanes) // 2
+    blocks = [slice(row_lanes, middle), slice(middle, left_ref.shape[1])]
+    rows = [picked(holder ^ step, groups) for step in range(1, ex_count)]
+    return rows, picked(holder & 1, blocks)
+
+
+def send_kernel(ex_count, left_ref, right_ref, send_ref):
+    rows, columns = last_half(ex_count, lax.axis_index("tp") // 2 ^ 1, left_ref, right_ref)
+    lanes = (ex_count - 1) * HALF
+    send_ref[:, :lanes] = join(rows, 1)
+    send_ref[:, lanes:] = columns
+
+
+def last_sent(left, right, ex_count):
+    row_lanes = ex_count * HALF
+    shape = (left.shape[0], (left.shape[1] - row_lanes) // 2 + row_lanes - HALF)
+    return call(
+        functools.partial(send_kernel, ex_count),
+        [(shape, jnp.float32)],
+        [VMEM, VMEM],
+        0.5,
+        "last_sent",
+    )(left, right)[0]
+
+
+def pieces_kernel(ex_count, scaling, left_ref, right_ref, came_ref, _, *piece_refs):
+    holder = lax.axis_index("tp") // 2
+    rows, columns = last_half(ex_count, holder, left_ref, right_ref)
+    rows = [
+        ((row + came_ref[:, place * HALF : (place + 1) * HALF]) * scaling).astype(jnp.bfloat16)
+        for place, row in enumerate(rows)
+    ]
+    columns = ((columns + came_ref[:, (ex_count - 1) * HALF :]) * scaling).astype(jnp.bfloat16)
     for step, ref in enumerate(piece_refs):
-        ref[:, :HALF] = group_at(total, (words_ref[5] ^ step ^ (words_ref[4] // 2)) - 1, ex_count - 1)
-        ref[:, HALF:] = total[:, (ex_count - 1) * HALF :]
-
-
-def pieces(words, left, right, ex_count, scaling, after):
-    shape = (left.shape[0], left.shape[1] - (ex_count - 2) * HALF)
+        distance = lax.axis_index("ex") ^ step ^ holder
+        wanted = rows[0]
+        for place in range(1, ex_count - 1):
+            wanted = jnp.where(distance - 1 == place, rows[place], wanted)
+        ref[:, :HALF] = wanted
+        ref[:, HALF:] = columns
+
+
+def pieces(left, right, came, ex_count, scaling, after):
+    shape = (left.shape[0], came.shape[1] - (ex_count - 2) * HALF)
     return call(
         functools.partial(pieces_kernel, ex_count, scaling),
         [(shape, jnp.bfloat16)] * ex_count,
-        [SMEM, VMEM, VMEM, ANYWHERE],
+        [VMEM, VMEM, VMEM, ANYWHERE],
         0.5,
         "pieces",
-    )(words, left, right, after)
+    )(left, right, came, after)
 
 
 def tdot(left, right):
@@ -235,40 +281,47 @@
 
 def factor_stripe(rows_u, rows_z, offset):
     groups = len(rows_u)
+    count = 8 * groups
     sub = lax.broadcasted_iota(jnp.int32, (8, BLOCK), 0)
     rows_u, rows_z = list(rows_u), list(rows_z)
     pivots = [jnp.ones((8, BLOCK), jnp.float32) for _ in range(groups)]
-    for base in range(0, 8 * groups, SUB):
-        columns = {
+
+    def taken(base):
+        return {
             c: {
                 v: jnp.broadcast_to(rows_u[v][:, offset + c : offset + c + 1], (8, BLOCK))
                 for v in range(c // 8, groups)
             }
             for c in range(base, base + SUB)
         }
-        pivot = row_of(columns[base][base // 8], 0)
-        for j in range(base, base + SUB):
-            g, s = divmod(j, 8)
-            column = columns[j]
-            inverse = 1.0 / pivot
-            pivots[g] = jnp.where(sub == s, pivot, pivots[g])
-            if j + 1 < base + SUB:
-                n, r = divmod(j + 1, 8)
-                weight = row_of(column[n], r)
-                following = columns[j + 1]
-                pivot = row_of(following[n], r) - (weight * weight) * inverse
-                for v in range(n, groups):
-                    following[v] = following[v] - (column[v] * weight) * inverse
-            factors = {v: column[v] * inverse for v in range(g, groups)}
-            for c in range(j + 2, base + SUB):
+
+    columns = taken(0)
+    pivot = row_of(columns[0][0], 0)
+    for j in range(count):
+        g, s = divmod(j, 8)
+        if j % SUB == SUB - LEAD and j + LEAD < count:
+            columns.update(taken(j + LEAD))
+        column = columns.pop(j)
+        inverse = 1.0 / pivot
+        pivots[g] = jnp.where(sub == s, pivot, pivots[g])
+        if j + 1 < count:
+            n, r = divmod(j + 1, 8)
+            weight = row_of(column[n], r)
+            following = columns[j + 1]
+            pivot = row_of(following[n], r) - (weight * weight) * inverse
+            for v in range(n, groups):
+                following[v] = following[v] - (column[v] * weight) * inverse
+        factors = {v: column[v] * inverse for v in range(g, groups)}
+        for c, other in columns.items():
+            if c > j + 1:
                 weight = row_of(column[c // 8], c % 8)
                 for v in range(c // 8, groups):
-                    columns[c][v] = columns[c][v] - factors[v] * weight
-            factors[g] = jnp.where(sub > s, factors[g], 0.0)
-            row_u, row_z = row_of(rows_u[g], s), row_of(rows_z[g], s)
-            for v in range(g + (s == 7), groups):
-                rows_u[v] = rows_u[v] - factors[v] * row_u
-                rows_z[v] = rows_z[v] - factors[v] * row_z
+                    other[v] = other[v] - factors[v] * weight
+        factors[g] = jnp.where(sub > s, factors[g], 0.0)
+        row_u, row_z = row_of(rows_u[g], s), row_of(rows_z[g], s)
+        for v in range(g + (s == 7), groups):
+            rows_u[v] = rows_u[v] - factors[v] * row_u
+            rows_z[v] = rows_z[v] - factors[v] * row_z
     scales = [lax.rsqrt(pivot) for pivot in pivots]
     return (
         [row * scale for row, scale in zip(rows_u, scales)],
@@ -352,11 +405,11 @@
         rest_refs[1][...] = turned
 
 
-def first_blocks_kernel(blocks, count, words_ref, ridge_ref, *refs):
+def first_blocks_kernel(blocks, count, ridge_ref, *refs):
     phi_refs, out_refs = refs[:count], refs[count:]
-    phi = in_pair_order(words_ref[2] == 0, phi_refs)
+    phi = in_pair_order(even_of_pair(), phi_refs)
     examples, width = phi.shape
-    gram = tdot(phi, phi) * (1.0 / examples) + jnp.where(identity_mask((width, width)), ridge_ref[0], 0.0)
+    gram = tdot(phi, phi) * (1.0 / examples) + jnp.where(identity_mask((width, width)), ridge_ref[...], 0.0)
     eliminate(
         gram, phi.astype(jnp.float32), out_refs[:blocks], out_refs[blocks : 2 * blocks], out_refs[2 * blocks :]
     )
@@ -378,15 +431,15 @@
     return list(results[:blocks]), list(results[blocks : 2 * blocks]), results[2 * blocks :]
 
 
-def first_blocks(words, ridge_value, phi, blocks):
+def first_blocks(ridge, phi, blocks):
     examples, width = sum(part.shape[0] for part in phi), phi[0].shape[1]
     results = call(
         functools.partial(first_blocks_kernel, blocks, len(phi)),
         block_shapes(width, examples, blocks),
-        [SMEM, SMEM] + [VMEM] * len(phi),
+        [VMEM] * (1 + len(phi)),
         3.5,
         "gram_first_blocks",
-    )(words, ridge_value, *phi)
+    )(ridge, *phi)
     return taken_apart(results, blocks)
 
 
@@ -402,14 +455,15 @@
     return taken_apart(results, blocks)
 
 
-def finish_kernel(blocks, count, words_ref, ridge_ref, *refs):
+def finish_kernel(blocks, count, blk_count, ridge_ref, *refs):
     uppers, dones = refs[:blocks], refs[blocks : 2 * blocks]
     phi_refs, piece_refs = refs[2 * blocks : 2 * blocks + count], refs[2 * blocks + count : -3]
     panel_ref, trailing_ref, solved_ref = refs[-3:]
     height, panel = panel_ref.shape
     width = trailing_ref.shape[1]
-    even = words_ref[2] == 0
-    row_group, column_block = words_ref[6], words_ref[4]
+    even = even_of_pair()
+    ex_index, column_block, blk_index = (lax.axis_index(axis) for axis in ("ex", "tp", "blk"))
+    row_group = ex_index * blk_count + blk_index
     phi = in_pair_order(even, phi_refs)
     examples = phi.shape[0]
     mine, others = piece_refs[: count // 2], piece_refs[count // 2 :]
@@ -419,10 +473,10 @@
     )
     rows = in_pair_order(even, piece_refs, slice(0, height))
     groups = width // height
-    holder = words_ref[3] // groups
-    held = jnp.where(holder == words_ref[2], columns, pair_columns)
+    holder = blk_index // groups
+    held = jnp.where(holder == column_block % 2, columns, pair_columns)
     for place in range(groups):
-        inside = (words_ref[5] == column_block // 2) & (words_ref[3] % groups == place)
+        inside = (ex_index == column_block // 2) & (blk_index % groups == place)
         rows = jnp.where(inside, held[:, place * height : (place + 1) * height], rows)
     for start in range(0, panel, height):
         rows = jnp.where(row_group * height == start, phi[:, start : start + height], rows)
@@ -453,22 +507,22 @@
     ) == column_block * width + lax.broadcasted_iota(jnp.int32, shape, 1)
     gram = jnp.dot(turned[:height], columns, preferred_element_type=jnp.float32) * scale
     trailing_ref[...] = (
-        gram + jnp.where(diagonal, ridge_ref[0], 0.0) - exact_dot(panel_ref[...], solved_ref[...], (1, 1))
+        gram + jnp.where(diagonal, ridge_ref[...], 0.0) - exact_dot(panel_ref[...], solved_ref[...], (1, 1))
     )
 
 
-def finish(words, ridge_value, uppers, dones, phi, gathered, height, width):
+def finish(ridge, uppers, dones, phi, gathered, height, width, blk_count):
     panel = uppers[0].shape[1]
     operands = [*uppers, *dones, *phi, *gathered]
     return call(
-        functools.partial(finish_kernel, len(uppers), len(phi)),
+        functools.partial(finish_kernel, len(uppers), len(phi), blk_count),
         [((height, panel), jnp.float32), ((height, width), jnp.float32)],
-        [SMEM, SMEM] + [VMEM] * len(operands),
+        [VMEM] * (1 + len(operands)),
         3,
         "finish",
         [pltpu.VMEM((width, panel), jnp.float32)],
         vmem=24,
-    )(words, ridge_value, *operands)
+    )(ridge, *operands)
 
 
 def swapped(value, axis, bit):
@@ -487,23 +541,12 @@
     ex_count = lax.axis_size("ex")
     tp_count = lax.axis_size("tp")
     blk_count = lax.axis_size("blk")
-    ex_index, tp_index, blk_index = (lax.axis_index(axis) for axis in ("ex", "tp", "blk"))
     coord_dev = gradients.shape[1]
     column_width = HALF * ex_count * blk_count // tp_count
     scaling = 1.0 / math.sqrt(coord_dev * tp_count)
-    words = jnp.stack(
-        [
-            seed_value[0],
-            tp_index * coord_dev,
-            tp_index % 2,
-            blk_index,
-            tp_index,
-            ex_index,
-            ex_index * blk_count + blk_index,
-        ]
-    ).astype(jnp.int32)
-
-    mine, theirs, chosen = panel_part(words, selection, gradients)
+    seed, ridge = seed_value.reshape(1, 1), ridge_value.reshape(1, 1)
+
+    mine, theirs, chosen = panel_part(seed, selection, gradients)
     total = mine + swapped(theirs, "tp", 1)
     halves = total
     bit = 2
@@ -512,25 +555,26 @@
         bit *= 2
     phi = ex_parts([(total * scaling).astype(jnp.bfloat16)] * ex_count)
 
-    first = blocks_part(words, chosen, range(1, 1 + tp_count // 2), column_width, halves)
-    left, right = other_parts(words, chosen, first, tp_count, blk_count, total)
+    first = blocks_part(seed, chosen, range(1, 1 + tp_count // 2), column_width, halves)
+    left, right = other_parts(seed, chosen, first, tp_count, blk_count, total)
     phi[1:], right = lax.optimization_barrier((phi[1:], right))
     right = swapped(right, "tp", 1)
     bit = tp_count // 2
-    while bit > 1:
-        left, right = halve(words, left, right, ex_count, bit)
+    while bit > 2:
+        left, right = halve(left, right, ex_count, bit)
         right = swapped(right, "tp", bit)
         bit //= 2
+    came = swapped(last_sent(left, right, ex_count), "tp", 2)
 
     phi = with_pair(phi)
     half = PANEL // BLOCK // 2
-    uppers, dones, rest = first_blocks(words, ridge_value, phi, half)
-    gathered = pieces(words, left, right, ex_count, scaling, dones[-1])
+    uppers, dones, rest = first_blocks(ridge, phi, half)
+    gathered = pieces(left, right, came, ex_count, scaling, dones[-1])
     gathered = with_pair(ex_parts(gathered))
     while rest:
         more_uppers, more_dones, rest = next_blocks(rest, 1)
         uppers, dones = uppers + more_uppers, dones + more_dones
-    return tuple(finish(words, ridge_value, uppers, dones, phi, gathered, HALF, column_width))
+    return tuple(finish(ridge, uppers, dones, phi, gathered, HALF, column_width, blk_count))
 
 
 def solution(mesh):

time: 43.3 us -> 40.8 us (0.942)
  Pallas kernels: 29 us -> 24.9 us
  waiting for transfers between devices: 3.29 us -> 4.44 us
  starting transfers between devices: 8.66 us -> 9.23 us
    ppermute x10, waiting for transfers between devices: 3.29 us -> 4.44 us  [swapped(): lax.ppermute(value, axis, [(s, s ^ bit) for s in range(lax.axis_size(axis...]
    pallas_call x1, Pallas kernels: 7.51 us -> 6.43 us  [first_blocks(): call(functools.partial(first_blocks_kernel, blocks, len(phi)), block_shap...]
    pallas_call x3, Pallas kernels: 6.53 us -> 5.72 us  [the longest x1 3.19 us: finish(): call(functools.partial(finish_kernel, len(uppers), len(phi), blk_count),...]
    ppermute x10, starting transfers between devices: 8.66 us -> 9.23 us  [swapped(): lax.ppermute(value, axis, [(s, s ^ bit) for s in range(lax.axis_size(axis...]
    pallas_call x1, Pallas kernels: 1.15 us -> 0.61 us  [panel_part(): call(panel_part_kernel, [((rows // 2, PANEL), jnp.float32)] * 2 + [((rows...]
    pallas_call x1, Pallas kernels: 0.58 us -> 0.08 us  [pieces(): call(functools.partial(pieces_kernel, ex_count, scaling), [(shape, jnp.bf...]
    pallas_call x1, Pallas kernels: 2.8 us -> 2.32 us  [other_parts(): call(functools.partial(other_parts_kernel, tp_count, blk_count), [((rows...]
  transfers between devices with their start and end apart: 10 -> 10, of which waited for: 4 -> 5; matrix products, arithmetic and copies ran while one was open for 0% -> 0% of each run, Pallas kernels for 50% -> 46%
where the time goes in v5:
time: 40.8 us; the launch traced here: 40.7 us
  Pallas kernels  24.9 us (61%)
  starting transfers between devices  9.23 us (23%)
  waiting for transfers between devices  4.44 us (11%)
  between operations  2.07 us (5%)
    ppermute x10, starting transfers between devices, swapped(): lax.ppermute(value, axis, [(s, s ^ bit) for s in range(lax.axis_size(axis...  9.23 us
    pallas_call x1, Pallas kernels, first_blocks(): call(functools.partial(first_blocks_kernel, blocks, len(phi)), block_shap...  6.43 us
    pallas_call x2, Pallas kernels, next_blocks(): call(functools.partial(next_blocks_kernel, blocks), block_shapes(gram.sha...  5.89 us
    ppermute x10, waiting for transfers between devices, swapped(): lax.ppermute(value, axis, [(s, s ^ bit) for s in range(lax.axis_size(axis...  4.44 us
    pallas_call x1, Pallas kernels, blocks_part(): call(functools.partial(blocks_part_kernel, blocks), [((chosen.shape[0], w...  3.84 us
    pallas_call x1, Pallas kernels, finish(): call(functools.partial(finish_kernel, len(uppers), len(phi), blk_count),...  3.19 us
    pallas_call x1, Pallas kernels, panel_signs(): call(panel_signs_kernel, [((coordinates, PANEL), jnp.bfloat16)], [VMEM],...  2.46 us
    pallas_call x1, Pallas kernels, other_parts(): call(functools.partial(other_parts_kernel, tp_count, blk_count), [((rows...  2.32 us
  transfers between devices with their start and end apart: 10, of which 5 were waited for; matrix products, arithmetic and copies ran while one was open for 0% of the time, Pallas kernels for 46%

profile of v5, /device:TPU:0, one launch (start us, length us, event | category | flops | bytes accessed | tf_op | source)
XLA Modules:
  0.0 40.7 jit_solution(15567518343063733611)
XLA Ops:
  1.3 0.0 copy-start
  1.3 0.0 copy-start.1
  1.3 2.5 %panel_signs.1.signs_ref = bf16[2048,512]{1,0:T(8,128)(2,1)S(1)} custom-call(s32[1,1]{1,0:T(1,128)} %bitcast.3.seed_ref), custom_call_target="tpu_custom_call" | custom-call | flops 2200000000 | bytes 1000000 | tf_op jit(solution)/shard_map/panel_signs/pallas_call | solution.py:88
  3.8 0.0 copy-done
  3.8 0.0 copy-done.1
  3.8 0.6 %panel_part.1 = (f32[64,512]{1,0:T(8,128)S(1)}, f32[64,512]{1,0:T(8,128)S(1)}, bf16[128,2048]{1,0:T(8,128)(2,1)S(1)}) custom-call(s32[1,128]{1,0:T(1,128)S(1)} %bitcast.8, bf16[256,2048]{1,0:T(8,128)(2,1)S(1)} %copy-done, bf16[2048,512]{1,0:T(8,128)(2,1)S(1)} %panel_signs.1.signs_ref), custom_call_target="tpu_custom_call" | custom-call | flops 1100000000 | bytes 1000000 | tf_op jit(solution)/shard_map/panel_part/pallas_call | solution.py:107
  4.4 0.5 %collective-permute-start = (f32[64,512]{1,0:T(8,128)S(1)}, f32[64,512]{1,0:T(8,128)S(1)}, u32[]{:S(2)}, u32[]{:S(2)}) collective-permute-start(f32[64,512]{1,0:T(8,128)S(1)} %get-tuple-element.26), channel_id=1, source_target_pairs={{0,4},{4,0},{8,12},{12,8},{1,5},{5,1},{9,13},{13,9},{2,6},{6,2},{1... | collective-permute-start | bytes 393224 | tf_op jit(solution)/shard_map/ppermute | solution.py:529
  4.9 1.0 %collective-permute-done = f32[64,512]{1,0:T(8,128)S(1)} collective-permute-done((f32[64,512]{1,0:T(8,128)S(1)}, f32[64,512]{1,0:T(8,128)S(1)}, u32[]{:S(2)}, u32[]{:S(2)}) %collective-permute-start) | collective-permute-done | bytes 131104 | tf_op jit(solution)/shard_map/ppermute | solution.py:529
  5.9 2.9 %collective-permute-start.1 = (f32[64,512]{1,0:T(8,128)S(1)}, f32[64,512]{1,0:T(8,128)S(1)}, u32[]{:S(2)}, u32[]{:S(2)}) collective-permute-start(f32[64,512]{1,0:T(8,128)S(1)} %add.6._), channel_id=1, source_target_pairs={{0,8},{4,12},{8,0},{12,4},{1,9},{5,13},{9,1},{13,5},{2,10},{6,14},... | collective-permute-start | bytes 393224 | tf_op jit(solution)/shard_map/ppermute | solution.py:529
  8.9 3.8 %blocks_part.1 = (f32[128,512]{1,0:T(8,128)S(1)}, f32[128,512]{1,0:T(8,128)S(1)}) custom-call(s32[1,1]{1,0:T(1,128)} %bitcast.4.seed_ref, bf16[128,2048]{1,0:T(8,128)(2,1)S(1)} %get-tuple-element.27.chosen_ref, f32[64,512]{1,0:T(8,128)S(1)} %add.6._), custom_call_target="tpu_custom_call" | custom-call | flops 4400000000 | bytes 1000000 | tf_op jit(solution)/shard_map/blocks_part/pallas_call | solution.py:123
  12.7 0.0 collective-permute-done.1
  12.8 1.7 %collective-permute-start.2 = (bf16[64,512]{1,0:T(8,128)(2,1)S(1)}, bf16[64,512]{1,0:T(8,128)(2,1)S(1)}, u32[]{:S(2)}, u32[]{:S(2)}) collective-permute-start(bf16[64,512]{1,0:T(8,128)(2,1)S(1)} %get-tuple-element.48.refs_0_.refs_8_), channel_id=1, source_target_pairs={{0,16},{16,0},{1,17},{17,1},{2,18},{18,2},{3,19},{19,3},{4,20},{20... | collective-permute-start | bytes 196616 | tf_op jit(solution)/shard_map/ppermute | solution.py:529
  14.5 2.3 %other_parts.1 = (f32[64,2560]{1,0:T(8,128)S(1)}, f32[64,2560]{1,0:T(8,128)S(1)}) custom-call(s32[1,1]{1,0:T(1,128)} %bitcast.5.seed_ref, bf16[128,2048]{1,0:T(8,128)(2,1)S(1)} %get-tuple-element.27.chosen_ref, f32[64,512]{1,0:T(8,128)S(1)} %get-tuple-element.49._, f32[128,512]{1,0:T(8,128)S(1)} %get-tuple-element.28.refs_0_, ...), custom_call_target="tpu_custom_call" | custom-call | flops 2200000000 | bytes 1000000 | tf_op jit(solution)/shard_map/other_parts/pallas_call | solution.py:169
  16.8 0.3 collective-permute-done.2.refs_1_.refs_9_
  17.1 0.0 collective-permute-start.5
  17.1 0.5 %collective-permute-start.3 = (bf16[64,512]{1,0:T(8,128)(2,1)S(1)}, bf16[64,512]{1,0:T(8,128)(2,1)S(1)}, u32[]{:S(2)}, u32[]{:S(2)}) collective-permute-start(bf16[64,512]{1,0:T(8,128)(2,1)S(1)} %get-tuple-element.48.refs_0_.refs_8_), channel_id=1, source_target_pairs={{0,4},{4,0},{8,12},{12,8},{1,5},{5,1},{9,13},{13,9},{2,6},{6,2},{1... | collective-permute-start | bytes 196616 | tf_op jit(solution)/shard_map/ppermute | solution.py:529
  17.6 0.0 collective-permute-start.4
  18.3 0.9 %collective-permute-done.5.right_ref = f32[64,2560]{1,0:T(8,128)S(1)} collective-permute-done((f32[64,2560]{1,0:T(8,128)S(1)}, f32[64,2560]{1,0:T(8,128)S(1)}, u32[]{:S(2)}, u32[]{:S(2)}) %collective-permute-start.5) | collective-permute-done | bytes 655392 | tf_op jit(solution)/shard_map/ppermute | solution.py:529
  19.2 0.1 last_sent.1
  19.3 1.8 %collective-permute-start.6 = (f32[64,1280]{1,0:T(8,128)S(1)}, f32[64,1280]{1,0:T(8,128)S(1)}, u32[]{:S(2)}, u32[]{:S(2)}) collective-permute-start(f32[64,1280]{1,0:T(8,128)S(1)} %last_sent.1), channel_id=1, source_target_pairs={{0,8},{4,12},{8,0},{12,4},{1,9},{5,13},{9,1},{13,5},{2,10},{6,14},... | collective-permute-start | bytes 983048 | tf_op jit(solution)/shard_map/ppermute | solution.py:529
  21.0 0.0 collective-permute-done.3.refs_2_.refs_10_
  21.0 0.0 collective-permute-done.4.refs_3_.refs_11_
  21.0 6.4 %gram_first_blocks.1 = (f32[128,512]{1,0:T(8,128)S(1)}, f32[128,384]{1,0:T(8,128)S(1)}, f32[256,128]{1,0:T(8,128)S(1)}, f32[256,128]{1,0:T(8,128)S(1)}, f32[256,256]{1,0:T(8,128)S(1)}, /*index=5*/f32[256,256]{1,0:T(8,128)S(1)}) custom-call(f32[1,1]{1,0:T(1,128)} %bitcast.6.ridge_ref, bf16[64,512]{1,0:T(8,128)(2,1)S(1)} %get-tuple-element.48.refs_0_.refs_8_, ...), custom_call_target="tpu_custom_call" | custom-call | flops 3849999872 | bytes 1000000 | tf_op jit(solution)/shard_map/gram_first_blocks/pallas_call | solution.py:436
  27.5 1.6 %collective-permute-done.6.came_ref = f32[64,1280]{1,0:T(8,128)S(1)} collective-permute-done((f32[64,1280]{1,0:T(8,128)S(1)}, f32[64,1280]{1,0:T(8,128)S(1)}, u32[]{:S(2)}, u32[]{:S(2)}) %collective-permute-start.6) | collective-permute-done | bytes 327712 | tf_op jit(solution)/shard_map/ppermute | solution.py:529
  29.1 0.1 pieces.1
  29.2 1.7 %collective-permute-start.7 = (bf16[64,1280]{1,0:T(8,128)(2,1)S(1)}, bf16[64,1280]{1,0:T(8,128)(2,1)S(1)}, u32[]{:S(2)}, u32[]{:S(2)}) collective-permute-start(bf16[64,1280]{1,0:T(8,128)(2,1)S(1)} %get-tuple-element.47), channel_id=1, source_target_pairs={{0,16},{16,0},{1,17},{17,1},{2,18},{18,2},{3,19},{19,3},{4,20},{20... | collective-permute-start | bytes 491528 | tf_op jit(solution)/shard_map/ppermute | solution.py:529
  30.9 3.1 %eliminate_blocks.2 = (f32[128,256]{1,0:T(8,128)S(1)}, f32[256,128]{1,0:T(8,128)S(1)}, f32[128,128]{1,0:T(8,128)S(1)}, f32[256,128]{1,0:T(8,128)S(1)}) custom-call(f32[256,256]{1,0:T(8,128)S(1)} %get-tuple-element.34.gram_ref, f32[256,256]{1,0:T(8,128)S(1)} %get-tuple-element.35.turned_ref), custom_call_target="tpu_custom_call" | custom-call | flops 4400000000 | bytes 1000000 | tf_op jit(solution)/shard_map/eliminate_blocks/pallas_call | solution.py:448
  34.0 0.1 collective-permute-start.8
  34.1 0.6 %collective-permute-done.7.refs_13_ = bf16[64,1280]{1,0:T(8,128)(2,1)S(1)} collective-permute-done((bf16[64,1280]{1,0:T(8,128)(2,1)S(1)}, bf16[64,1280]{1,0:T(8,128)(2,1)S(1)}, u32[]{:S(2)}, u32[]{:S(2)}) %collective-permute-start.7) | collective-permute-done | bytes 163872 | tf_op jit(solution)/shard_map/ppermute | solution.py:529
  34.7 0.0 collective-permute-start.9
  34.7 2.8 %eliminate_blocks.3 = (f32[128,128]{1,0:T(8,128)S(1)}, f32[256,128]{1,0:T(8,128)S(1)}) custom-call(f32[128,128]{1,0:T(8,128)S(1)} %get-tuple-element.37.gram_ref, f32[256,128]{1,0:T(8,128)S(1)} %get-tuple-element.38.turned_ref), custom_call_target="tpu_custom_call" | custom-call | flops 4400000000 | bytes 1000000 | tf_op jit(solution)/shard_map/eliminate_blocks/pallas_call | solution.py:448
  37.5 0.0 collective-permute-done.8.refs_14_
  37.5 0.0 collective-permute-done.9.refs_15_
  37.5 3.2 %finish.1 = (f32[256,512]{1,0:T(8,128)}, f32[256,512]{1,0:T(8,128)}) custom-call(f32[1,1]{1,0:T(1,128)} %bitcast.7.ridge_ref, f32[128,512]{1,0:T(8,128)S(1)} %get-tuple-element.32.refs_0_, f32[128,384]{1,0:T(8,128)S(1)} %get-tuple-element.33.refs_1_, f32[128,256]{1,0:T(8,128)S(1)} %get-tuple-element.36.refs_2_, f32[128,128]{1,0:T(8,128)S(1)} %get-tuple-element.39.refs_3_, ...), custom_call_target="tpu_custom_call" | custom-call | flops 3300000000 | bytes 1000000 | tf_op jit(solution)/shard_map/finish/pallas_call | solution.py:517
  (2 shorter events, 0.0 us)
Async XLA Ops:
  1.3 2.5 %copy-start = (bf16[256,2048]{1,0:T(8,128)(2,1)S(1)}, bf16[256,2048]{1,0:T(8,128)(2,1)}, u32[]{:S(2)}) copy-start(bf16[256,2048]{1,0:T(8,128)(2,1)} %pool_ref.1) | copy-start | bytes 3145732
  1.3 2.5 %copy-start.1 = (s32[128]{0:T(128)S(1)}, s32[128]{0:T(128)}, u32[]{:S(2)}) copy-start(s32[128]{0:T(128)} %param.5) | copy-start | bytes 1540
  4.4 1.5 %collective-permute-start = (f32[64,512]{1,0:T(8,128)S(1)}, f32[64,512]{1,0:T(8,128)S(1)}, u32[]{:S(2)}, u32[]{:S(2)}) collective-permute-start(f32[64,512]{1,0:T(8,128)S(1)} %get-tuple-element.26), channel_id=1, source_target_pairs={{0,4},{4,0},{8,12},{12,8},{1,5},{5,1},{9,13},{13,9},{2,6},{6,2},{1... | collective-permute-start | bytes 393224 | tf_op jit(solution)/shard_map/ppermute | solution.py:529
  5.9 6.8 %collective-permute-start.1 = (f32[64,512]{1,0:T(8,128)S(1)}, f32[64,512]{1,0:T(8,128)S(1)}, u32[]{:S(2)}, u32[]{:S(2)}) collective-permute-start(f32[64,512]{1,0:T(8,128)S(1)} %add.6._), channel_id=1, source_target_pairs={{0,8},{4,12},{8,0},{12,4},{1,9},{5,13},{9,1},{13,5},{2,10},{6,14},... | collective-permute-start | bytes 393224 | tf_op jit(solution)/shard_map/ppermute | solution.py:529
  12.8 4.3 %collective-permute-start.2 = (bf16[64,512]{1,0:T(8,128)(2,1)S(1)}, bf16[64,512]{1,0:T(8,128)(2,1)S(1)}, u32[]{:S(2)}, u32[]{:S(2)}) collective-permute-start(bf16[64,512]{1,0:T(8,128)(2,1)S(1)} %get-tuple-element.48.refs_0_.refs_8_), channel_id=1, source_target_pairs={{0,16},{16,0},{1,17},{17,1},{2,18},{18,2},{3,19},{19,3},{4,20},{20... | collective-permute-start | bytes 196616 | tf_op jit(solution)/shard_map/ppermute | solution.py:529
  17.1 2.1 %collective-permute-start.5 = (f32[64,2560]{1,0:T(8,128)S(1)}, f32[64,2560]{1,0:T(8,128)S(1)}, u32[]{:S(2)}, u32[]{:S(2)}) collective-permute-start(f32[64,2560]{1,0:T(8,128)S(1)} %get-tuple-element.45), channel_id=1, source_target_pairs={{0,4},{4,0},{8,12},{12,8},{1,5},{5,1},{9,13},{13,9},{2,6},{6,2},{1... | collective-permute-start | bytes 1966088 | tf_op jit(solution)/shard_map/ppermute | solution.py:529
  17.1 3.9 %collective-permute-start.3 = (bf16[64,512]{1,0:T(8,128)(2,1)S(1)}, bf16[64,512]{1,0:T(8,128)(2,1)S(1)}, u32[]{:S(2)}, u32[]{:S(2)}) collective-permute-start(bf16[64,512]{1,0:T(8,128)(2,1)S(1)} %get-tuple-element.48.refs_0_.refs_8_), channel_id=1, source_target_pairs={{0,4},{4,0},{8,12},{12,8},{1,5},{5,1},{9,13},{13,9},{2,6},{6,2},{1... | collective-permute-start | bytes 196616 | tf_op jit(solution)/shard_map/ppermute | solution.py:529
  17.6 3.4 %collective-permute-start.4 = (bf16[64,512]{1,0:T(8,128)(2,1)S(1)}, bf16[64,512]{1,0:T(8,128)(2,1)S(1)}, u32[]{:S(2)}, u32[]{:S(2)}) collective-permute-start(bf16[64,512]{1,0:T(8,128)(2,1)S(1)} %collective-permute-done.2.refs_1_.refs_9_), channel_id=1, source_target_pairs={{0,4},{4,0},{8,12},{12,8},{1,5},{5,1},{9,13},{13,9},{2,6},{6,2},{1... | collective-permute-start | bytes 196616 | tf_op jit(solution)/shard_map/ppermute | solution.py:529
  19.3 9.8 %collective-permute-start.6 = (f32[64,1280]{1,0:T(8,128)S(1)}, f32[64,1280]{1,0:T(8,128)S(1)}, u32[]{:S(2)}, u32[]{:S(2)}) collective-permute-start(f32[64,1280]{1,0:T(8,128)S(1)} %last_sent.1), channel_id=1, source_target_pairs={{0,8},{4,12},{8,0},{12,4},{1,9},{5,13},{9,1},{13,5},{2,10},{6,14},... | collective-permute-start | bytes 983048 | tf_op jit(solution)/shard_map/ppermute | solution.py:529
  29.2 5.5 %collective-permute-start.7 = (bf16[64,1280]{1,0:T(8,128)(2,1)S(1)}, bf16[64,1280]{1,0:T(8,128)(2,1)S(1)}, u32[]{:S(2)}, u32[]{:S(2)}) collective-permute-start(bf16[64,1280]{1,0:T(8,128)(2,1)S(1)} %get-tuple-element.47), channel_id=1, source_target_pairs={{0,16},{16,0},{1,17},{17,1},{2,18},{18,2},{3,19},{19,3},{4,20},{20... | collective-permute-start | bytes 491528 | tf_op jit(solution)/shard_map/ppermute | solution.py:529
  34.0 3.5 %collective-permute-start.8 = (bf16[64,1280]{1,0:T(8,128)(2,1)S(1)}, bf16[64,1280]{1,0:T(8,128)(2,1)S(1)}, u32[]{:S(2)}, u32[]{:S(2)}) collective-permute-start(bf16[64,1280]{1,0:T(8,128)(2,1)S(1)} %get-tuple-element.46.refs_12_), channel_id=1, source_target_pairs={{0,4},{4,0},{8,12},{12,8},{1,5},{5,1},{9,13},{13,9},{2,6},{6,2},{1... | collective-permute-start | bytes 491528 | tf_op jit(solution)/shard_map/ppermute | solution.py:529
  34.7 2.8 %collective-permute-start.9 = (bf16[64,1280]{1,0:T(8,128)(2,1)S(1)}, bf16[64,1280]{1,0:T(8,128)(2,1)S(1)}, u32[]{:S(2)}, u32[]{:S(2)}) collective-permute-start(bf16[64,1280]{1,0:T(8,128)(2,1)S(1)} %collective-permute-done.7.refs_13_), channel_id=1, source_target_pairs={{0,4},{4,0},{8,12},{12,8},{1,5},{5,1},{9,13},{13,9},{2,6},{6,2},{1... | collective-permute-start | bytes 491528 | tf_op jit(solution)/shard_map/ppermute | solution.py:529

commit v6 on v5

--- a/solution.py
+++ b/solution.py
@@ -357,20 +357,30 @@
     return lax.broadcasted_iota(jnp.int32, shape, 0) == lax.broadcasted_iota(jnp.int32, shape, 1)
 
 
-def factor_block(block):
+def factor_start(block):
     unit = identity_mask(block.shape).astype(jnp.float32)
-    rows_u = [block[8 * v : 8 * v + 8] for v in range(BLOCK // 8)]
-    rows_z = [unit[8 * v : 8 * v + 8] for v in range(BLOCK // 8)]
+    return factor_step(block, unit, 0)
+
+
+def factor_step(rest_u, rest_z, offset):
     groups = STRIPE // 8
-    done = []
-    for end in range(STRIPE, BLOCK + 1, STRIPE):
-        upper, inverse = factor_stripe(rows_u[:groups], rows_z[:groups], end - STRIPE)
-        done += inverse
-        if end < BLOCK:
-            upper, inverse = jnp.concatenate(upper, axis=0), jnp.concatenate(inverse, axis=0)
-            update = exact_dot(upper, jnp.concatenate([upper, inverse], axis=1), (0, 0))[end:]
-            rows_u = [row - update[8 * v : 8 * v + 8, :BLOCK] for v, row in enumerate(rows_u[groups:])]
-            rows_z = [row - update[8 * v : 8 * v + 8, BLOCK:] for v, row in enumerate(rows_z[groups:])]
+    upper, inverse = factor_stripe(
+        [rest_u[8 * v : 8 * v + 8] for v in range(groups)],
+        [rest_z[8 * v : 8 * v + 8] for v in range(groups)],
+        offset,
+    )
+    upper, inverse = jnp.concatenate(upper, axis=0), jnp.concatenate(inverse, axis=0)
+    if offset + STRIPE == BLOCK:
+        return inverse, None, None
+    update = exact_dot(upper, jnp.concatenate([upper, inverse], axis=1), (0, 0))[offset + STRIPE :]
+    return inverse, rest_u[STRIPE:] - update[:, :BLOCK], rest_z[STRIPE:] - update[:, BLOCK:]
+
+
+def factor_end(inverse, rest_u, rest_z):
+    done = [inverse]
+    for offset in range(STRIPE, BLOCK, STRIPE):
+        inverse, rest_u, rest_z = factor_step(rest_u, rest_z, offset)
+        done.append(inverse)
     return jnp.concatenate(done, axis=0)
 
 
@@ -381,12 +391,14 @@
     return join([jnp.where(even, mine, other), jnp.where(even, other, mine)], 0)
 
 
-def eliminate(gram, turned, upper_refs, done_refs, rest_refs):
+def eliminate(gram, turned, upper_refs, done_refs, rest_refs, started=None):
     square = (BLOCK, BLOCK)
     keep = lax.broadcasted_iota(jnp.int32, square, 0) <= lax.broadcasted_iota(jnp.int32, square, 1)
     block = gram[:BLOCK, :BLOCK]
     for index, (upper_ref, done_ref) in enumerate(zip(upper_refs, done_refs)):
-        inverse = factor_block(block)
+        if index > 0 or started is None:
+            started = factor_start(block)
+        inverse = factor_end(*started)
         if index + 1 < len(upper_refs):
             beside = exact_dot(inverse, gram[:BLOCK, BLOCK : 2 * BLOCK])
             ahead = gram[BLOCK : 2 * BLOCK, BLOCK : 2 * BLOCK] - exact_dot(beside, beside, (0, 0))
@@ -415,8 +427,14 @@
     )
 
 
-def next_blocks_kernel(blocks, gram_ref, turned_ref, *refs):
-    eliminate(gram_ref[...], turned_ref[...], refs[:blocks], refs[blocks : 2 * blocks], refs[2 * blocks :])
+def start_block_kernel(block_ref, *out_refs):
+    for ref, value in zip(out_refs, factor_start(block_ref[:BLOCK, :BLOCK])):
+        ref[...] = value
+
+
+def last_blocks_kernel(blocks, gram_ref, turned_ref, inverse_ref, rest_u_ref, rest_z_ref, *refs):
+    started = (inverse_ref[...], rest_u_ref[...], rest_z_ref[...])
+    eliminate(gram_ref[...], turned_ref[...], refs[:blocks], refs[blocks:], (), started)
 
 
 def block_shapes(width, examples, blocks):
@@ -443,84 +461,132 @@
     return taken_apart(results, blocks)
 
 
-def next_blocks(rest, blocks):
+def start_block(gram):
+    shapes = [(STRIPE, BLOCK), (BLOCK - STRIPE, BLOCK), (BLOCK - STRIPE, BLOCK)]
+    return call(
+        start_block_kernel, [(shape, jnp.float32) for shape in shapes], [VMEM], 1.5, "start_block"
+    )(gram)
+
+
+def last_blocks(rest, started):
     gram, turned = rest
+    blocks = gram.shape[0] // BLOCK
     results = call(
-        functools.partial(next_blocks_kernel, blocks),
+        functools.partial(last_blocks_kernel, blocks),
         block_shapes(gram.shape[0], turned.shape[0], blocks),
-        [VMEM, VMEM],
-        4 * blocks,
-        "eliminate_blocks",
-    )(gram, turned)
+        [VMEM] * (2 + len(started)),
+        4.5,
+        "last_blocks",
+    )(gram, turned, *started)
     return taken_apart(results, blocks)
 
 
-def finish_kernel(blocks, count, blk_count, ridge_ref, *refs):
+def assembled_columns(refs, height, width):
+    return join([ref[:, start : start + width] for start in (height, height + width) for ref in refs], 0)
+
+
+def lower(uppers, row, lane):
+    if row < lane:
+        return jnp.zeros((BLOCK, BLOCK), jnp.float32)
+    return uppers[lane // BLOCK][:, row - lane : row - lane + BLOCK].T
+
+
+def put_lower(uppers, ref, first):
+    for row in range(0, ref.shape[0], BLOCK):
+        for lane in range(0, ref.shape[1], BLOCK):
+            ref[row : row + BLOCK, lane : lane + BLOCK] = lower(uppers, first + row, lane)
+
+
+def solve(features, parts_ref):
+    turned = features.T
+    product = jnp.dot(join([turned] * 3, 1), parts_ref[...], preferred_element_type=jnp.float32)
+    return turned, product * (1.0 / features.shape[0])
+
+
+def column_kernel(blocks, count, height, *refs):
     uppers, dones = refs[:blocks], refs[blocks : 2 * blocks]
-    phi_refs, piece_refs = refs[2 * blocks : 2 * blocks + count], refs[2 * blocks + count : -3]
-    panel_ref, trailing_ref, solved_ref = refs[-3:]
+    phi_refs, mine = refs[2 * blocks : 2 * blocks + count], refs[2 * blocks + count : -6]
+    columns_ref, parts_ref, *third_refs, solved_ref = refs[-6:]
+    width = columns_ref.shape[1]
+    column_block = lax.axis_index("tp")
+    phi = in_pair_order(even_of_pair(), phi_refs)
+    columns = jnp.where(column_block == 0, phi, assembled_columns(mine, height, width))
+    columns_ref[...] = columns
+    parts_ref[...] = join(list(thirds(join([ref[...] for ref in dones], 1))), 0)
+    solved_ref[...] = solve(columns, parts_ref)[1]
+    pl.when(column_block == 0)(functools.partial(put_lower, uppers, solved_ref, 0))
+    for ref, part in zip(third_refs, thirds(solved_ref[...])):
+        ref[...] = part
+
+
+def columns_solved(uppers, dones, phi, mine, height, width):
+    panel, examples = uppers[0].shape[1], sum(part.shape[0] for part in phi)
+    operands = [*uppers, *dones, *phi, *mine]
+    shapes = [(examples, width), (3 * examples, panel)] + [(width, panel)] * 3
+    return call(
+        functools.partial(column_kernel, len(uppers), len(phi), height),
+        [(shape, jnp.bfloat16) for shape in shapes],
+        [VMEM] * len(operands),
+        1,
+        "columns_solved",
+        [pltpu.VMEM((width, panel), jnp.float32)],
+        vmem=24,
+    )(*operands)
+
+
+def finish_kernel(blocks, count, blk_count, ridge_ref, columns_ref, parts_ref, *refs):
+    solved, refs = [ref[...] for ref in refs[:3]], refs[3:]
+    uppers = refs[:blocks]
+    phi_refs, piece_refs = refs[blocks : blocks + count], refs[blocks + count : -2]
+    panel_ref, trailing_ref = refs[-2:]
     height, panel = panel_ref.shape
     width = trailing_ref.shape[1]
     even = even_of_pair()
     ex_index, column_block, blk_index = (lax.axis_index(axis) for axis in ("ex", "tp", "blk"))
     row_group = ex_index * blk_count + blk_index
     phi = in_pair_order(even, phi_refs)
-    examples = phi.shape[0]
-    mine, others = piece_refs[: count // 2], piece_refs[count // 2 :]
-    columns, pair_columns = (
-        join([ref[:, start : start + width] for start in (height, height + width) for ref in some], 0)
-        for some in (mine, others)
-    )
     rows = in_pair_order(even, piece_refs, slice(0, height))
+    columns = columns_ref[...]
+    pair_columns = assembled_columns(piece_refs[count // 2 :], height, width)
     groups = width // height
-    holder = blk_index // groups
-    held = jnp.where(holder == column_block % 2, columns, pair_columns)
+    held = jnp.where(blk_index // groups == column_block % 2, columns, pair_columns)
     for place in range(groups):
         inside = (ex_index == column_block // 2) & (blk_index % groups == place)
         rows = jnp.where(inside, held[:, place * height : (place + 1) * height], rows)
     for start in range(0, panel, height):
         rows = jnp.where(row_group * height == start, phi[:, start : start + height], rows)
-    columns = jnp.where(column_block == 0, phi, columns)
-    turned = jnp.concatenate([rows, columns], axis=1).T
-    parts = join(list(thirds(join([ref[...] for ref in dones], 1))), 0)
-    scale = 1.0 / examples
-    solved = jnp.dot(join([turned] * 3, 1), parts, preferred_element_type=jnp.float32) * scale
-    panel_ref[...] = solved[:height]
-    solved_ref[...] = solved[height:]
-
-    def lower(row, lane):
-        if row < lane:
-            return jnp.zeros((BLOCK, BLOCK), jnp.float32)
-        return uppers[lane // BLOCK][:, row - lane : row - lane + BLOCK].T
-
-    def put(ref, first):
-        for row in range(0, ref.shape[0], BLOCK):
-            for lane in range(0, panel, BLOCK):
-                ref[row : row + BLOCK, lane : lane + BLOCK] = lower(first + row, lane)
-
-    pl.when(column_block == 0)(functools.partial(put, solved_ref, 0))
+    turned, panel_ref[...] = solve(rows, parts_ref)
     for group in range(panel // height):
-        pl.when(row_group == group)(functools.partial(put, panel_ref, group * height))
+        pl.when(row_group == group)(functools.partial(put_lower, uppers, panel_ref, group * height))
     shape = (height, width)
     diagonal = row_group * height + lax.broadcasted_iota(
         jnp.int32, shape, 0
     ) == column_block * width + lax.broadcasted_iota(jnp.int32, shape, 1)
-    gram = jnp.dot(turned[:height], columns, preferred_element_type=jnp.float32) * scale
-    trailing_ref[...] = (
-        gram + jnp.where(diagonal, ridge_ref[...], 0.0) - exact_dot(panel_ref[...], solved_ref[...], (1, 1))
-    )
+    gram = jnp.dot(turned, columns, preferred_element_type=jnp.float32) * (1.0 / columns.shape[0])
+    total = gram + jnp.where(diagonal, ridge_ref[...], 0.0)
+    for left, right in zip(*term_parts(thirds(panel_ref[...]), solved)):
+        total = total - lax.dot_general(
+            left, right, (((1,), (1,)), ((), ())), preferred_element_type=jnp.float32
+        )
+    trailing_ref[...] = total
+
+
+def term_parts(left_parts, right_parts):
+    terms = ((0, 0), (0, 1), (1, 0), (0, 2), (2, 0), (1, 1))
+    return [left_parts[i] for i, _ in terms], [right_parts[j] for _, j in terms]
 
 
 def finish(ridge, uppers, dones, phi, gathered, height, width, blk_count):
     panel = uppers[0].shape[1]
-    operands = [*uppers, *dones, *phi, *gathered]
+    mine = gathered[: len(gathered) // 2]
+    solved = columns_solved(uppers, dones, phi, mine, height, width)
+    operands = [*solved, *uppers, *phi, *gathered]
     return call(
         functools.partial(finish_kernel, len(uppers), len(phi), blk_count),
         [((height, panel), jnp.float32), ((height, width), jnp.float32)],
         [VMEM] * (1 + len(operands)),
-        3,
+        2,
         "finish",
-        [pltpu.VMEM((width, panel), jnp.float32)],
         vmem=24,
     )(ridge, *operands)
 
@@ -569,11 +635,15 @@
     phi = with_pair(phi)
     half = PANEL // BLOCK // 2
     uppers, dones, rest = first_blocks(ridge, phi, half)
-    gathered = pieces(left, right, came, ex_count, scaling, dones[-1])
-    gathered = with_pair(ex_parts(gathered))
-    while rest:
-        more_uppers, more_dones, rest = next_blocks(rest, 1)
-        uppers, dones = uppers + more_uppers, dones + more_dones
+    started = start_block(rest[0])
+    gathered = pieces(left, right, came, ex_count, scaling, started[0])
+    other = swapped(gathered[0], "tp", 1)
+    gathered = ex_parts(gathered)
+    started, other = lax.optimization_barrier((started, other))
+    more_uppers, more_dones, _ = last_blocks(rest, started)
+    gathered[1:], more_dones = lax.optimization_barrier((gathered[1:], more_dones))
+    gathered = [*gathered, other, *(swapped(part, "tp", 1) for part in gathered[1:])]
+    uppers, dones = uppers + more_uppers, dones + more_dones
     return tuple(finish(ridge, uppers, dones, phi, gathered, HALF, column_width, blk_count))
 
 

time: 40.8 us -> 40 us (0.980)
  waiting for transfers between devices: 4.44 us -> 3.16 us
    ppermute x10, waiting for transfers between devices: 4.44 us -> 3.16 us  [swapped(): lax.ppermute(value, axis, [(s, s ^ bit) for s in range(lax.axis_size(axis...]
    pallas_call x2 -> x3, Pallas kernels: 5.89 us -> 6.95 us  [the longest x1 4.47 us: last_blocks(): call(functools.partial(last_blocks_kernel, blocks), block_shapes(gram.sha...]
    pallas_call x1, Pallas kernels: 3.19 us -> 2.58 us  [finish(): call(functools.partial(finish_kernel, len(uppers), len(phi), blk_count),...]
  transfers between devices with their start and end apart: 10 -> 10, of which waited for: 5 -> 6; matrix products, arithmetic and copies ran while one was open for 0% -> 0% of each run, Pallas kernels for 46% -> 49%
where the time goes in v6:
time: 40 us; the launch traced here: 39.8 us
  Pallas kernels  25.3 us (63%)
  starting transfers between devices  9.23 us (23%)
  waiting for transfers between devices  3.16 us (8%)
  between operations  2.06 us (5%)
    ppermute x10, starting transfers between devices, swapped(): lax.ppermute(value, axis, [(s, s ^ bit) for s in range(lax.axis_size(axis...  9.23 us
    pallas_call x1, Pallas kernels, first_blocks(): call(functools.partial(first_blocks_kernel, blocks, len(phi)), block_shap...  6.43 us
    pallas_call x1, Pallas kernels, last_blocks(): call(functools.partial(last_blocks_kernel, blocks), block_shapes(gram.sha...  4.47 us
    pallas_call x1, Pallas kernels, blocks_part(): call(functools.partial(blocks_part_kernel, blocks), [((chosen.shape[0], w...  3.84 us
    ppermute x10, waiting for transfers between devices, swapped(): lax.ppermute(value, axis, [(s, s ^ bit) for s in range(lax.axis_size(axis...  3.16 us
    pallas_call x1, Pallas kernels, finish(): call(functools.partial(finish_kernel, len(uppers), len(phi), blk_count),...  2.58 us
    pallas_call x1, Pallas kernels, panel_signs(): call(panel_signs_kernel, [((coordinates, PANEL), jnp.bfloat16)], [VMEM],...  2.46 us
    pallas_call x1, Pallas kernels, other_parts(): call(functools.partial(other_parts_kernel, tp_count, blk_count), [((rows...  2.32 us
  transfers between devices with their start and end apart: 10, of which 6 were waited for; matrix products, arithmetic and copies ran while one was open for 0% of the time, Pallas kernels for 49%

profile of v6, /device:TPU:0, one launch (start us, length us, event | category | flops | bytes accessed | tf_op | source)
XLA Modules:
  0.0 39.8 jit_solution(7736462394784936400)
XLA Ops:
  1.3 0.0 copy-start
  1.3 0.0 copy-start.1
  1.3 2.5 %panel_signs.1.signs_ref = bf16[2048,512]{1,0:T(8,128)(2,1)S(1)} custom-call(s32[1,1]{1,0:T(1,128)} %bitcast.3.seed_ref), custom_call_target="tpu_custom_call" | custom-call | flops 2200000000 | bytes 1000000 | tf_op jit(solution)/shard_map/panel_signs/pallas_call | solution.py:88
  3.8 0.0 copy-done
  3.8 0.0 copy-done.1
  3.8 0.6 %panel_part.1 = (f32[64,512]{1,0:T(8,128)S(1)}, f32[64,512]{1,0:T(8,128)S(1)}, bf16[128,2048]{1,0:T(8,128)(2,1)S(1)}) custom-call(s32[1,128]{1,0:T(1,128)S(1)} %bitcast.8, bf16[256,2048]{1,0:T(8,128)(2,1)S(1)} %copy-done, bf16[2048,512]{1,0:T(8,128)(2,1)S(1)} %panel_signs.1.signs_ref), custom_call_target="tpu_custom_call" | custom-call | flops 1100000000 | bytes 1000000 | tf_op jit(solution)/shard_map/panel_part/pallas_call | solution.py:107
  4.4 0.5 %collective-permute-start = (f32[64,512]{1,0:T(8,128)S(1)}, f32[64,512]{1,0:T(8,128)S(1)}, u32[]{:S(2)}, u32[]{:S(2)}) collective-permute-start(f32[64,512]{1,0:T(8,128)S(1)} %get-tuple-element.39), channel_id=1, source_target_pairs={{0,4},{4,0},{8,12},{12,8},{1,5},{5,1},{9,13},{13,9},{2,6},{6,2},{1... | collective-permute-start | bytes 393224 | tf_op jit(solution)/shard_map/ppermute | solution.py:595
  4.9 1.0 %collective-permute-done = f32[64,512]{1,0:T(8,128)S(1)} collective-permute-done((f32[64,512]{1,0:T(8,128)S(1)}, f32[64,512]{1,0:T(8,128)S(1)}, u32[]{:S(2)}, u32[]{:S(2)}) %collective-permute-start) | collective-permute-done | bytes 131104 | tf_op jit(solution)/shard_map/ppermute | solution.py:595
  5.9 2.9 %collective-permute-start.1 = (f32[64,512]{1,0:T(8,128)S(1)}, f32[64,512]{1,0:T(8,128)S(1)}, u32[]{:S(2)}, u32[]{:S(2)}) collective-permute-start(f32[64,512]{1,0:T(8,128)S(1)} %add.6._), channel_id=1, source_target_pairs={{0,8},{4,12},{8,0},{12,4},{1,9},{5,13},{9,1},{13,5},{2,10},{6,14},... | collective-permute-start | bytes 393224 | tf_op jit(solution)/shard_map/ppermute | solution.py:595
  8.9 3.8 %blocks_part.1 = (f32[128,512]{1,0:T(8,128)S(1)}, f32[128,512]{1,0:T(8,128)S(1)}) custom-call(s32[1,1]{1,0:T(1,128)} %bitcast.4.seed_ref, bf16[128,2048]{1,0:T(8,128)(2,1)S(1)} %get-tuple-element.40.chosen_ref, f32[64,512]{1,0:T(8,128)S(1)} %add.6._), custom_call_target="tpu_custom_call" | custom-call | flops 4400000000 | bytes 1000000 | tf_op jit(solution)/shard_map/blocks_part/pallas_call | solution.py:123
  12.7 0.0 collective-permute-done.1
  12.8 1.7 %collective-permute-start.2 = (bf16[64,512]{1,0:T(8,128)(2,1)S(1)}, bf16[64,512]{1,0:T(8,128)(2,1)S(1)}, u32[]{:S(2)}, u32[]{:S(2)}) collective-permute-start(bf16[64,512]{1,0:T(8,128)(2,1)S(1)} %get-tuple-element.74.refs_0_.refs_8_.refs_7_), channel_id=1, source_target_pairs={{0,16},{16,0},{1,17},{17,1},{2,18},{18,2},{3,19},{19,3},{4,20},{20... | collective-permute-start | bytes 196616 | tf_op jit(solution)/shard_map/ppermute | solution.py:595
  14.5 2.3 %other_parts.1 = (f32[64,2560]{1,0:T(8,128)S(1)}, f32[64,2560]{1,0:T(8,128)S(1)}) custom-call(s32[1,1]{1,0:T(1,128)} %bitcast.5.seed_ref, bf16[128,2048]{1,0:T(8,128)(2,1)S(1)} %get-tuple-element.40.chosen_ref, f32[64,512]{1,0:T(8,128)S(1)} %get-tuple-element.75._, f32[128,512]{1,0:T(8,128)S(1)} %get-tuple-element.41.refs_0_, ...), custom_call_target="tpu_custom_call" | custom-call | flops 2200000000 | bytes 1000000 | tf_op jit(solution)/shard_map/other_parts/pallas_call | solution.py:169
  16.8 0.3 collective-permute-done.2.refs_1_.refs_9_.refs_8_
  17.1 0.0 collective-permute-start.5
  17.1 0.5 %collective-permute-start.3 = (bf16[64,512]{1,0:T(8,128)(2,1)S(1)}, bf16[64,512]{1,0:T(8,128)(2,1)S(1)}, u32[]{:S(2)}, u32[]{:S(2)}) collective-permute-start(bf16[64,512]{1,0:T(8,128)(2,1)S(1)} %get-tuple-element.74.refs_0_.refs_8_.refs_7_), channel_id=1, source_target_pairs={{0,4},{4,0},{8,12},{12,8},{1,5},{5,1},{9,13},{13,9},{2,6},{6,2},{1... | collective-permute-start | bytes 196616 | tf_op jit(solution)/shard_map/ppermute | solution.py:595
  17.6 0.0 collective-permute-start.4
  18.3 0.9 %collective-permute-done.5.right_ref = f32[64,2560]{1,0:T(8,128)S(1)} collective-permute-done((f32[64,2560]{1,0:T(8,128)S(1)}, f32[64,2560]{1,0:T(8,128)S(1)}, u32[]{:S(2)}, u32[]{:S(2)}) %collective-permute-start.5) | collective-permute-done | bytes 655392 | tf_op jit(solution)/shard_map/ppermute | solution.py:595
  19.2 0.1 last_sent.1
  19.3 1.8 %collective-permute-start.6 = (f32[64,1280]{1,0:T(8,128)S(1)}, f32[64,1280]{1,0:T(8,128)S(1)}, u32[]{:S(2)}, u32[]{:S(2)}) collective-permute-start(f32[64,1280]{1,0:T(8,128)S(1)} %last_sent.1), channel_id=1, source_target_pairs={{0,8},{4,12},{8,0},{12,4},{1,9},{5,13},{9,1},{13,5},{2,10},{6,14},... | collective-permute-start | bytes 983048 | tf_op jit(solution)/shard_map/ppermute | solution.py:595
  21.0 0.0 collective-permute-done.3.refs_2_.refs_10_.refs_9_
  21.0 0.0 collective-permute-done.4.refs_3_.refs_11_.refs_10_
  21.0 6.4 %gram_first_blocks.1 = (f32[128,512]{1,0:T(8,128)S(1)}, f32[128,384]{1,0:T(8,128)S(1)}, f32[256,128]{1,0:T(8,128)S(1)}, f32[256,128]{1,0:T(8,128)S(1)}, f32[256,256]{1,0:T(8,128)S(1)}, /*index=5*/f32[256,256]{1,0:T(8,128)S(1)}) custom-call(f32[1,1]{1,0:T(1,128)} %bitcast.6.ridge_ref, bf16[64,512]{1,0:T(8,128)(2,1)S(1)} %get-tuple-element.74.refs_0_.refs_8_.refs_7_, ...), custom_call_target="tpu_custom_call" | custom-call | flops 3849999872 | bytes 1000000 | tf_op jit(solution)/shard_map/gram_first_blocks/pallas_call | solution.py:454
  27.5 1.4 %start_block.1 = (f32[64,128]{1,0:T(8,128)S(1)}, f32[64,128]{1,0:T(8,128)S(1)}, f32[64,128]{1,0:T(8,128)S(1)}) custom-call(f32[256,256]{1,0:T(8,128)S(1)} %get-tuple-element.47.block_ref.gram_ref), custom_call_target="tpu_custom_call" | custom-call | flops 1650000000 | bytes 1000000 | tf_op jit(solution)/shard_map/start_block/pallas_call | solution.py:466
  28.8 0.3 collective-permute-done.6.came_ref
  29.1 0.1 pieces.1
  29.2 0.1 collective-permute-start.7
  29.3 1.7 %collective-permute-start.8 = (bf16[64,1280]{1,0:T(8,128)(2,1)S(1)}, bf16[64,1280]{1,0:T(8,128)(2,1)S(1)}, u32[]{:S(2)}, u32[]{:S(2)}) collective-permute-start(bf16[64,1280]{1,0:T(8,128)(2,1)S(1)} %get-tuple-element.62), channel_id=1, source_target_pairs={{0,16},{16,0},{1,17},{17,1},{2,18},{18,2},{3,19},{19,3},{4,20},{20... | collective-permute-start | bytes 491528 | tf_op jit(solution)/shard_map/ppermute | solution.py:595
  31.0 0.0 collective-permute-done.7.refs_13_
  31.0 4.5 %last_blocks.1 = (f32[128,256]{1,0:T(8,128)S(1)}, f32[128,128]{1,0:T(8,128)S(1)}, f32[256,128]{1,0:T(8,128)S(1)}, f32[256,128]{1,0:T(8,128)S(1)}) custom-call(f32[256,256]{1,0:T(8,128)S(1)} %get-tuple-element.47.block_ref.gram_ref, f32[256,256]{1,0:T(8,128)S(1)} %get-tuple-element.48.turned_ref, f32[64,128]{1,0:T(8,128)S(1)} %get-tuple-element.55._.inverse_ref, ...), custom_call_target="tpu_custom_call" | custom-call | flops 4950000128 | bytes 1000000 | tf_op jit(solution)/shard_map/last_blocks/pallas_call | solution.py:474
  35.4 0.4 %collective-permute-done.8.refs_13_.refs_12_ = bf16[64,1280]{1,0:T(8,128)(2,1)S(1)} collective-permute-done((bf16[64,1280]{1,0:T(8,128)(2,1)S(1)}, bf16[64,1280]{1,0:T(8,128)(2,1)S(1)}, u32[]{:S(2)}, u32[]{:S(2)}) %collective-permute-start.8) | collective-permute-done | bytes 163872 | tf_op jit(solution)/shard_map/ppermute | solution.py:595
  35.9 0.0 collective-permute-start.9
  35.9 1.1 %columns_solved.1 = (bf16[256,512]{1,0:T(8,128)(2,1)S(1)}, bf16[768,512]{1,0:T(8,128)(2,1)S(1)}, bf16[512,512]{1,0:T(8,128)(2,1)S(1)}, bf16[512,512]{1,0:T(8,128)(2,1)S(1)}, bf16[512,512]{1,0:T(8,128)(2,1)S(1)}) custom-call(f32[128,512]{1,0:T(8,128)S(1)} %get-tuple-element.45.refs_0_.refs_3_, f32[128,384]{1,0:T(8,128)S(1)} %get-tuple-element.46.refs_1_.refs_4_, ...), custom_call_target="tpu_custom_call" | custom-call | flops 1100000000 | bytes 1000000 | tf_op jit(solution)/shard_map/columns_solved/pallas_call | solution.py:526
  37.0 0.3 collective-permute-done.9.refs_14_
  37.3 2.6 %finish.1 = (f32[256,512]{1,0:T(8,128)}, f32[256,512]{1,0:T(8,128)}) custom-call(f32[1,1]{1,0:T(1,128)} %bitcast.7.ridge_ref, bf16[256,512]{1,0:T(8,128)(2,1)S(1)} %get-tuple-element.68.columns_ref, bf16[768,512]{1,0:T(8,128)(2,1)S(1)} %get-tuple-element.69.parts_ref, bf16[512,512]{1,0:T(8,128)(2,1)S(1)} %get-tuple-element.70.refs_0_, ...), custom_call_target="tpu_custom_call" | custom-call | flops 2200000000 | bytes 1000000 | tf_op jit(solution)/shard_map/finish/pallas_call | solution.py:584
  (2 shorter events, 0.0 us)
Async XLA Ops:
  1.3 2.5 %copy-start = (bf16[256,2048]{1,0:T(8,128)(2,1)S(1)}, bf16[256,2048]{1,0:T(8,128)(2,1)}, u32[]{:S(2)}) copy-start(bf16[256,2048]{1,0:T(8,128)(2,1)} %pool_ref.1) | copy-start | bytes 3145732
  1.3 2.5 %copy-start.1 = (s32[128]{0:T(128)S(1)}, s32[128]{0:T(128)}, u32[]{:S(2)}) copy-start(s32[128]{0:T(128)} %param.5) | copy-start | bytes 1540
  4.4 1.5 %collective-permute-start = (f32[64,512]{1,0:T(8,128)S(1)}, f32[64,512]{1,0:T(8,128)S(1)}, u32[]{:S(2)}, u32[]{:S(2)}) collective-permute-start(f32[64,512]{1,0:T(8,128)S(1)} %get-tuple-element.39), channel_id=1, source_target_pairs={{0,4},{4,0},{8,12},{12,8},{1,5},{5,1},{9,13},{13,9},{2,6},{6,2},{1... | collective-permute-start | bytes 393224 | tf_op jit(solution)/shard_map/ppermute | solution.py:595
  5.9 6.8 %collective-permute-start.1 = (f32[64,512]{1,0:T(8,128)S(1)}, f32[64,512]{1,0:T(8,128)S(1)}, u32[]{:S(2)}, u32[]{:S(2)}) collective-permute-start(f32[64,512]{1,0:T(8,128)S(1)} %add.6._), channel_id=1, source_target_pairs={{0,8},{4,12},{8,0},{12,4},{1,9},{5,13},{9,1},{13,5},{2,10},{6,14},... | collective-permute-start | bytes 393224 | tf_op jit(solution)/shard_map/ppermute | solution.py:595
  12.8 4.3 %collective-permute-start.2 = (bf16[64,512]{1,0:T(8,128)(2,1)S(1)}, bf16[64,512]{1,0:T(8,128)(2,1)S(1)}, u32[]{:S(2)}, u32[]{:S(2)}) collective-permute-start(bf16[64,512]{1,0:T(8,128)(2,1)S(1)} %get-tuple-element.74.refs_0_.refs_8_.refs_7_), channel_id=1, source_target_pairs={{0,16},{16,0},{1,17},{17,1},{2,18},{18,2},{3,19},{19,3},{4,20},{20... | collective-permute-start | bytes 196616 | tf_op jit(solution)/shard_map/ppermute | solution.py:595
  17.1 2.1 %collective-permute-start.5 = (f32[64,2560]{1,0:T(8,128)S(1)}, f32[64,2560]{1,0:T(8,128)S(1)}, u32[]{:S(2)}, u32[]{:S(2)}) collective-permute-start(f32[64,2560]{1,0:T(8,128)S(1)} %get-tuple-element.53), channel_id=1, source_target_pairs={{0,4},{4,0},{8,12},{12,8},{1,5},{5,1},{9,13},{13,9},{2,6},{6,2},{1... | collective-permute-start | bytes 1966088 | tf_op jit(solution)/shard_map/ppermute | solution.py:595
  17.1 3.9 %collective-permute-start.3 = (bf16[64,512]{1,0:T(8,128)(2,1)S(1)}, bf16[64,512]{1,0:T(8,128)(2,1)S(1)}, u32[]{:S(2)}, u32[]{:S(2)}) collective-permute-start(bf16[64,512]{1,0:T(8,128)(2,1)S(1)} %get-tuple-element.74.refs_0_.refs_8_.refs_7_), channel_id=1, source_target_pairs={{0,4},{4,0},{8,12},{12,8},{1,5},{5,1},{9,13},{13,9},{2,6},{6,2},{1... | collective-permute-start | bytes 196616 | tf_op jit(solution)/shard_map/ppermute | solution.py:595
  17.6 3.4 %collective-permute-start.4 = (bf16[64,512]{1,0:T(8,128)(2,1)S(1)}, bf16[64,512]{1,0:T(8,128)(2,1)S(1)}, u32[]{:S(2)}, u32[]{:S(2)}) collective-permute-start(bf16[64,512]{1,0:T(8,128)(2,1)S(1)} %collective-permute-done.2.refs_1_.refs_9_.refs_8_), channel_id=1, source_target_pairs={{0,4},{4,0},{8,12},{12,8},{1,5},{5,1},{9,13},{13,9},{2,6},{6,2},{1... | collective-permute-start | bytes 196616 | tf_op jit(solution)/shard_map/ppermute | solution.py:595
  19.3 9.8 %collective-permute-start.6 = (f32[64,1280]{1,0:T(8,128)S(1)}, f32[64,1280]{1,0:T(8,128)S(1)}, u32[]{:S(2)}, u32[]{:S(2)}) collective-permute-start(f32[64,1280]{1,0:T(8,128)S(1)} %last_sent.1), channel_id=1, source_target_pairs={{0,8},{4,12},{8,0},{12,4},{1,9},{5,13},{9,1},{13,5},{2,10},{6,14},... | collective-permute-start | bytes 983048 | tf_op jit(solution)/shard_map/ppermute | solution.py:595
  29.2 1.8 %collective-permute-start.7 = (bf16[64,1280]{1,0:T(8,128)(2,1)S(1)}, bf16[64,1280]{1,0:T(8,128)(2,1)S(1)}, u32[]{:S(2)}, u32[]{:S(2)}) collective-permute-start(bf16[64,1280]{1,0:T(8,128)(2,1)S(1)} %get-tuple-element.54.refs_12_.refs_11_), channel_id=1, source_target_pairs={{0,4},{4,0},{8,12},{12,8},{1,5},{5,1},{9,13},{13,9},{2,6},{6,2},{1... | collective-permute-start | bytes 491528 | tf_op jit(solution)/shard_map/ppermute | solution.py:595
  29.3 6.6 %collective-permute-start.8 = (bf16[64,1280]{1,0:T(8,128)(2,1)S(1)}, bf16[64,1280]{1,0:T(8,128)(2,1)S(1)}, u32[]{:S(2)}, u32[]{:S(2)}) collective-permute-start(bf16[64,1280]{1,0:T(8,128)(2,1)S(1)} %get-tuple-element.62), channel_id=1, source_target_pairs={{0,16},{16,0},{1,17},{17,1},{2,18},{18,2},{3,19},{19,3},{4,20},{20... | collective-permute-start | bytes 491528 | tf_op jit(solution)/shard_map/ppermute | solution.py:595
  35.9 1.4 %collective-permute-start.9 = (bf16[64,1280]{1,0:T(8,128)(2,1)S(1)}, bf16[64,1280]{1,0:T(8,128)(2,1)S(1)}, u32[]{:S(2)}, u32[]{:S(2)}) collective-permute-start(bf16[64,1280]{1,0:T(8,128)(2,1)S(1)} %collective-permute-done.8.refs_13_.refs_12_), channel_id=1, source_target_pairs={{0,4},{4,0},{8,12},{12,8},{1,5},{5,1},{9,13},{13,9},{2,6},{6,2},{1... | collective-permute-start | bytes 491528 | tf_op jit(solution)/shard_map/ppermute | solution.py:595

commit v7 on v6

--- a/solution.py
+++ b/solution.py
@@ -17,6 +17,7 @@
 DEPTH = 256
 SEGMENT = 128
 VMEM = pl.BlockSpec(memory_space=pltpu.VMEM)
+SMEM = pl.BlockSpec(memory_space=pltpu.SMEM)
 ANYWHERE = pl.BlockSpec(memory_space=pl.ANY)
 
 
@@ -56,7 +57,8 @@
 
 def segment_signs(seed_ref, coordinates, feature, width, index):
     first = lax.axis_index("tp") * coordinates + index * SEGMENT
-    return sign_tile(seed_ref[...], first, feature, (SEGMENT, width))
+    seed = seed_ref[0] if len(seed_ref.shape) == 1 else seed_ref[...]
+    return sign_tile(seed, first, feature, (SEGMENT, width))
 
 
 def project_step(seed_ref, chosen_ref, feature, width, index, total):
@@ -86,7 +88,7 @@
 
 def panel_signs(seed, coordinates):
     return call(
-        panel_signs_kernel, [((coordinates, PANEL), jnp.bfloat16)], [VMEM], 2, "panel_signs"
+        panel_signs_kernel, [((coordinates, PANEL), jnp.bfloat16)], [SMEM], 2, "panel_signs"
     )(seed)[0]
 
 
@@ -110,7 +112,7 @@
         [VMEM, VMEM, VMEM],
         1,
         "panel_part",
-    )(selection[None, :], pool, panel_signs(seed, coordinates))
+    )(selection[None, :], pool, panel_signs(seed.reshape(-1), coordinates))
 
 
 def blocks_part_kernel(blocks, seed_ref, chosen_ref, _, *part_refs):

time: 40 us -> 39.2 us (0.980)
  Pallas kernels: 25.3 us -> 24.5 us
    pallas_call x1, Pallas kernels: 2.46 us -> 1.66 us  [panel_signs(): call(panel_signs_kernel, [((coordinates, PANEL), jnp.bfloat16)], [SMEM],...]
  transfers between devices with their start and end apart: 10 -> 10, of which waited for: 6 -> 6; matrix products, arithmetic and copies ran while one was open for 0% -> 0% of each run, Pallas kernels for 49% -> 50%
where the time goes in v7:
time: 39.2 us; the launch traced here: 39 us
  Pallas kernels  24.5 us (62%)
  starting transfers between devices  9.25 us (24%)
  waiting for transfers between devices  3.13 us (8%)
  between operations  2.06 us (5%)
    ppermute x10, starting transfers between devices, swapped(): lax.ppermute(value, axis, [(s, s ^ bit) for s in range(lax.axis_size(axis...  9.25 us
    pallas_call x1, Pallas kernels, first_blocks(): call(functools.partial(first_blocks_kernel, blocks, len(phi)), block_shap...  6.43 us
    pallas_call x1, Pallas kernels, last_blocks(): call(functools.partial(last_blocks_kernel, blocks), block_shapes(gram.sha...  4.47 us
    pallas_call x1, Pallas kernels, blocks_part(): call(functools.partial(blocks_part_kernel, blocks), [((chosen.shape[0], w...  3.84 us
    ppermute x10, waiting for transfers between devices, swapped(): lax.ppermute(value, axis, [(s, s ^ bit) for s in range(lax.axis_size(axis...  3.13 us
    pallas_call x1, Pallas kernels, finish(): call(functools.partial(finish_kernel, len(uppers), len(phi), blk_count),...  2.58 us
    pallas_call x1, Pallas kernels, other_parts(): call(functools.partial(other_parts_kernel, tp_count, blk_count), [((rows...  2.32 us
    pallas_call x1, Pallas kernels, panel_signs(): call(panel_signs_kernel, [((coordinates, PANEL), jnp.bfloat16)], [SMEM],...  1.66 us
  transfers between devices with their start and end apart: 10, of which 6 were waited for; matrix products, arithmetic and copies ran while one was open for 0% of the time, Pallas kernels for 50%

profile of v7, /device:TPU:0, one launch (start us, length us, event | category | flops | bytes accessed | tf_op | source)
XLA Modules:
  0.0 39.0 jit_solution(3698304002152818047)
XLA Ops:
  1.3 0.0 copy-start
  1.3 0.0 copy-start.1
  1.3 1.7 %panel_signs.1.signs_ref = bf16[2048,512]{1,0:T(8,128)(2,1)S(1)} custom-call(s32[1]{0:T(128)} %copy.6.seed_ref), custom_call_target="tpu_custom_call" | custom-call | flops 2200000000 | bytes 1000000 | tf_op jit(solution)/shard_map/panel_signs/pallas_call | solution.py:90
  3.0 0.0 copy-done
  3.0 0.0 copy-done.1
  3.0 0.6 %panel_part.1 = (f32[64,512]{1,0:T(8,128)S(1)}, f32[64,512]{1,0:T(8,128)S(1)}, bf16[128,2048]{1,0:T(8,128)(2,1)S(1)}) custom-call(s32[1,128]{1,0:T(1,128)S(1)} %bitcast.7, bf16[256,2048]{1,0:T(8,128)(2,1)S(1)} %copy-done, bf16[2048,512]{1,0:T(8,128)(2,1)S(1)} %panel_signs.1.signs_ref), custom_call_target="tpu_custom_call" | custom-call | flops 1100000000 | bytes 1000000 | tf_op jit(solution)/shard_map/panel_part/pallas_call | solution.py:109
  3.6 0.5 %collective-permute-start = (f32[64,512]{1,0:T(8,128)S(1)}, f32[64,512]{1,0:T(8,128)S(1)}, u32[]{:S(2)}, u32[]{:S(2)}) collective-permute-start(f32[64,512]{1,0:T(8,128)S(1)} %get-tuple-element.39), channel_id=1, source_target_pairs={{0,4},{4,0},{8,12},{12,8},{1,5},{5,1},{9,13},{13,9},{2,6},{6,2},{1... | collective-permute-start | bytes 393224 | tf_op jit(solution)/shard_map/ppermute | solution.py:597
  4.1 1.0 %collective-permute-done = f32[64,512]{1,0:T(8,128)S(1)} collective-permute-done((f32[64,512]{1,0:T(8,128)S(1)}, f32[64,512]{1,0:T(8,128)S(1)}, u32[]{:S(2)}, u32[]{:S(2)}) %collective-permute-start) | collective-permute-done | bytes 131104 | tf_op jit(solution)/shard_map/ppermute | solution.py:597
  5.1 2.9 %collective-permute-start.1 = (f32[64,512]{1,0:T(8,128)S(1)}, f32[64,512]{1,0:T(8,128)S(1)}, u32[]{:S(2)}, u32[]{:S(2)}) collective-permute-start(f32[64,512]{1,0:T(8,128)S(1)} %add.6._), channel_id=1, source_target_pairs={{0,8},{4,12},{8,0},{12,4},{1,9},{5,13},{9,1},{13,5},{2,10},{6,14},... | collective-permute-start | bytes 393224 | tf_op jit(solution)/shard_map/ppermute | solution.py:597
  8.1 3.8 %blocks_part.1 = (f32[128,512]{1,0:T(8,128)S(1)}, f32[128,512]{1,0:T(8,128)S(1)}) custom-call(s32[1,1]{1,0:T(1,128)} %bitcast.3.seed_ref, bf16[128,2048]{1,0:T(8,128)(2,1)S(1)} %get-tuple-element.40.chosen_ref, f32[64,512]{1,0:T(8,128)S(1)} %add.6._), custom_call_target="tpu_custom_call" | custom-call | flops 4400000000 | bytes 1000000 | tf_op jit(solution)/shard_map/blocks_part/pallas_call | solution.py:125
  11.9 0.0 collective-permute-done.1
  11.9 1.7 %collective-permute-start.2 = (bf16[64,512]{1,0:T(8,128)(2,1)S(1)}, bf16[64,512]{1,0:T(8,128)(2,1)S(1)}, u32[]{:S(2)}, u32[]{:S(2)}) collective-permute-start(bf16[64,512]{1,0:T(8,128)(2,1)S(1)} %get-tuple-element.74.refs_0_.refs_8_.refs_7_), channel_id=1, source_target_pairs={{0,16},{16,0},{1,17},{17,1},{2,18},{18,2},{3,19},{19,3},{4,20},{20... | collective-permute-start | bytes 196616 | tf_op jit(solution)/shard_map/ppermute | solution.py:597
  13.7 2.3 %other_parts.1 = (f32[64,2560]{1,0:T(8,128)S(1)}, f32[64,2560]{1,0:T(8,128)S(1)}) custom-call(s32[1,1]{1,0:T(1,128)} %bitcast.4.seed_ref, bf16[128,2048]{1,0:T(8,128)(2,1)S(1)} %get-tuple-element.40.chosen_ref, f32[64,512]{1,0:T(8,128)S(1)} %get-tuple-element.75._, f32[128,512]{1,0:T(8,128)S(1)} %get-tuple-element.41.refs_0_, ...), custom_call_target="tpu_custom_call" | custom-call | flops 2200000000 | bytes 1000000 | tf_op jit(solution)/shard_map/other_parts/pallas_call | solution.py:171
  16.0 0.3 collective-permute-done.2.refs_1_.refs_9_.refs_8_
  16.3 0.0 collective-permute-start.5
  16.3 0.5 %collective-permute-start.3 = (bf16[64,512]{1,0:T(8,128)(2,1)S(1)}, bf16[64,512]{1,0:T(8,128)(2,1)S(1)}, u32[]{:S(2)}, u32[]{:S(2)}) collective-permute-start(bf16[64,512]{1,0:T(8,128)(2,1)S(1)} %get-tuple-element.74.refs_0_.refs_8_.refs_7_), channel_id=1, source_target_pairs={{0,4},{4,0},{8,12},{12,8},{1,5},{5,1},{9,13},{13,9},{2,6},{6,2},{1... | collective-permute-start | bytes 196616 | tf_op jit(solution)/shard_map/ppermute | solution.py:597
  16.8 0.0 collective-permute-start.4
  17.4 0.9 %collective-permute-done.5.right_ref = f32[64,2560]{1,0:T(8,128)S(1)} collective-permute-done((f32[64,2560]{1,0:T(8,128)S(1)}, f32[64,2560]{1,0:T(8,128)S(1)}, u32[]{:S(2)}, u32[]{:S(2)}) %collective-permute-start.5) | collective-permute-done | bytes 655392 | tf_op jit(solution)/shard_map/ppermute | solution.py:597
  18.4 0.1 last_sent.1
  18.4 1.8 %collective-permute-start.6 = (f32[64,1280]{1,0:T(8,128)S(1)}, f32[64,1280]{1,0:T(8,128)S(1)}, u32[]{:S(2)}, u32[]{:S(2)}) collective-permute-start(f32[64,1280]{1,0:T(8,128)S(1)} %last_sent.1), channel_id=1, source_target_pairs={{0,8},{4,12},{8,0},{12,4},{1,9},{5,13},{9,1},{13,5},{2,10},{6,14},... | collective-permute-start | bytes 983048 | tf_op jit(solution)/shard_map/ppermute | solution.py:597
  20.2 0.0 collective-permute-done.3.refs_2_.refs_10_.refs_9_
  20.2 0.0 collective-permute-done.4.refs_3_.refs_11_.refs_10_
  20.2 6.4 %gram_first_blocks.1 = (f32[128,512]{1,0:T(8,128)S(1)}, f32[128,384]{1,0:T(8,128)S(1)}, f32[256,128]{1,0:T(8,128)S(1)}, f32[256,128]{1,0:T(8,128)S(1)}, f32[256,256]{1,0:T(8,128)S(1)}, /*index=5*/f32[256,256]{1,0:T(8,128)S(1)}) custom-call(f32[1,1]{1,0:T(1,128)} %bitcast.5.ridge_ref, bf16[64,512]{1,0:T(8,128)(2,1)S(1)} %get-tuple-element.74.refs_0_.refs_8_.refs_7_, ...), custom_call_target="tpu_custom_call" | custom-call | flops 3849999872 | bytes 1000000 | tf_op jit(solution)/shard_map/gram_first_blocks/pallas_call | solution.py:456
  26.6 1.4 %start_block.1 = (f32[64,128]{1,0:T(8,128)S(1)}, f32[64,128]{1,0:T(8,128)S(1)}, f32[64,128]{1,0:T(8,128)S(1)}) custom-call(f32[256,256]{1,0:T(8,128)S(1)} %get-tuple-element.47.block_ref.gram_ref), custom_call_target="tpu_custom_call" | custom-call | flops 1650000000 | bytes 1000000 | tf_op jit(solution)/shard_map/start_block/pallas_call | solution.py:468
  28.0 0.3 collective-permute-done.6.came_ref
  28.3 0.1 pieces.1
  28.4 0.1 collective-permute-start.7
  28.4 1.7 %collective-permute-start.8 = (bf16[64,1280]{1,0:T(8,128)(2,1)S(1)}, bf16[64,1280]{1,0:T(8,128)(2,1)S(1)}, u32[]{:S(2)}, u32[]{:S(2)}) collective-permute-start(bf16[64,1280]{1,0:T(8,128)(2,1)S(1)} %get-tuple-element.62), channel_id=1, source_target_pairs={{0,16},{16,0},{1,17},{17,1},{2,18},{18,2},{3,19},{19,3},{4,20},{20... | collective-permute-start | bytes 491528 | tf_op jit(solution)/shard_map/ppermute | solution.py:597
  30.2 0.0 collective-permute-done.7.refs_13_
  30.2 4.5 %last_blocks.1 = (f32[128,256]{1,0:T(8,128)S(1)}, f32[128,128]{1,0:T(8,128)S(1)}, f32[256,128]{1,0:T(8,128)S(1)}, f32[256,128]{1,0:T(8,128)S(1)}) custom-call(f32[256,256]{1,0:T(8,128)S(1)} %get-tuple-element.47.block_ref.gram_ref, f32[256,256]{1,0:T(8,128)S(1)} %get-tuple-element.48.turned_ref, f32[64,128]{1,0:T(8,128)S(1)} %get-tuple-element.55._.inverse_ref, ...), custom_call_target="tpu_custom_call" | custom-call | flops 4950000128 | bytes 1000000 | tf_op jit(solution)/shard_map/last_blocks/pallas_call | solution.py:476
  34.6 0.4 %collective-permute-done.8.refs_13_.refs_12_ = bf16[64,1280]{1,0:T(8,128)(2,1)S(1)} collective-permute-done((bf16[64,1280]{1,0:T(8,128)(2,1)S(1)}, bf16[64,1280]{1,0:T(8,128)(2,1)S(1)}, u32[]{:S(2)}, u32[]{:S(2)}) %collective-permute-start.8) | collective-permute-done | bytes 163872 | tf_op jit(solution)/shard_map/ppermute | solution.py:597
  35.1 0.0 collective-permute-start.9
  35.1 1.1 %columns_solved.1 = (bf16[256,512]{1,0:T(8,128)(2,1)S(1)}, bf16[768,512]{1,0:T(8,128)(2,1)S(1)}, bf16[512,512]{1,0:T(8,128)(2,1)S(1)}, bf16[512,512]{1,0:T(8,128)(2,1)S(1)}, bf16[512,512]{1,0:T(8,128)(2,1)S(1)}) custom-call(f32[128,512]{1,0:T(8,128)S(1)} %get-tuple-element.45.refs_0_.refs_3_, f32[128,384]{1,0:T(8,128)S(1)} %get-tuple-element.46.refs_1_.refs_4_, ...), custom_call_target="tpu_custom_call" | custom-call | flops 1100000000 | bytes 1000000 | tf_op jit(solution)/shard_map/columns_solved/pallas_call | solution.py:528
  36.2 0.3 collective-permute-done.9.refs_14_
  36.4 2.6 %finish.1 = (f32[256,512]{1,0:T(8,128)}, f32[256,512]{1,0:T(8,128)}) custom-call(f32[1,1]{1,0:T(1,128)} %bitcast.6.ridge_ref, bf16[256,512]{1,0:T(8,128)(2,1)S(1)} %get-tuple-element.68.columns_ref, bf16[768,512]{1,0:T(8,128)(2,1)S(1)} %get-tuple-element.69.parts_ref, bf16[512,512]{1,0:T(8,128)(2,1)S(1)} %get-tuple-element.70.refs_0_, ...), custom_call_target="tpu_custom_call" | custom-call | flops 2200000000 | bytes 1000000 | tf_op jit(solution)/shard_map/finish/pallas_call | solution.py:586
  (2 shorter events, 0.0 us)
Async XLA Ops:
  1.3 1.7 %copy-start = (bf16[256,2048]{1,0:T(8,128)(2,1)S(1)}, bf16[256,2048]{1,0:T(8,128)(2,1)}, u32[]{:S(2)}) copy-start(bf16[256,2048]{1,0:T(8,128)(2,1)} %pool_ref.1) | copy-start | bytes 3145732
  1.3 1.7 %copy-start.1 = (s32[128]{0:T(128)S(1)}, s32[128]{0:T(128)}, u32[]{:S(2)}) copy-start(s32[128]{0:T(128)} %param.5) | copy-start | bytes 1540
  3.6 1.5 %collective-permute-start = (f32[64,512]{1,0:T(8,128)S(1)}, f32[64,512]{1,0:T(8,128)S(1)}, u32[]{:S(2)}, u32[]{:S(2)}) collective-permute-start(f32[64,512]{1,0:T(8,128)S(1)} %get-tuple-element.39), channel_id=1, source_target_pairs={{0,4},{4,0},{8,12},{12,8},{1,5},{5,1},{9,13},{13,9},{2,6},{6,2},{1... | collective-permute-start | bytes 393224 | tf_op jit(solution)/shard_map/ppermute | solution.py:597
  5.1 6.8 %collective-permute-start.1 = (f32[64,512]{1,0:T(8,128)S(1)}, f32[64,512]{1,0:T(8,128)S(1)}, u32[]{:S(2)}, u32[]{:S(2)}) collective-permute-start(f32[64,512]{1,0:T(8,128)S(1)} %add.6._), channel_id=1, source_target_pairs={{0,8},{4,12},{8,0},{12,4},{1,9},{5,13},{9,1},{13,5},{2,10},{6,14},... | collective-permute-start | bytes 393224 | tf_op jit(solution)/shard_map/ppermute | solution.py:597
  11.9 4.3 %collective-permute-start.2 = (bf16[64,512]{1,0:T(8,128)(2,1)S(1)}, bf16[64,512]{1,0:T(8,128)(2,1)S(1)}, u32[]{:S(2)}, u32[]{:S(2)}) collective-permute-start(bf16[64,512]{1,0:T(8,128)(2,1)S(1)} %get-tuple-element.74.refs_0_.refs_8_.refs_7_), channel_id=1, source_target_pairs={{0,16},{16,0},{1,17},{17,1},{2,18},{18,2},{3,19},{19,3},{4,20},{20... | collective-permute-start | bytes 196616 | tf_op jit(solution)/shard_map/ppermute | solution.py:597
  16.3 2.1 %collective-permute-start.5 = (f32[64,2560]{1,0:T(8,128)S(1)}, f32[64,2560]{1,0:T(8,128)S(1)}, u32[]{:S(2)}, u32[]{:S(2)}) collective-permute-start(f32[64,2560]{1,0:T(8,128)S(1)} %get-tuple-element.53), channel_id=1, source_target_pairs={{0,4},{4,0},{8,12},{12,8},{1,5},{5,1},{9,13},{13,9},{2,6},{6,2},{1... | collective-permute-start | bytes 1966088 | tf_op jit(solution)/shard_map/ppermute | solution.py:597
  16.3 3.9 %collective-permute-start.3 = (bf16[64,512]{1,0:T(8,128)(2,1)S(1)}, bf16[64,512]{1,0:T(8,128)(2,1)S(1)}, u32[]{:S(2)}, u32[]{:S(2)}) collective-permute-start(bf16[64,512]{1,0:T(8,128)(2,1)S(1)} %get-tuple-element.74.refs_0_.refs_8_.refs_7_), channel_id=1, source_target_pairs={{0,4},{4,0},{8,12},{12,8},{1,5},{5,1},{9,13},{13,9},{2,6},{6,2},{1... | collective-permute-start | bytes 196616 | tf_op jit(solution)/shard_map/ppermute | solution.py:597
  16.8 3.4 %collective-permute-start.4 = (bf16[64,512]{1,0:T(8,128)(2,1)S(1)}, bf16[64,512]{1,0:T(8,128)(2,1)S(1)}, u32[]{:S(2)}, u32[]{:S(2)}) collective-permute-start(bf16[64,512]{1,0:T(8,128)(2,1)S(1)} %collective-permute-done.2.refs_1_.refs_9_.refs_8_), channel_id=1, source_target_pairs={{0,4},{4,0},{8,12},{12,8},{1,5},{5,1},{9,13},{13,9},{2,6},{6,2},{1... | collective-permute-start | bytes 196616 | tf_op jit(solution)/shard_map/ppermute | solution.py:597
  18.4 9.8 %collective-permute-start.6 = (f32[64,1280]{1,0:T(8,128)S(1)}, f32[64,1280]{1,0:T(8,128)S(1)}, u32[]{:S(2)}, u32[]{:S(2)}) collective-permute-start(f32[64,1280]{1,0:T(8,128)S(1)} %last_sent.1), channel_id=1, source_target_pairs={{0,8},{4,12},{8,0},{12,4},{1,9},{5,13},{9,1},{13,5},{2,10},{6,14},... | collective-permute-start | bytes 983048 | tf_op jit(solution)/shard_map/ppermute | solution.py:597
  28.4 1.8 %collective-permute-start.7 = (bf16[64,1280]{1,0:T(8,128)(2,1)S(1)}, bf16[64,1280]{1,0:T(8,128)(2,1)S(1)}, u32[]{:S(2)}, u32[]{:S(2)}) collective-permute-start(bf16[64,1280]{1,0:T(8,128)(2,1)S(1)} %get-tuple-element.54.refs_12_.refs_11_), channel_id=1, source_target_pairs={{0,4},{4,0},{8,12},{12,8},{1,5},{5,1},{9,13},{13,9},{2,6},{6,2},{1... | collective-permute-start | bytes 491528 | tf_op jit(solution)/shard_map/ppermute | solution.py:597
  28.4 6.6 %collective-permute-start.8 = (bf16[64,1280]{1,0:T(8,128)(2,1)S(1)}, bf16[64,1280]{1,0:T(8,128)(2,1)S(1)}, u32[]{:S(2)}, u32[]{:S(2)}) collective-permute-start(bf16[64,1280]{1,0:T(8,128)(2,1)S(1)} %get-tuple-element.62), channel_id=1, source_target_pairs={{0,16},{16,0},{1,17},{17,1},{2,18},{18,2},{3,19},{19,3},{4,20},{20... | collective-permute-start | bytes 491528 | tf_op jit(solution)/shard_map/ppermute | solution.py:597
  35.1 1.4 %collective-permute-start.9 = (bf16[64,1280]{1,0:T(8,128)(2,1)S(1)}, bf16[64,1280]{1,0:T(8,128)(2,1)S(1)}, u32[]{:S(2)}, u32[]{:S(2)}) collective-permute-start(bf16[64,1280]{1,0:T(8,128)(2,1)S(1)} %collective-permute-done.8.refs_13_.refs_12_), channel_id=1, source_target_pairs={{0,4},{4,0},{8,12},{12,8},{1,5},{5,1},{9,13},{13,9},{2,6},{6,2},{1... | collective-permute-start | bytes 491528 | tf_op jit(solution)/shard_map/ppermute | solution.py:597

commit v8 on v7

--- a/solution.py
+++ b/solution.py
@@ -15,7 +15,7 @@
 LEAD = 3
 BLOCK = 128
 DEPTH = 256
-SEGMENT = 128
+SEGMENT = 256
 VMEM = pl.BlockSpec(memory_space=pltpu.VMEM)
 SMEM = pl.BlockSpec(memory_space=pltpu.SMEM)
 ANYWHERE = pl.BlockSpec(memory_space=pl.ANY)

time: 39.2 us -> 39.2 us (level)
  Pallas kernels: 24.5 us -> 24 us
  transfers between devices with their start and end apart: 10 -> 10, of which waited for: 6 -> 7; matrix products, arithmetic and copies ran while one was open for 0% -> 0% of each run, Pallas kernels for 50% -> 49%
where the time goes in v8:
time: 39.2 us; the launch traced here: 39 us
  Pallas kernels  24 us (61%)
  starting transfers between devices  9.39 us (24%)
  waiting for transfers between devices  3.48 us (9%)
  between operations  2.06 us (5%)
    ppermute x10, starting transfers between devices, swapped(): lax.ppermute(value, axis, [(s, s ^ bit) for s in range(lax.axis_size(axis...  9.39 us
    pallas_call x1, Pallas kernels, first_blocks(): call(functools.partial(first_blocks_kernel, blocks, len(phi)), block_shap...  6.43 us
    pallas_call x1, Pallas kernels, last_blocks(): call(functools.partial(last_blocks_kernel, blocks), block_shapes(gram.sha...  4.47 us
    pallas_call x1, Pallas kernels, blocks_part(): call(functools.partial(blocks_part_kernel, blocks), [((chosen.shape[0], w...  3.49 us
    ppermute x10, waiting for transfers between devices, swapped(): lax.ppermute(value, axis, [(s, s ^ bit) for s in range(lax.axis_size(axis...  3.48 us
    pallas_call x1, Pallas kernels, finish(): call(functools.partial(finish_kernel, len(uppers), len(phi), blk_count),...  2.58 us
    pallas_call x1, Pallas kernels, other_parts(): call(functools.partial(other_parts_kernel, tp_count, blk_count), [((rows...  2.13 us
    pallas_call x1, Pallas kernels, panel_signs(): call(panel_signs_kernel, [((coordinates, PANEL), jnp.bfloat16)], [SMEM],...  1.66 us
  transfers between devices with their start and end apart: 10, of which 7 were waited for; matrix products, arithmetic and copies ran while one was open for 0% of the time, Pallas kernels for 49%

profile of v8, /device:TPU:0, one launch (start us, length us, event | category | flops | bytes accessed | tf_op | source)
XLA Modules:
  0.0 39.0 jit_solution(13325603532112196455)
XLA Ops:
  1.3 0.0 copy-start
  1.3 0.0 copy-start.1
  1.3 1.7 %panel_signs.1.signs_ref = bf16[2048,512]{1,0:T(8,128)(2,1)S(1)} custom-call(s32[1]{0:T(128)} %copy.6.seed_ref), custom_call_target="tpu_custom_call" | custom-call | flops 2200000000 | bytes 1000000 | tf_op jit(solution)/shard_map/panel_signs/pallas_call | solution.py:90
  3.0 0.0 copy-done
  3.0 0.0 copy-done.1
  3.0 0.6 %panel_part.1 = (f32[64,512]{1,0:T(8,128)S(1)}, f32[64,512]{1,0:T(8,128)S(1)}, bf16[128,2048]{1,0:T(8,128)(2,1)S(1)}) custom-call(s32[1,128]{1,0:T(1,128)S(1)} %bitcast.7, bf16[256,2048]{1,0:T(8,128)(2,1)S(1)} %copy-done, bf16[2048,512]{1,0:T(8,128)(2,1)S(1)} %panel_signs.1.signs_ref), custom_call_target="tpu_custom_call" | custom-call | flops 1100000000 | bytes 1000000 | tf_op jit(solution)/shard_map/panel_part/pallas_call | solution.py:109
  3.6 0.5 %collective-permute-start = (f32[64,512]{1,0:T(8,128)S(1)}, f32[64,512]{1,0:T(8,128)S(1)}, u32[]{:S(2)}, u32[]{:S(2)}) collective-permute-start(f32[64,512]{1,0:T(8,128)S(1)} %get-tuple-element.39), channel_id=1, source_target_pairs={{0,4},{4,0},{8,12},{12,8},{1,5},{5,1},{9,13},{13,9},{2,6},{6,2},{1... | collective-permute-start | bytes 393224 | tf_op jit(solution)/shard_map/ppermute | solution.py:597
  4.1 1.0 %collective-permute-done = f32[64,512]{1,0:T(8,128)S(1)} collective-permute-done((f32[64,512]{1,0:T(8,128)S(1)}, f32[64,512]{1,0:T(8,128)S(1)}, u32[]{:S(2)}, u32[]{:S(2)}) %collective-permute-start) | collective-permute-done | bytes 131104 | tf_op jit(solution)/shard_map/ppermute | solution.py:597
  5.1 2.9 %collective-permute-start.1 = (f32[64,512]{1,0:T(8,128)S(1)}, f32[64,512]{1,0:T(8,128)S(1)}, u32[]{:S(2)}, u32[]{:S(2)}) collective-permute-start(f32[64,512]{1,0:T(8,128)S(1)} %add.6._), channel_id=1, source_target_pairs={{0,8},{4,12},{8,0},{12,4},{1,9},{5,13},{9,1},{13,5},{2,10},{6,14},... | collective-permute-start | bytes 393224 | tf_op jit(solution)/shard_map/ppermute | solution.py:597
  8.1 3.5 %blocks_part.1 = (f32[128,512]{1,0:T(8,128)S(1)}, f32[128,512]{1,0:T(8,128)S(1)}) custom-call(s32[1,1]{1,0:T(1,128)} %bitcast.3.seed_ref, bf16[128,2048]{1,0:T(8,128)(2,1)S(1)} %get-tuple-element.40.chosen_ref, f32[64,512]{1,0:T(8,128)S(1)} %add.6._), custom_call_target="tpu_custom_call" | custom-call | flops 4400000000 | bytes 1000000 | tf_op jit(solution)/shard_map/blocks_part/pallas_call | solution.py:125
  11.6 0.3 collective-permute-done.1
  11.9 1.8 %collective-permute-start.2 = (bf16[64,512]{1,0:T(8,128)(2,1)S(1)}, bf16[64,512]{1,0:T(8,128)(2,1)S(1)}, u32[]{:S(2)}, u32[]{:S(2)}) collective-permute-start(bf16[64,512]{1,0:T(8,128)(2,1)S(1)} %get-tuple-element.74.refs_0_.refs_8_.refs_7_), channel_id=1, source_target_pairs={{0,16},{16,0},{1,17},{17,1},{2,18},{18,2},{3,19},{19,3},{4,20},{20... | collective-permute-start | bytes 196616 | tf_op jit(solution)/shard_map/ppermute | solution.py:597
  13.7 2.1 %other_parts.1 = (f32[64,2560]{1,0:T(8,128)S(1)}, f32[64,2560]{1,0:T(8,128)S(1)}) custom-call(s32[1,1]{1,0:T(1,128)} %bitcast.4.seed_ref, bf16[128,2048]{1,0:T(8,128)(2,1)S(1)} %get-tuple-element.40.chosen_ref, f32[64,512]{1,0:T(8,128)S(1)} %get-tuple-element.75._, f32[128,512]{1,0:T(8,128)S(1)} %get-tuple-element.41.refs_0_, ...), custom_call_target="tpu_custom_call" | custom-call | flops 2200000000 | bytes 1000000 | tf_op jit(solution)/shard_map/other_parts/pallas_call | solution.py:171
  15.8 0.4 %collective-permute-done.2.refs_1_.refs_9_.refs_8_ = bf16[64,512]{1,0:T(8,128)(2,1)S(1)} collective-permute-done((bf16[64,512]{1,0:T(8,128)(2,1)S(1)}, bf16[64,512]{1,0:T(8,128)(2,1)S(1)}, u32[]{:S(2)}, u32[]{:S(2)}) %collective-permute-start.2) | collective-permute-done | bytes 65568 | tf_op jit(solution)/shard_map/ppermute | solution.py:597
  16.2 0.0 collective-permute-start.5
  16.2 0.5 %collective-permute-start.3 = (bf16[64,512]{1,0:T(8,128)(2,1)S(1)}, bf16[64,512]{1,0:T(8,128)(2,1)S(1)}, u32[]{:S(2)}, u32[]{:S(2)}) collective-permute-start(bf16[64,512]{1,0:T(8,128)(2,1)S(1)} %get-tuple-element.74.refs_0_.refs_8_.refs_7_), channel_id=1, source_target_pairs={{0,4},{4,0},{8,12},{12,8},{1,5},{5,1},{9,13},{13,9},{2,6},{6,2},{1... | collective-permute-start | bytes 196616 | tf_op jit(solution)/shard_map/ppermute | solution.py:597
  16.8 0.0 collective-permute-start.4
  17.4 0.9 %collective-permute-done.5.right_ref = f32[64,2560]{1,0:T(8,128)S(1)} collective-permute-done((f32[64,2560]{1,0:T(8,128)S(1)}, f32[64,2560]{1,0:T(8,128)S(1)}, u32[]{:S(2)}, u32[]{:S(2)}) %collective-permute-start.5) | collective-permute-done | bytes 655392 | tf_op jit(solution)/shard_map/ppermute | solution.py:597
  18.3 0.1 last_sent.1
  18.4 1.8 %collective-permute-start.6 = (f32[64,1280]{1,0:T(8,128)S(1)}, f32[64,1280]{1,0:T(8,128)S(1)}, u32[]{:S(2)}, u32[]{:S(2)}) collective-permute-start(f32[64,1280]{1,0:T(8,128)S(1)} %last_sent.1), channel_id=1, source_target_pairs={{0,8},{4,12},{8,0},{12,4},{1,9},{5,13},{9,1},{13,5},{2,10},{6,14},... | collective-permute-start | bytes 983048 | tf_op jit(solution)/shard_map/ppermute | solution.py:597
  20.2 0.0 collective-permute-done.3.refs_2_.refs_10_.refs_9_
  20.2 0.0 collective-permute-done.4.refs_3_.refs_11_.refs_10_
  20.2 6.4 %gram_first_blocks.1 = (f32[128,512]{1,0:T(8,128)S(1)}, f32[128,384]{1,0:T(8,128)S(1)}, f32[256,128]{1,0:T(8,128)S(1)}, f32[256,128]{1,0:T(8,128)S(1)}, f32[256,256]{1,0:T(8,128)S(1)}, /*index=5*/f32[256,256]{1,0:T(8,128)S(1)}) custom-call(f32[1,1]{1,0:T(1,128)} %bitcast.5.ridge_ref, bf16[64,512]{1,0:T(8,128)(2,1)S(1)} %get-tuple-element.74.refs_0_.refs_8_.refs_7_, ...), custom_call_target="tpu_custom_call" | custom-call | flops 3849999872 | bytes 1000000 | tf_op jit(solution)/shard_map/gram_first_blocks/pallas_call | solution.py:456
  26.7 1.4 %start_block.1 = (f32[64,128]{1,0:T(8,128)S(1)}, f32[64,128]{1,0:T(8,128)S(1)}, f32[64,128]{1,0:T(8,128)S(1)}) custom-call(f32[256,256]{1,0:T(8,128)S(1)} %get-tuple-element.47.block_ref.gram_ref), custom_call_target="tpu_custom_call" | custom-call | flops 1650000000 | bytes 1000000 | tf_op jit(solution)/shard_map/start_block/pallas_call | solution.py:468
  28.0 0.2 collective-permute-done.6.came_ref
  28.2 0.1 pieces.1
  28.3 0.1 collective-permute-start.7
  28.4 1.8 %collective-permute-start.8 = (bf16[64,1280]{1,0:T(8,128)(2,1)S(1)}, bf16[64,1280]{1,0:T(8,128)(2,1)S(1)}, u32[]{:S(2)}, u32[]{:S(2)}) collective-permute-start(bf16[64,1280]{1,0:T(8,128)(2,1)S(1)} %get-tuple-element.62), channel_id=1, source_target_pairs={{0,16},{16,0},{1,17},{17,1},{2,18},{18,2},{3,19},{19,3},{4,20},{20... | collective-permute-start | bytes 491528 | tf_op jit(solution)/shard_map/ppermute | solution.py:597
  30.2 0.0 collective-permute-done.7.refs_13_
  30.2 4.5 %last_blocks.1 = (f32[128,256]{1,0:T(8,128)S(1)}, f32[128,128]{1,0:T(8,128)S(1)}, f32[256,128]{1,0:T(8,128)S(1)}, f32[256,128]{1,0:T(8,128)S(1)}) custom-call(f32[256,256]{1,0:T(8,128)S(1)} %get-tuple-element.47.block_ref.gram_ref, f32[256,256]{1,0:T(8,128)S(1)} %get-tuple-element.48.turned_ref, f32[64,128]{1,0:T(8,128)S(1)} %get-tuple-element.55._.inverse_ref, ...), custom_call_target="tpu_custom_call" | custom-call | flops 4950000128 | bytes 1000000 | tf_op jit(solution)/shard_map/last_blocks/pallas_call | solution.py:476
  34.7 0.4 collective-permute-done.8.refs_13_.refs_12_
  35.0 0.0 collective-permute-start.9
  35.0 1.1 %columns_solved.1 = (bf16[256,512]{1,0:T(8,128)(2,1)S(1)}, bf16[768,512]{1,0:T(8,128)(2,1)S(1)}, bf16[512,512]{1,0:T(8,128)(2,1)S(1)}, bf16[512,512]{1,0:T(8,128)(2,1)S(1)}, bf16[512,512]{1,0:T(8,128)(2,1)S(1)}) custom-call(f32[128,512]{1,0:T(8,128)S(1)} %get-tuple-element.45.refs_0_.refs_3_, f32[128,384]{1,0:T(8,128)S(1)} %get-tuple-element.46.refs_1_.refs_4_, ...), custom_call_target="tpu_custom_call" | custom-call | flops 1100000000 | bytes 1000000 | tf_op jit(solution)/shard_map/columns_solved/pallas_call | solution.py:528
  36.1 0.3 collective-permute-done.9.refs_14_
  36.4 2.6 %finish.1 = (f32[256,512]{1,0:T(8,128)}, f32[256,512]{1,0:T(8,128)}) custom-call(f32[1,1]{1,0:T(1,128)} %bitcast.6.ridge_ref, bf16[256,512]{1,0:T(8,128)(2,1)S(1)} %get-tuple-element.68.columns_ref, bf16[768,512]{1,0:T(8,128)(2,1)S(1)} %get-tuple-element.69.parts_ref, bf16[512,512]{1,0:T(8,128)(2,1)S(1)} %get-tuple-element.70.refs_0_, ...), custom_call_target="tpu_custom_call" | custom-call | flops 2200000000 | bytes 1000000 | tf_op jit(solution)/shard_map/finish/pallas_call | solution.py:586
  (2 shorter events, 0.0 us)
Async XLA Ops:
  1.3 1.7 %copy-start = (bf16[256,2048]{1,0:T(8,128)(2,1)S(1)}, bf16[256,2048]{1,0:T(8,128)(2,1)}, u32[]{:S(2)}) copy-start(bf16[256,2048]{1,0:T(8,128)(2,1)} %pool_ref.1) | copy-start | bytes 3145732
  1.3 1.7 %copy-start.1 = (s32[128]{0:T(128)S(1)}, s32[128]{0:T(128)}, u32[]{:S(2)}) copy-start(s32[128]{0:T(128)} %param.5) | copy-start | bytes 1540
  3.6 1.5 %collective-permute-start = (f32[64,512]{1,0:T(8,128)S(1)}, f32[64,512]{1,0:T(8,128)S(1)}, u32[]{:S(2)}, u32[]{:S(2)}) collective-permute-start(f32[64,512]{1,0:T(8,128)S(1)} %get-tuple-element.39), channel_id=1, source_target_pairs={{0,4},{4,0},{8,12},{12,8},{1,5},{5,1},{9,13},{13,9},{2,6},{6,2},{1... | collective-permute-start | bytes 393224 | tf_op jit(solution)/shard_map/ppermute | solution.py:597
  5.1 6.8 %collective-permute-start.1 = (f32[64,512]{1,0:T(8,128)S(1)}, f32[64,512]{1,0:T(8,128)S(1)}, u32[]{:S(2)}, u32[]{:S(2)}) collective-permute-start(f32[64,512]{1,0:T(8,128)S(1)} %add.6._), channel_id=1, source_target_pairs={{0,8},{4,12},{8,0},{12,4},{1,9},{5,13},{9,1},{13,5},{2,10},{6,14},... | collective-permute-start | bytes 393224 | tf_op jit(solution)/shard_map/ppermute | solution.py:597
  11.9 4.3 %collective-permute-start.2 = (bf16[64,512]{1,0:T(8,128)(2,1)S(1)}, bf16[64,512]{1,0:T(8,128)(2,1)S(1)}, u32[]{:S(2)}, u32[]{:S(2)}) collective-permute-start(bf16[64,512]{1,0:T(8,128)(2,1)S(1)} %get-tuple-element.74.refs_0_.refs_8_.refs_7_), channel_id=1, source_target_pairs={{0,16},{16,0},{1,17},{17,1},{2,18},{18,2},{3,19},{19,3},{4,20},{20... | collective-permute-start | bytes 196616 | tf_op jit(solution)/shard_map/ppermute | solution.py:597
  16.2 2.1 %collective-permute-start.5 = (f32[64,2560]{1,0:T(8,128)S(1)}, f32[64,2560]{1,0:T(8,128)S(1)}, u32[]{:S(2)}, u32[]{:S(2)}) collective-permute-start(f32[64,2560]{1,0:T(8,128)S(1)} %get-tuple-element.53), channel_id=1, source_target_pairs={{0,4},{4,0},{8,12},{12,8},{1,5},{5,1},{9,13},{13,9},{2,6},{6,2},{1... | collective-permute-start | bytes 1966088 | tf_op jit(solution)/shard_map/ppermute | solution.py:597
  16.2 4.0 %collective-permute-start.3 = (bf16[64,512]{1,0:T(8,128)(2,1)S(1)}, bf16[64,512]{1,0:T(8,128)(2,1)S(1)}, u32[]{:S(2)}, u32[]{:S(2)}) collective-permute-start(bf16[64,512]{1,0:T(8,128)(2,1)S(1)} %get-tuple-element.74.refs_0_.refs_8_.refs_7_), channel_id=1, source_target_pairs={{0,4},{4,0},{8,12},{12,8},{1,5},{5,1},{9,13},{13,9},{2,6},{6,2},{1... | collective-permute-start | bytes 196616 | tf_op jit(solution)/shard_map/ppermute | solution.py:597
  16.8 3.5 %collective-permute-start.4 = (bf16[64,512]{1,0:T(8,128)(2,1)S(1)}, bf16[64,512]{1,0:T(8,128)(2,1)S(1)}, u32[]{:S(2)}, u32[]{:S(2)}) collective-permute-start(bf16[64,512]{1,0:T(8,128)(2,1)S(1)} %collective-permute-done.2.refs_1_.refs_9_.refs_8_), channel_id=1, source_target_pairs={{0,4},{4,0},{8,12},{12,8},{1,5},{5,1},{9,13},{13,9},{2,6},{6,2},{1... | collective-permute-start | bytes 196616 | tf_op jit(solution)/shard_map/ppermute | solution.py:597
  18.4 9.8 %collective-permute-start.6 = (f32[64,1280]{1,0:T(8,128)S(1)}, f32[64,1280]{1,0:T(8,128)S(1)}, u32[]{:S(2)}, u32[]{:S(2)}) collective-permute-start(f32[64,1280]{1,0:T(8,128)S(1)} %last_sent.1), channel_id=1, source_target_pairs={{0,8},{4,12},{8,0},{12,4},{1,9},{5,13},{9,1},{13,5},{2,10},{6,14},... | collective-permute-start | bytes 983048 | tf_op jit(solution)/shard_map/ppermute | solution.py:597
  28.3 1.9 %collective-permute-start.7 = (bf16[64,1280]{1,0:T(8,128)(2,1)S(1)}, bf16[64,1280]{1,0:T(8,128)(2,1)S(1)}, u32[]{:S(2)}, u32[]{:S(2)}) collective-permute-start(bf16[64,1280]{1,0:T(8,128)(2,1)S(1)} %get-tuple-element.54.refs_12_.refs_11_), channel_id=1, source_target_pairs={{0,4},{4,0},{8,12},{12,8},{1,5},{5,1},{9,13},{13,9},{2,6},{6,2},{1... | collective-permute-start | bytes 491528 | tf_op jit(solution)/shard_map/ppermute | solution.py:597
  28.4 6.6 %collective-permute-start.8 = (bf16[64,1280]{1,0:T(8,128)(2,1)S(1)}, bf16[64,1280]{1,0:T(8,128)(2,1)S(1)}, u32[]{:S(2)}, u32[]{:S(2)}) collective-permute-start(bf16[64,1280]{1,0:T(8,128)(2,1)S(1)} %get-tuple-element.62), channel_id=1, source_target_pairs={{0,16},{16,0},{1,17},{17,1},{2,18},{18,2},{3,19},{19,3},{4,20},{20... | collective-permute-start | bytes 491528 | tf_op jit(solution)/shard_map/ppermute | solution.py:597
  35.0 1.4 %collective-permute-start.9 = (bf16[64,1280]{1,0:T(8,128)(2,1)S(1)}, bf16[64,1280]{1,0:T(8,128)(2,1)S(1)}, u32[]{:S(2)}, u32[]{:S(2)}) collective-permute-start(bf16[64,1280]{1,0:T(8,128)(2,1)S(1)} %collective-permute-done.8.refs_13_.refs_12_), channel_id=1, source_target_pairs={{0,4},{4,0},{8,12},{12,8},{1,5},{5,1},{9,13},{13,9},{2,6},{6,2},{1... | collective-permute-start | bytes 491528 | tf_op jit(solution)/shard_map/ppermute | solution.py:597
